TPU v7x, 32 devices: a whole 2x2x4 slice. The times are simulated.
32 devices in a mesh: row: 4 (over y, x), col: 8 (over z, core).
Axes of the slice: x: 2, y: 2, z: 4, core: 2. Of those that a mesh axis runs over, the one named last changes fastest.
Arguments:
- slip: float32 [65536, 256], P(('row', 'col')), may hold values from -2 to 2
- state: float32 [65536, 256], P(('row', 'col')), may hold values from 0.4 to 0.9
- tau_load: float32 [65536], P(('row', 'col')), may hold values from 1 to 2
- normal_stress: float32 [65536], P(('row', 'col')), may hold values from 6 to 8
- direct_effect: float32 [65536], P(('row', 'col')), may hold values from 0.8 to 1.6
- evolution_effect: float32 [65536], P(('row', 'col')), may hold values from 0.5 to 1
- slip_distance: float32 [65536], P(('row', 'col')), may hold values from 0.5 to 2
- self_stiffness: float32 [65536], P(('row', 'col')), may hold values from 0.5 to 2
- near_blocks: bfloat16 [3, 65536, 256], P(None, ('row', 'col')), may hold values from -0.21875 to 0.21875
- basis_in: bfloat16 [32, 65536], P(None, ('row', 'col')), may hold values from -0.375 to 0.375
- basis_out: bfloat16 [32, 65536], P(None, ('row', 'col')), may hold values from -1 to 1
- coupling: bfloat16 [8192, 4, 2048], P('row', None, 'col'), may hold values from -0.09375 to 0.09375
- block_rank: int32 [256, 4, 64], P('row', None, 'col'), may hold values from 8 to 32
- adj_bricks: int32 [8, 65536], P(None, ('row', 'col')), may hold values from 0 to 1023
- adj_count: int32 [65536], P(('row', 'col')), may hold values from 1 to 8
- adj_weight: float32 [8, 65536], P(None, ('row', 'col')), may hold values from 0.05 to 1
- pressure_now: bfloat16 [1024, 256], P('col'), may hold values from 0.099609375 to 1
- pressure_rate: bfloat16 [1024, 256], P('col'), may hold values from 0.5 to 5
Outputs:
- slip_out: float32 [65536, 256], P(('row', 'col'))
- state_out: float32 [65536, 256], P(('row', 'col'))
Inputs may be any that keep to these rules, and one draw needn't show every extreme that they name: Only the first adj_count entries of a patch's brick list are read. `adj_bricks`: brick numbers index the whole reservoir. `block_rank`: ranks of pairs with |i - j| <= 1 are not read.
All inputs are finite; a program needn't handle non-finite values.
Results may differ from a plain program's by a relative error of at most 0.0007.
Values may be sent and summed in bfloat16 or wider, within the bound.
No kernel may reach another device: no remote copies, remote signals or barrier semaphores. Data moves between devices by JAX's collectives and lax.ppermute only.
A program may use at most 192 MiB of HBM per device.

v0:
```python
import functools

import jax
import jax.numpy as jnp
from jax import lax
from jax.experimental import pallas as pl
from jax.experimental.pallas import tpu as pltpu
from jax.sharding import PartitionSpec as P

BS = 256
R = 32

STEP_SIZE = 0.5
REF_FRICTION = 0.6
LIMIT = 16 * 1024 * 1024
F32 = jnp.float32
BF16 = jnp.bfloat16


def dot(a, b):
    return jnp.dot(a, b, preferred_element_type=F32)


def dot_t(a, b):
    return lax.dot_general(a, b, (((0,), (0,)), ((), ())), preferred_element_type=F32)


def params():
    return pltpu.CompilerParams(vmem_limit_bytes=LIMIT)


def project_kernel(slip_ref, basis_ref, coeff_ref, rounded_ref):
    rounded = slip_ref[...].astype(BF16)
    rounded_ref[...] = rounded
    coeff_ref[...] = dot(basis_ref[...], rounded).astype(BF16)


def project(slip, basis_in):
    patches, ens = slip.shape
    count = patches // BS
    return pl.pallas_call(
        project_kernel,
        grid=(count,),
        in_specs=[
            pl.BlockSpec((BS, ens), lambda n: (n, 0)),
            pl.BlockSpec((R, BS), lambda n: (0, n)),
        ],
        out_specs=[
            pl.BlockSpec((R, ens), lambda n: (n, 0)),
            pl.BlockSpec((BS, ens), lambda n: (n, 0)),
        ],
        out_shape=[
            jax.ShapeDtypeStruct((count * R, ens), BF16),
            jax.ShapeDtypeStruct((patches, ens), BF16),
        ],
        compiler_params=params(),
    )(slip, basis_in)


def couple_kernel(sources, where_ref, matrix_ref, *refs):
    coeffs, out_ref = refs[:sources], refs[sources]
    total = None
    for d in range(sources):
        term = dot(matrix_ref[where_ref[1 + d]], coeffs[d][...])
        total = term if total is None else total + term
    out_ref[...] = total.astype(out_ref.dtype)


def couple(where, matrix, coeffs, heights, kind):
    sources, rows, width = matrix.shape
    share, ens = coeffs[0].shape
    grid_spec = pltpu.PrefetchScalarGridSpec(
        num_scalar_prefetch=1,
        grid=(heights,),
        in_specs=[
            pl.BlockSpec(
                (sources, share, width),
                lambda d, w: (0, 2 * lax.rem(lax.div(w[0], 2) + d, heights) + lax.rem(w[0], 2), 0),
            )
        ]
        + [pl.BlockSpec((share, ens), lambda d, w: (0, 0))] * sources,
        out_specs=pl.BlockSpec((share, ens), lambda d, w: (d, 0)),
    )
    return pl.pallas_call(
        functools.partial(couple_kernel, sources),
        grid_spec=grid_spec,
        out_shape=jax.ShapeDtypeStruct((heights * share, ens), kind),
        compiler_params=params(),
    )(where, matrix, *coeffs)


def chip_sum_kernel(kept_ref, sent_ref, *outs):
    share = outs[0].shape[0]
    for d, out_ref in enumerate(outs):
        rows = slice(d * share, (d + 1) * share)
        out_ref[...] = (kept_ref[rows] + sent_ref[rows].astype(F32)).astype(BF16)


def chip_sum(kept, sent, heights):
    rows, ens = kept.shape
    return pl.pallas_call(
        chip_sum_kernel,
        out_shape=[jax.ShapeDtypeStruct((rows // heights, ens), BF16)] * heights,
        compiler_params=params(),
    )(kept, sent)


def fill_weights(bricks_ref, weight_ref, matrix):
    slots = bricks_ref.shape[0]
    ids = bricks_ref[...].T
    weights = weight_ref[...].T
    rows = 16
    lane = lax.broadcasted_iota(jnp.int32, (rows, 128), 1).astype(F32)
    for top in range(0, BS, rows):
        id_of = [jnp.broadcast_to(ids[top : top + rows, k : k + 1], (rows, 128)) for k in range(slots)]
        weight_of = [
            jnp.broadcast_to(weights[top : top + rows, k : k + 1], (rows, 128)) for k in range(slots)
        ]
        for left in range(0, matrix.shape[1], 128):
            here = lane + float(left)
            tile = jnp.zeros((rows, 128), F32)
            for k in range(slots):
                tile = jnp.where(id_of[k] == here, weight_of[k], tile)
            matrix[top : top + rows, left : left + 128] = tile.astype(BF16)


def near_tau(slip, numbers, near_ref, rounded_ref, first_ref, last_ref):
    n = pl.program_id(0)
    count = pl.num_programs(0)
    before_at = pl.multiple_of(jnp.maximum(n - 1, 0) * BS, BS)
    own_at = pl.multiple_of(n * BS, BS)
    after_at = pl.multiple_of(jnp.minimum(n + 1, count - 1) * BS, BS)
    before = jnp.where(n == 0, first_ref[...], rounded_ref[pl.ds(before_at, BS), :])
    after = jnp.where(n == count - 1, last_ref[...], rounded_ref[pl.ds(after_at, BS), :])
    near = dot(near_ref[0], before) + dot(near_ref[1], rounded_ref[pl.ds(own_at, BS), :]) + dot(near_ref[2], after)
    return numbers[:, 0:1] - numbers[:, 5:6] * slip - near


def prepare_first_kernel(
    bricks_ref, weight_ref, own_ref, other_ref, slip_ref, state_ref, numbers_ref, near_ref, rounded_ref, first_ref,
    last_ref, shift_ref, scale_ref, rest_ref, scale_mid_ref, matrix,
):
    fill_weights(bricks_ref, weight_ref, matrix)
    half = own_ref.shape[0]
    ens = slip_ref.shape[1]
    total = dot(matrix[:, :half], own_ref[...]) + dot(matrix[:, half:], other_ref[...])
    numbers = numbers_ref[...].T
    normal, inv_direct, inv_evolution, ratio = (numbers[:, k : k + 1] for k in range(1, 5))
    base = total[:, :ens]
    scale = inv_direct / (normal - base)
    scale_ref[...] = scale
    scale_mid_ref[...] = inv_direct / (normal - (base + STEP_SIZE * total[:, ens:]))
    state = state_ref[...]
    tau = near_tau(slip_ref[...], numbers, near_ref, rounded_ref, first_ref, last_ref)
    shift_ref[...] = tau * scale - state * inv_direct
    rest_ref[...] = state + (STEP_SIZE * ratio) * jnp.exp((REF_FRICTION - state) * inv_evolution)


def finish_first_kernel(
    heights, shift_ref, scale_ref, rest_ref, slip_ref, numbers_ref, basis_out_ref, basis_in_ref, *refs
):
    parts, (slip_mid_ref, state_mid_ref, rounded_ref, coeff_ref) = refs[:heights], refs[heights:]
    speed = jnp.exp(shift_ref[...] - scale_ref[...] * far_field(basis_out_ref, parts))
    slip_mid = slip_ref[...] + STEP_SIZE * speed
    slip_mid_ref[...] = slip_mid
    state_mid_ref[...] = rest_ref[...] - (STEP_SIZE * numbers_ref[4:5, :].T) * speed
    rounded = slip_mid.astype(BF16)
    rounded_ref[...] = rounded
    coeff_ref[...] = dot(basis_in_ref[...], rounded).astype(BF16)


def prepare_second_kernel(
    slip_ref, state_ref, slip_mid_ref, state_mid_ref, scale_ref, numbers_ref, near_ref, rounded_ref, first_ref,
    last_ref, shift_ref, slip_rest_ref, rest_ref,
):
    numbers = numbers_ref[...].T
    inv_direct, inv_evolution, ratio = (numbers[:, k : k + 1] for k in range(2, 5))
    slip = slip_mid_ref[...]
    state = state_mid_ref[...]
    tau = near_tau(slip, numbers, near_ref, rounded_ref, first_ref, last_ref)
    shift_ref[...] = tau * scale_ref[...] - state * inv_direct
    slip_rest_ref[...] = 0.5 * (slip_ref[...] + slip)
    friction = jnp.exp((REF_FRICTION - state) * inv_evolution)
    rest_ref[...] = 0.5 * (state_ref[...] + state) + (0.5 * STEP_SIZE * ratio) * friction


def finish_second_kernel(heights, shift_ref, scale_ref, rest_ref, slip_rest_ref, numbers_ref, basis_out_ref, *refs):
    parts, (slip_out_ref, state_out_ref) = refs[:heights], refs[heights:]
    speed = jnp.exp(shift_ref[...] - scale_ref[...] * far_field(basis_out_ref, parts))
    slip_out_ref[...] = slip_rest_ref[...] + (0.5 * STEP_SIZE) * speed
    state_out_ref[...] = rest_ref[...] - (0.5 * STEP_SIZE * numbers_ref[4:5, :].T) * speed


def far_field(basis_ref, parts):
    far = parts[0][...].astype(F32)
    for part in parts[1:]:
        far = far + part[...].astype(F32)
    return dot_t(basis_ref[...], far.astype(BF16))


class Specs:
    def __init__(self, slip, numbers):
        patches, ens = slip.shape
        self.count = patches // BS
        self.block = pl.BlockSpec((BS, ens), lambda n: (n, 0))
        self.edge = pl.BlockSpec((BS, ens), lambda n: (0, 0))
        self.all = pl.BlockSpec((patches, ens), lambda n: (0, 0))
        self.basis = pl.BlockSpec((R, BS), lambda n: (0, n))
        self.levels = pl.BlockSpec((R, ens), lambda n: (n, 0))
        self.numbers = pl.BlockSpec((numbers.shape[0], BS), lambda n: (0, n))
        self.near = pl.BlockSpec((3, BS, BS), lambda n: (0, n, 0))
        self.full = jax.ShapeDtypeStruct((patches, ens), F32)
        self.half = jax.ShapeDtypeStruct((patches, ens), BF16)


def prepare_first(bricks, weights, own, other, slip, state, numbers, near_blocks, rounded, first, last):
    s = Specs(slip, numbers)
    slots = pl.BlockSpec((bricks.shape[0], BS), lambda n: (0, n))
    field = pl.BlockSpec(own.shape, lambda n: (0, 0))
    return pl.pallas_call(
        prepare_first_kernel,
        grid=(s.count,),
        in_specs=[slots, slots, field, field, s.block, s.block, s.numbers, s.near, s.all, s.edge, s.edge],
        out_specs=[s.block] * 4,
        out_shape=[s.full] * 4,
        scratch_shapes=[pltpu.VMEM((BS, 2 * own.shape[0]), BF16)],
        compiler_params=params(),
    )(bricks, weights, own, other, slip, state, numbers, near_blocks, rounded, first, last)


def prepare_second(slip, state, slip_mid, state_mid, scale, numbers, near_blocks, rounded, first, last):
    s = Specs(slip, numbers)
    return pl.pallas_call(
        prepare_second_kernel,
        grid=(s.count,),
        in_specs=[s.block] * 5 + [s.numbers, s.near, s.all, s.edge, s.edge],
        out_specs=[s.block] * 3,
        out_shape=[s.full] * 3,
        compiler_params=params(),
    )(slip, state, slip_mid, state_mid, scale, numbers, near_blocks, rounded, first, last)


def finish_first(shift, scale, rest, slip, numbers, basis_out, basis_in, parts):
    s = Specs(slip, numbers)
    return pl.pallas_call(
        functools.partial(finish_first_kernel, len(parts)),
        grid=(s.count,),
        in_specs=[s.block] * 4 + [s.numbers, s.basis, s.basis] + [s.levels] * len(parts),
        out_specs=[s.block, s.block, s.block, s.levels],
        out_shape=[s.full, s.full, s.half, jax.ShapeDtypeStruct((s.count * R, slip.shape[1]), BF16)],
        compiler_params=params(),
    )(shift, scale, rest, slip, numbers, basis_out, basis_in, *parts)


def finish_second(shift, scale, rest, slip_rest, numbers, basis_out, parts):
    s = Specs(shift, numbers)
    return pl.pallas_call(
        functools.partial(finish_second_kernel, len(parts)),
        grid=(s.count,),
        in_specs=[s.block] * 4 + [s.numbers, s.basis] + [s.levels] * len(parts),
        out_specs=[s.block] * 2,
        out_shape=[s.full] * 2,
        compiler_params=params(),
    )(shift, scale, rest, slip_rest, numbers, basis_out, *parts)


def brick_weights(adj_bricks, adj_count, adj_weight):
    slots = adj_bricks.shape[0]
    live = adj_count[None, :] > jnp.arange(slots, dtype=jnp.int32)[:, None]
    weights = jnp.where(live, adj_weight, 0.0)
    total = jnp.sum(weights, axis=0)
    merged = []
    for k in range(slots):
        same = adj_bricks == adj_bricks[k][None, :]
        merged.append(jnp.sum(jnp.where(same, weights, 0.0), axis=0))
    return live, jnp.stack(merged) / total[None, :]


def masked_coupling(coupling, block_rank, row_index, col_index, row_count, col_count):
    rows, sources, width = coupling.shape
    share = width // R
    blocks = rows // R
    receiver = row_index * blocks + jnp.arange(blocks, dtype=jnp.int32)
    source = (
        (jnp.arange(sources, dtype=jnp.int32)[:, None] * col_count + col_index) * share
        + jnp.arange(share, dtype=jnp.int32)[None, :]
    )
    apart = jnp.abs(receiver[:, None, None] - source[None]) > 1
    rank = jnp.where(apart, block_rank, 0)
    rank = jnp.transpose(rank, (1, 0, 2))
    rank_full = jnp.repeat(rank, R, axis=2).reshape(sources, blocks, 1, width)
    level = jnp.maximum(
        jnp.arange(R, dtype=jnp.int32)[:, None], jnp.arange(width, dtype=jnp.int32)[None, :] % R
    )
    keep = level[None, None] < rank_full
    matrix = jnp.transpose(coupling, (1, 0, 2)).reshape(sources, blocks, R, width)
    return jnp.where(keep, matrix, jnp.zeros((), BF16)).reshape(sources, rows, width)


def per_device(
    slip,
    state,
    tau_load,
    normal_stress,
    direct_effect,
    evolution_effect,
    slip_distance,
    self_stiffness,
    near_blocks,
    basis_in,
    basis_out,
    coupling,
    block_rank,
    adj_bricks,
    adj_count,
    adj_weight,
    pressure_now,
    pressure_rate,
):
    row_count = lax.axis_size("row")
    col_count = lax.axis_size("col")
    row_index = lax.axis_index("row")
    col_index = lax.axis_index("col")
    heights = col_count // 2
    height, core = col_index // 2, col_index % 2
    both = ("row", "col")
    devices = row_count * col_count

    def to_row(array, d):
        return lax.ppermute(array, "row", [(i, (i + d) % row_count) for i in range(row_count)])

    def to_height(array, d):
        pairs = [(2 * z + k, 2 * ((z + d) % heights) + k) for z in range(heights) for k in range(2)]
        return lax.ppermute(array, "col", pairs)

    def to_core(array):
        return lax.ppermute(array, "col", [(2 * z + k, 2 * z + 1 - k) for z in range(heights) for k in range(2)])

    def halo(rounded):
        up = [(i, i + 1) for i in range(devices - 1)]
        down = [(j, i) for i, j in up]
        before = lax.ppermute(rounded[-BS:], both, up)
        after = lax.ppermute(rounded[:BS], both, down)
        return before, after

    size = pressure_now.shape[0]
    live, weights = brick_weights(adj_bricks, adj_count, adj_weight)
    owner, within = adj_bricks // size, adj_bricks % size
    distance = (height - owner // 2) % heights
    other = (owner % 2 != core).astype(jnp.int32)
    bricks = jnp.where(live, (other * heights + distance) * size + within, -1).astype(F32)

    numbers = jnp.stack(
        [
            tau_load,
            normal_stress,
            1.0 / direct_effect,
            1.0 / evolution_effect,
            evolution_effect / slip_distance,
            self_stiffness,
            tau_load,
            tau_load,
        ]
    )
    masked = masked_coupling(coupling, block_rank, row_index, col_index, row_count, col_count)
    source_rows = [(row_index - d) % row_count for d in range(row_count)]
    own_where = jnp.stack([col_index] + source_rows).astype(jnp.int32)
    pair_where = jnp.stack([2 * height + 1 - core] + source_rows).astype(jnp.int32)
    share = coupling.shape[2]

    def far_parts(coeffs):
        sent = to_core(couple(pair_where, masked, coeffs, heights, BF16))
        kept = couple(own_where, masked, coeffs, heights, F32)
        pieces = list(chip_sum(kept, sent, heights))
        return pieces[:1] + [to_height(pieces[d], d) for d in range(1, heights)]

    def row_coeffs(coeff):
        return [coeff] + [to_row(coeff, d) for d in range(1, row_count)]

    coeff, rounded = project(slip, basis_in)
    coeffs = row_coeffs(coeff)
    now, rate, _ = lax.optimization_barrier((pressure_now, pressure_rate, coeff))
    joined = jnp.concatenate([now, rate], axis=1)
    own = jnp.concatenate([joined] + [to_height(joined, d) for d in range(1, heights)], axis=0)
    first, last = halo(rounded)
    coeffs, first, last, own = lax.optimization_barrier((coeffs, first, last, own))
    other = to_core(own)
    parts = far_parts(coeffs)
    shift, scale, rest, scale_mid = prepare_first(
        bricks, weights, own, other, slip, state, numbers, near_blocks, rounded, first, last
    )
    slip_mid, state_mid, rounded, coeff = finish_first(
        shift, scale, rest, slip, numbers, basis_out, basis_in, parts
    )
    coeffs = row_coeffs(coeff)
    first, last = halo(rounded)
    coeffs, first, last = lax.optimization_barrier((coeffs, first, last))
    parts = far_parts(coeffs)
    shift, slip_rest, rest = prepare_second(
        slip, state, slip_mid, state_mid, scale_mid, numbers, near_blocks, rounded, first, last
    )
    slip_out, state_out = finish_second(shift, scale_mid, rest, slip_rest, numbers, basis_out, parts)
    return (slip_out, state_out)


def solution(mesh):
    in_specs = (
        P(("row", "col"), None),
        P(("row", "col"), None),
        P(("row", "col")),
        P(("row", "col")),
        P(("row", "col")),
        P(("row", "col")),
        P(("row", "col")),
        P(("row", "col")),
        P(None, ("row", "col"), None),
        P(None, ("row", "col")),
        P(None, ("row", "col")),
        P("row", None, "col"),
        P("row", None, "col"),
        P(None, ("row", "col")),
        P(("row", "col")),
        P(None, ("row", "col")),
        P("col", None),
        P("col", None),
    )
    out_specs = (P(("row", "col"), None), P(("row", "col"), None))
    return jax.shard_map(
        per_device, mesh=mesh, in_specs=in_specs, out_specs=out_specs, check_vma=False
    )
```

profile of v0, /device:TPU:12, one launch (start us, length us, event | category | flops | bytes accessed | tf_op | source)
XLA Modules:
  0.0 121.5 jit_solution(1071097999255231106)
XLA Ops:
  0.6 1.6 %copy-done.3 = f32[2048,256]{1,0:T(8,128)S(1)} copy-done((f32[2048,256]{1,0:T(8,128)S(1)}, f32[2048,256]{1,0:T(8,128)}, u32[]{:S(2)}) %copy-start.3) | copy-done | bytes 2097176
  2.2 0.9 copy-done.12
  3.2 1.3 %shard_map.185 = (bf16[256,256]{1,0:T(8,128)(2,1)S(1)}, bf16[2048,256]{1,0:T(8,128)(2,1)S(1)}) custom-call(f32[2048,256]{1,0:T(8,128)S(1)} %copy-done.3, bf16[32,2048]{1,0:T(8,128)(2,1)S(1)} %copy-done.12), custom_call_target="tpu_custom_call" | custom-call | tf_op jit(solution)/shard_map/pallas_call | solution.py:41
  5.0 2.6 %collective-permute-start.6 = (bf16[128,512]{1,0:T(8,128)(2,1)S(1)}, bf16[128,512]{1,0:T(8,128)(2,1)S(1)}, u32[]{:S(2)}, u32[]{:S(2)}) collective-permute-start(bf16[128,512]{1,0:T(8,128)(2,1)S(1)} %constant_dynamic-update-slice_fusion), channel_id=1, source_target_pairs={{0,4},{1,5},{2,6},{3,7},{4,0},{5,1},{6,2},{7,3},{8,12},{9,13},{10,... | collective-permute-start | bytes 393224 | tf_op jit(solution)/shard_map/ppermute | solution.py:334
  7.6 2.5 %collective-permute-start.5 = (bf16[128,512]{1,0:T(8,128)(2,1)S(1)}, bf16[128,512]{1,0:T(8,128)(2,1)S(1)}, u32[]{:S(2)}, u32[]{:S(2)}) collective-permute-start(bf16[128,512]{1,0:T(8,128)(2,1)S(1)} %constant_dynamic-update-slice_fusion), channel_id=1, source_target_pairs={{0,2},{1,3},{2,4},{3,5},{4,6},{5,7},{6,0},{7,1},{8,10},{9,11},{10,... | collective-permute-start | bytes 393224 | tf_op jit(solution)/shard_map/ppermute | solution.py:334
  10.0 1.4 %collective-permute-start.2 = (bf16[256,256]{1,0:T(8,128)(2,1)S(1)}, bf16[256,256]{1,0:T(8,128)(2,1)S(1)}, u32[]{:S(2)}, u32[]{:S(2)}) collective-permute-start(bf16[256,256]{1,0:T(8,128)(2,1)S(1)} %get-tuple-element.48.refs_0_), channel_id=1, source_target_pairs={{0,24},{8,0},{16,8},{24,16},{1,25},{9,1},{17,9},{25,17},{2,26},{10... | collective-permute-start | bytes 393224 | tf_op jit(solution)/shard_map/ppermute | solution.py:330
  11.5 1.5 %collective-permute-start.1 = (bf16[256,256]{1,0:T(8,128)(2,1)S(1)}, bf16[256,256]{1,0:T(8,128)(2,1)S(1)}, u32[]{:S(2)}, u32[]{:S(2)}) collective-permute-start(bf16[256,256]{1,0:T(8,128)(2,1)S(1)} %get-tuple-element.48.refs_0_), channel_id=1, source_target_pairs={{0,16},{8,24},{16,0},{24,8},{1,17},{9,25},{17,1},{25,9},{2,18},{10... | collective-permute-start | bytes 393224 | tf_op jit(solution)/shard_map/ppermute | solution.py:330
  13.1 0.7 fusion.15
  14.2 2.3 %collective-permute-done.6 = bf16[128,512]{1,0:T(8,128)(2,1)S(1)} collective-permute-done((bf16[128,512]{1,0:T(8,128)(2,1)S(1)}, bf16[128,512]{1,0:T(8,128)(2,1)S(1)}, u32[]{:S(2)}, u32[]{:S(2)}) %collective-permute-start.6) | collective-permute-done | bytes 131104 | tf_op jit(solution)/shard_map/ppermute | solution.py:334
  16.5 4.1 %collective-permute-start.4 = (bf16[256,256]{1,0:T(8,128)(2,1)}, bf16[256,256]{1,0:T(8,128)(2,1)S(1)}, u32[]{:S(2)}, u32[]{:S(2)}) collective-permute-start(bf16[256,256]{1,0:T(8,128)(2,1)} %get-tuple-element.85), channel_id=1, source_target_pairs={{1,0},{2,1},{3,2},{4,3},{5,4},{6,5},{7,6},{8,7},{9,8},{10,9},{11,1... | collective-permute-start | bytes 393224 | tf_op jit(solution)/shard_map/ppermute | solution.py:343
  20.7 0.6 copy-done.28
  21.3 1.9 %collective-permute-start.3 = (bf16[256,256]{1,0:T(8,128)(2,1)}, bf16[256,256]{1,0:T(8,128)(2,1)S(1)}, u32[]{:S(2)}, u32[]{:S(2)}) collective-permute-start(bf16[256,256]{1,0:T(8,128)(2,1)} %get-tuple-element.86), channel_id=1, source_target_pairs={{0,1},{1,2},{2,3},{3,4},{4,5},{5,6},{6,7},{7,8},{8,9},{9,10},{10,1... | collective-permute-start | bytes 393224 | tf_op jit(solution)/shard_map/ppermute | solution.py:342
  24.1 5.0 %fusion.matrix_ref = bf16[4,2048,256]{2,1,0:T(8,128)(2,1)} fusion(bf16[2048,4,256]{2,1,0:T(4,128)(2,1)} %param.29, s32[4,64,256]{2,1,0:T(8,128)S(1)} %copy.22, s32[2048,256]{1,0:T(8,128)S(1)} %bitcast.38), kind=kLoop, calls=%fused_computation.1 | loop fusion | flops 4194304 | bytes 10747904 | tf_op jit(solution)/shard_map/jit(_where)/select_n | solution.py:297
  29.4 0.7 copy-done.19
  30.1 0.6 copy-done.21
  31.2 2.2 %copy-done = bf16[4,2048,256]{2,1,0:T(8,128)(2,1)S(1)} copy-done((bf16[4,2048,256]{2,1,0:T(8,128)(2,1)S(1)}, bf16[4,2048,256]{2,1,0:T(8,128)(2,1)}, u32[]{:S(2)}) %copy-start) | copy-done | bytes 4194328
  33.4 3.0 %shard_map.188 = bf16[1024,256]{1,0:T(8,128)(2,1)} custom-call(s32[5]{0:T(128)S(1)} %stack.101.where_ref, bf16[4,2048,256]{2,1,0:T(8,128)(2,1)S(1)} %copy-done, bf16[256,256]{1,0:T(8,128)(2,1)S(1)} %get-tuple-element.48.refs_0_, bf16[256,256]{1,0:T(8,128)(2,1)S(1)} %collective-permute-done.refs_1_, bf16[256,256]{1,0:T(8,128)(2,1)S(1)} %collective-permute-done.1.refs_2_, ...), custom_call_target="tpu_custom_call" | custom-call | tf_op jit(solution)/shard_map/pallas_call | solution.py:84
  37.8 2.2 %copy-done.1 = bf16[4,2048,256]{2,1,0:T(8,128)(2,1)S(1)} copy-done((bf16[4,2048,256]{2,1,0:T(8,128)(2,1)S(1)}, bf16[4,2048,256]{2,1,0:T(8,128)(2,1)}, u32[]{:S(2)}) %copy-start.1) | copy-done | bytes 4194328
  40.0 0.9 copy-done.15
  40.9 0.9 copy-done.17
  41.8 2.1 %shard_map.187.kept_ref = f32[1024,256]{1,0:T(8,128)S(1)} custom-call(s32[5]{0:T(128)S(1)} %stack.99.where_ref, bf16[4,2048,256]{2,1,0:T(8,128)(2,1)S(1)} %copy-done.1, bf16[256,256]{1,0:T(8,128)(2,1)S(1)} %get-tuple-element.48.refs_0_, bf16[256,256]{1,0:T(8,128)(2,1)S(1)} %copy-done.17, bf16[256,256]{1,0:T(8,128)(2,1)S(1)} %copy-done.15, ...), custom_call_target="tpu_custom_call" | custom-call | tf_op jit(solution)/shard_map/pallas_call | solution.py:84
  43.9 1.9 %shard_map.189 = (bf16[256,256]{1,0:T(8,128)(2,1)S(1)}, bf16[256,256]{1,0:T(8,128)(2,1)}, bf16[256,256]{1,0:T(8,128)(2,1)}, bf16[256,256]{1,0:T(8,128)(2,1)}) custom-call(f32[1024,256]{1,0:T(8,128)S(1)} %shard_map.187.kept_ref, bf16[1024,256]{1,0:T(8,128)(2,1)} %collective-permute-done.9.sent_ref), custom_call_target="tpu_custom_call" | custom-call | tf_op jit(solution)/shard_map/pallas_call | solution.py:101
  45.7 1.4 %collective-permute-start.10 = (bf16[256,256]{1,0:T(8,128)(2,1)}, bf16[256,256]{1,0:T(8,128)(2,1)}, u32[]{:S(2)}, u32[]{:S(2)}) collective-permute-start(bf16[256,256]{1,0:T(8,128)(2,1)} %get-tuple-element.53), channel_id=1, source_target_pairs={{0,2},{1,3},{2,4},{3,5},{4,6},{5,7},{6,0},{7,1},{8,10},{9,11},{10,... | collective-permute-start | bytes 393224 | tf_op jit(solution)/shard_map/ppermute | solution.py:334
  47.1 3.7 %collective-permute-start.11 = (bf16[256,256]{1,0:T(8,128)(2,1)}, bf16[256,256]{1,0:T(8,128)(2,1)}, u32[]{:S(2)}, u32[]{:S(2)}) collective-permute-start(bf16[256,256]{1,0:T(8,128)(2,1)} %get-tuple-element.54), channel_id=1, source_target_pairs={{0,4},{1,5},{2,6},{3,7},{4,0},{5,1},{6,2},{7,3},{8,12},{9,13},{10,... | collective-permute-start | bytes 393224 | tf_op jit(solution)/shard_map/ppermute | solution.py:334
  50.8 0.9 collective-permute-start.12
  51.7 0.9 stack.93.numbers_ref
  52.6 1.9 %copy-done.5 = bf16[3,2048,256]{2,1,0:T(8,128)(2,1)S(1)} copy-done((bf16[3,2048,256]{2,1,0:T(8,128)(2,1)S(1)}, bf16[3,2048,256]{2,1,0:T(8,128)(2,1)}, u32[]{:S(2)}) %copy-start.5) | copy-done | bytes 3145752
  54.5 1.6 %copy-done.7 = f32[2048,256]{1,0:T(8,128)S(1)} copy-done((f32[2048,256]{1,0:T(8,128)S(1)}, f32[2048,256]{1,0:T(8,128)}, u32[]{:S(2)}) %copy-start.7) | copy-done | bytes 2097176
  56.1 1.2 %copy-done.10 = bf16[2048,256]{1,0:T(8,128)(2,1)S(1)} copy-done((bf16[2048,256]{1,0:T(8,128)(2,1)S(1)}, bf16[2048,256]{1,0:T(8,128)(2,1)}, u32[]{:S(2)}) %copy-start.10) | copy-done | bytes 1048600
  57.3 0.8 copy-done.18
  58.1 0.9 copy-done.20
  59.0 0.9 copy-done.22
  59.9 17.0 %shard_map.186 = (f32[2048,256]{1,0:T(8,128)S(1)}, f32[2048,256]{1,0:T(8,128)S(1)}, f32[2048,256]{1,0:T(8,128)S(1)}, f32[2048,256]{1,0:T(8,128)S(1)}) custom-call(f32[8,2048]{1,0:T(8,128)S(1)} %fusion.8.bricks_ref, f32[8,2048]{1,0:T(8,128)S(1)} %copy-done.18, bf16[512,512]{1,0:T(8,128)(2,1)S(1)} %pad_maximum_fusion.own_ref, ...), custom_call_target="tpu_custom_call" | custom-call | tf_op jit(solution)/shard_map/pallas_call | solution.py:220
  77.0 5.2 %shard_map.190 = (f32[2048,256]{1,0:T(8,128)S(1)}, f32[2048,256]{1,0:T(8,128)S(1)}, bf16[2048,256]{1,0:T(8,128)(2,1)S(1)}, bf16[256,256]{1,0:T(8,128)(2,1)S(1)}) custom-call(f32[2048,256]{1,0:T(8,128)S(1)} %get-tuple-element.45.shift_ref, f32[2048,256]{1,0:T(8,128)S(1)} %get-tuple-element.46.scale_ref, f32[2048,256]{1,0:T(8,128)S(1)} %get-tuple-element.47.rest_ref, ...), custom_call_target="tpu_custom_call" | custom-call | tf_op jit(solution)/shard_map/pallas_call | solution.py:245
  82.2 1.9 %collective-permute-start.15 = (bf16[256,256]{1,0:T(8,128)(2,1)S(1)}, bf16[256,256]{1,0:T(8,128)(2,1)S(1)}, u32[]{:S(2)}, u32[]{:S(2)}) collective-permute-start(bf16[256,256]{1,0:T(8,128)(2,1)S(1)} %get-tuple-element.66.refs_0_), channel_id=1, source_target_pairs={{0,24},{8,0},{16,8},{24,16},{1,25},{9,1},{17,9},{25,17},{2,26},{10... | collective-permute-start | bytes 393224 | tf_op jit(solution)/shard_map/ppermute | solution.py:330
  84.0 0.7 collective-permute-start.13
  84.7 1.9 %collective-permute-start.17 = (bf16[256,256]{1,0:T(8,128)(2,1)S(1)}, bf16[256,256]{1,0:T(8,128)(2,1)S(1)}, u32[]{:S(2)}, u32[]{:S(2)}) collective-permute-start(bf16[256,256]{1,0:T(8,128)(2,1)S(1)} %get-tuple-element.83), channel_id=1, source_target_pairs={{1,0},{2,1},{3,2},{4,3},{5,4},{6,5},{7,6},{8,7},{9,8},{10,9},{11,1... | collective-permute-start | bytes 393224 | tf_op jit(solution)/shard_map/ppermute | solution.py:343
  86.7 2.4 %collective-permute-start.16 = (bf16[256,256]{1,0:T(8,128)(2,1)S(1)}, bf16[256,256]{1,0:T(8,128)(2,1)S(1)}, u32[]{:S(2)}, u32[]{:S(2)}) collective-permute-start(bf16[256,256]{1,0:T(8,128)(2,1)S(1)} %get-tuple-element.84), channel_id=1, source_target_pairs={{0,1},{1,2},{2,3},{3,4},{4,5},{5,6},{6,7},{7,8},{8,9},{9,10},{10,1... | collective-permute-start | bytes 393224 | tf_op jit(solution)/shard_map/ppermute | solution.py:342
  89.1 2.5 %collective-permute-done.14.refs_2_ = bf16[256,256]{1,0:T(8,128)(2,1)S(1)} collective-permute-done((bf16[256,256]{1,0:T(8,128)(2,1)S(1)}, bf16[256,256]{1,0:T(8,128)(2,1)S(1)}, u32[]{:S(2)}, u32[]{:S(2)}) %collective-permute-start.14) | collective-permute-done | bytes 131104 | tf_op jit(solution)/shard_map/ppermute | solution.py:330
  91.6 1.5 %collective-permute-done.16.first_ref = bf16[256,256]{1,0:T(8,128)(2,1)S(1)} collective-permute-done((bf16[256,256]{1,0:T(8,128)(2,1)S(1)}, bf16[256,256]{1,0:T(8,128)(2,1)S(1)}, u32[]{:S(2)}, u32[]{:S(2)}) %collective-permute-start.16) | collective-permute-done | bytes 131104 | tf_op jit(solution)/shard_map/ppermute | solution.py:342
  93.1 2.1 %shard_map.193 = bf16[1024,256]{1,0:T(8,128)(2,1)S(1)} custom-call(s32[5]{0:T(128)S(1)} %stack.101.where_ref, bf16[4,2048,256]{2,1,0:T(8,128)(2,1)S(1)} %copy-done.2, bf16[256,256]{1,0:T(8,128)(2,1)S(1)} %get-tuple-element.66.refs_0_, bf16[256,256]{1,0:T(8,128)(2,1)S(1)} %collective-permute-done.13.refs_1_, ...), custom_call_target="tpu_custom_call" | custom-call | tf_op jit(solution)/shard_map/pallas_call | solution.py:84
  95.3 2.1 %shard_map.192.kept_ref = f32[1024,256]{1,0:T(8,128)S(1)} custom-call(s32[5]{0:T(128)S(1)} %stack.99.where_ref, bf16[4,2048,256]{2,1,0:T(8,128)(2,1)S(1)} %copy-done.2, bf16[256,256]{1,0:T(8,128)(2,1)S(1)} %get-tuple-element.66.refs_0_, bf16[256,256]{1,0:T(8,128)(2,1)S(1)} %collective-permute-done.13.refs_1_, ...), custom_call_target="tpu_custom_call" | custom-call | tf_op jit(solution)/shard_map/pallas_call | solution.py:84
  97.5 1.5 %collective-permute-start.19 = (bf16[256,256]{1,0:T(8,128)(2,1)S(1)}, bf16[256,256]{1,0:T(8,128)(2,1)S(1)}, u32[]{:S(2)}, u32[]{:S(2)}) collective-permute-start(bf16[256,256]{1,0:T(8,128)(2,1)S(1)} %get-tuple-element.71), channel_id=1, source_target_pairs={{0,2},{1,3},{2,4},{3,5},{4,6},{5,7},{6,0},{7,1},{8,10},{9,11},{10,... | collective-permute-start | bytes 393224 | tf_op jit(solution)/shard_map/ppermute | solution.py:334
  99.0 6.5 %collective-permute-start.20 = (bf16[256,256]{1,0:T(8,128)(2,1)S(1)}, bf16[256,256]{1,0:T(8,128)(2,1)S(1)}, u32[]{:S(2)}, u32[]{:S(2)}) collective-permute-start(bf16[256,256]{1,0:T(8,128)(2,1)S(1)} %get-tuple-element.72), channel_id=1, source_target_pairs={{0,4},{1,5},{2,6},{3,7},{4,0},{5,1},{6,2},{7,3},{8,12},{9,13},{10,... | collective-permute-start | bytes 393224 | tf_op jit(solution)/shard_map/ppermute | solution.py:334
  105.5 3.9 %shard_map.191 = (f32[2048,256]{1,0:T(8,128)S(1)}, f32[2048,256]{1,0:T(8,128)S(1)}, f32[2048,256]{1,0:T(8,128)S(1)}) custom-call(f32[2048,256]{1,0:T(8,128)S(1)} %copy-done.4, f32[2048,256]{1,0:T(8,128)S(1)} %copy-done.8, f32[2048,256]{1,0:T(8,128)S(1)} %get-tuple-element.56.slip_mid_ref, f32[2048,256]{1,0:T(8,128)S(1)} %get-tuple-element.57.state_mid_ref, ...), custom_call_target="tpu_custom_call" | custom-call | tf_op jit(solution)/shard_map/pallas_call | solution.py:233
  109.4 4.8 %collective-permute-done.20.refs_2_ = bf16[256,256]{1,0:T(8,128)(2,1)S(1)} collective-permute-done((bf16[256,256]{1,0:T(8,128)(2,1)S(1)}, bf16[256,256]{1,0:T(8,128)(2,1)S(1)}, u32[]{:S(2)}, u32[]{:S(2)}) %collective-permute-start.20) | collective-permute-done | bytes 131104 | tf_op jit(solution)/shard_map/ppermute | solution.py:334
  114.2 2.8 %collective-permute-done.21.refs_3_ = bf16[256,256]{1,0:T(8,128)(2,1)S(1)} collective-permute-done((bf16[256,256]{1,0:T(8,128)(2,1)S(1)}, bf16[256,256]{1,0:T(8,128)(2,1)S(1)}, u32[]{:S(2)}, u32[]{:S(2)}) %collective-permute-start.21) | collective-permute-done | bytes 131104 | tf_op jit(solution)/shard_map/ppermute | solution.py:334
  117.0 4.5 %shard_map.195 = (f32[2048,256]{1,0:T(8,128)}, f32[2048,256]{1,0:T(8,128)}) custom-call(f32[2048,256]{1,0:T(8,128)S(1)} %get-tuple-element.63.shift_ref, f32[2048,256]{1,0:T(8,128)S(1)} %get-tuple-element.58.scale_ref, f32[2048,256]{1,0:T(8,128)S(1)} %get-tuple-element.64.rest_ref, f32[2048,256]{1,0:T(8,128)S(1)} %get-tuple-element.65.slip_rest_ref, ...), custom_call_target="tpu_custom_call" | custom-call | tf_op jit(solution)/shard_map/pallas_call | solution.py:257
  (110 shorter events, 4.0 us)
Async XLA Ops:
  0.6 1.6 %copy-start.3 = (f32[2048,256]{1,0:T(8,128)S(1)}, f32[2048,256]{1,0:T(8,128)}, u32[]{:S(2)}) copy-start(f32[2048,256]{1,0:T(8,128)} %slip_ref.7) | copy-start | bytes 6291460
  3.1 9.9 %copy-start.23 = (s32[8,2048]{1,0:T(8,128)S(1)}, s32[8,2048]{1,0:T(8,128)}, u32[]{:S(2)}) copy-start(s32[8,2048]{1,0:T(8,128)} %param.31) | copy-start | bytes 196612
  3.1 10.7 %copy-start.35 = (s32[64,4,8]{0,2,1:T(8,128)S(1)}, s32[64,4,8]{0,2,1:T(8,128)}, u32[]{:S(2)}) copy-start(s32[64,4,8]{0,2,1:T(8,128)} %param.30) | copy-start | bytes 24580
  3.1 10.8 %copy-start.34 = (s32[2048]{0:T(1024)S(1)}, s32[2048]{0:T(1024)}, u32[]{:S(2)}) copy-start(s32[2048]{0:T(1024)} %param.32) | copy-start | bytes 24580
  3.2 20.1 %copy-start.31 = (f32[8,2048]{1,0:T(8,128)S(1)}, f32[8,2048]{1,0:T(8,128)}, u32[]{:S(2)}) copy-start(f32[8,2048]{1,0:T(8,128)} %param.33) | copy-start | bytes 196612
  4.4 19.6 %copy-start.9 = (bf16[2048,256]{1,0:T(8,128)(2,1)}, bf16[2048,256]{1,0:T(8,128)(2,1)S(1)}, u32[]{:S(2)}) copy-start(bf16[2048,256]{1,0:T(8,128)(2,1)S(1)} %get-tuple-element.39.rounded_ref) | copy-start | bytes 3145732
  4.5 9.7 %collective-permute-start.7 = (bf16[128,512]{1,0:T(8,128)(2,1)S(1)}, bf16[128,512]{1,0:T(8,128)(2,1)S(1)}, u32[]{:S(2)}, u32[]{:S(2)}) collective-permute-start(bf16[128,512]{1,0:T(8,128)(2,1)S(1)} %constant_dynamic-update-slice_fusion), channel_id=1, source_target_pairs={{0,6},{1,7},{2,0},{3,1},{4,2},{5,3},{6,4},{7,5},{8,14},{9,15},{10,... | collective-permute-start | bytes 393224 | tf_op jit(solution)/shard_map/ppermute | solution.py:334
  5.0 11.6 %collective-permute-start.6 = (bf16[128,512]{1,0:T(8,128)(2,1)S(1)}, bf16[128,512]{1,0:T(8,128)(2,1)S(1)}, u32[]{:S(2)}, u32[]{:S(2)}) collective-permute-start(bf16[128,512]{1,0:T(8,128)(2,1)S(1)} %constant_dynamic-update-slice_fusion), channel_id=1, source_target_pairs={{0,4},{1,5},{2,6},{3,7},{4,0},{5,1},{6,2},{7,3},{8,12},{9,13},{10,... | collective-permute-start | bytes 393224 | tf_op jit(solution)/shard_map/ppermute | solution.py:334
  7.6 13.1 %collective-permute-start.5 = (bf16[128,512]{1,0:T(8,128)(2,1)S(1)}, bf16[128,512]{1,0:T(8,128)(2,1)S(1)}, u32[]{:S(2)}, u32[]{:S(2)}) collective-permute-start(bf16[128,512]{1,0:T(8,128)(2,1)S(1)} %constant_dynamic-update-slice_fusion), channel_id=1, source_target_pairs={{0,2},{1,3},{2,4},{3,5},{4,6},{5,7},{6,0},{7,1},{8,10},{9,11},{10,... | collective-permute-start | bytes 393224 | tf_op jit(solution)/shard_map/ppermute | solution.py:334
  10.0 19.3 %collective-permute-start.2 = (bf16[256,256]{1,0:T(8,128)(2,1)S(1)}, bf16[256,256]{1,0:T(8,128)(2,1)S(1)}, u32[]{:S(2)}, u32[]{:S(2)}) collective-permute-start(bf16[256,256]{1,0:T(8,128)(2,1)S(1)} %get-tuple-element.48.refs_0_), channel_id=1, source_target_pairs={{0,24},{8,0},{16,8},{24,16},{1,25},{9,1},{17,9},{25,17},{2,26},{10... | collective-permute-start | bytes 393224 | tf_op jit(solution)/shard_map/ppermute | solution.py:330
  11.5 17.9 %collective-permute-start.1 = (bf16[256,256]{1,0:T(8,128)(2,1)S(1)}, bf16[256,256]{1,0:T(8,128)(2,1)S(1)}, u32[]{:S(2)}, u32[]{:S(2)}) collective-permute-start(bf16[256,256]{1,0:T(8,128)(2,1)S(1)} %get-tuple-element.48.refs_0_), channel_id=1, source_target_pairs={{0,16},{8,24},{16,0},{24,8},{1,17},{9,25},{17,1},{25,9},{2,18},{10... | collective-permute-start | bytes 393224 | tf_op jit(solution)/shard_map/ppermute | solution.py:330
  14.1 9.4 %copy-start.24 = (bf16[128,512]{1,0:T(8,128)(2,1)}, bf16[128,512]{1,0:T(8,128)(2,1)S(1)}, u32[]{:S(2)}) copy-start(bf16[128,512]{1,0:T(8,128)(2,1)S(1)} %collective-permute-done.7) | copy-start | bytes 393220
  14.1 15.2 %collective-permute-start = (bf16[256,256]{1,0:T(8,128)(2,1)S(1)}, bf16[256,256]{1,0:T(8,128)(2,1)S(1)}, u32[]{:S(2)}, u32[]{:S(2)}) collective-permute-start(bf16[256,256]{1,0:T(8,128)(2,1)S(1)} %get-tuple-element.48.refs_0_), channel_id=1, source_target_pairs={{0,8},{8,16},{16,24},{24,0},{1,9},{9,17},{17,25},{25,1},{2,10},{10... | collective-permute-start | bytes 393224 | tf_op jit(solution)/shard_map/ppermute | solution.py:330
  16.5 6.9 %copy-start.26 = (bf16[128,512]{1,0:T(8,128)(2,1)}, bf16[128,512]{1,0:T(8,128)(2,1)S(1)}, u32[]{:S(2)}) copy-start(bf16[128,512]{1,0:T(8,128)(2,1)S(1)} %collective-permute-done.6) | copy-start | bytes 393220
  16.5 12.8 %collective-permute-start.4 = (bf16[256,256]{1,0:T(8,128)(2,1)}, bf16[256,256]{1,0:T(8,128)(2,1)S(1)}, u32[]{:S(2)}, u32[]{:S(2)}) collective-permute-start(bf16[256,256]{1,0:T(8,128)(2,1)} %get-tuple-element.85), channel_id=1, source_target_pairs={{1,0},{2,1},{3,2},{4,3},{5,4},{6,5},{7,6},{8,7},{9,8},{10,9},{11,1... | collective-permute-start | bytes 393224 | tf_op jit(solution)/shard_map/ppermute | solution.py:343
  21.3 8.8 %collective-permute-start.3 = (bf16[256,256]{1,0:T(8,128)(2,1)}, bf16[256,256]{1,0:T(8,128)(2,1)S(1)}, u32[]{:S(2)}, u32[]{:S(2)}) collective-permute-start(bf16[256,256]{1,0:T(8,128)(2,1)} %get-tuple-element.86), channel_id=1, source_target_pairs={{0,1},{1,2},{2,3},{3,4},{4,5},{5,6},{6,7},{7,8},{8,9},{9,10},{10,1... | collective-permute-start | bytes 393224 | tf_op jit(solution)/shard_map/ppermute | solution.py:342
  24.0 5.2 %copy-start.25 = (bf16[128,512]{1,0:T(8,128)(2,1)S(1)}, bf16[128,512]{1,0:T(8,128)(2,1)}, u32[]{:S(2)}) copy-start(bf16[128,512]{1,0:T(8,128)(2,1)} %copy-done.24) | copy-start | bytes 393220
  24.0 5.2 %copy-start.27 = (bf16[128,512]{1,0:T(8,128)(2,1)S(1)}, bf16[128,512]{1,0:T(8,128)(2,1)}, u32[]{:S(2)}) copy-start(bf16[128,512]{1,0:T(8,128)(2,1)} %copy-done.26) | copy-start | bytes 393220
  24.1 5.2 %copy-start.29 = (bf16[128,512]{1,0:T(8,128)(2,1)S(1)}, bf16[128,512]{1,0:T(8,128)(2,1)}, u32[]{:S(2)}) copy-start(bf16[128,512]{1,0:T(8,128)(2,1)} %copy-done.28) | copy-start | bytes 393220
  29.3 7.9 %copy-start.37 = (f32[2048]{0:T(1024)S(1)}, f32[2048]{0:T(1024)}, u32[]{:S(2)}) copy-start(f32[2048]{0:T(1024)} %param.23) | copy-start | bytes 24580
  29.3 7.9 %copy-start.38 = (f32[2048]{0:T(1024)S(1)}, f32[2048]{0:T(1024)}, u32[]{:S(2)}) copy-start(f32[2048]{0:T(1024)} %param.24) | copy-start | bytes 24580
  29.3 7.0 %copy-start.14 = (bf16[256,256]{1,0:T(8,128)(2,1)}, bf16[256,256]{1,0:T(8,128)(2,1)S(1)}, u32[]{:S(2)}) copy-start(bf16[256,256]{1,0:T(8,128)(2,1)S(1)} %collective-permute-done.1.refs_2_) | copy-start | bytes 393220
  29.4 7.0 %copy-start.16 = (bf16[256,256]{1,0:T(8,128)(2,1)}, bf16[256,256]{1,0:T(8,128)(2,1)S(1)}, u32[]{:S(2)}) copy-start(bf16[256,256]{1,0:T(8,128)(2,1)S(1)} %collective-permute-done.refs_1_) | copy-start | bytes 393220
  30.8 21.8 %collective-permute-start.8 = (bf16[512,512]{1,0:T(8,128)(2,1)S(1)}, bf16[512,512]{1,0:T(8,128)(2,1)S(1)}, u32[]{:S(2)}, u32[]{:S(2)}) collective-permute-start(bf16[512,512]{1,0:T(8,128)(2,1)S(1)} %pad_maximum_fusion.own_ref), channel_id=1, source_target_pairs={{0,1},{1,0},{2,3},{3,2},{4,5},{5,4},{6,7},{7,6},{8,9},{9,8},{10,11... | collective-permute-start | bytes 1572872 | tf_op jit(solution)/shard_map/ppermute | solution.py:337
  31.2 2.2 %copy-start = (bf16[4,2048,256]{2,1,0:T(8,128)(2,1)S(1)}, bf16[4,2048,256]{2,1,0:T(8,128)(2,1)}, u32[]{:S(2)}) copy-start(bf16[4,2048,256]{2,1,0:T(8,128)(2,1)} %fusion.matrix_ref) | copy-start | bytes 12582916
  36.3 7.5 %collective-permute-start.9 = (bf16[1024,256]{1,0:T(8,128)(2,1)}, bf16[1024,256]{1,0:T(8,128)(2,1)}, u32[]{:S(2)}, u32[]{:S(2)}) collective-permute-start(bf16[1024,256]{1,0:T(8,128)(2,1)} %shard_map.188), channel_id=1, source_target_pairs={{0,1},{1,0},{2,3},{3,2},{4,5},{5,4},{6,7},{7,6},{8,9},{9,8},{10,11... | collective-permute-start | bytes 1572872 | tf_op jit(solution)/shard_map/ppermute | solution.py:337
  37.8 2.2 %copy-start.1 = (bf16[4,2048,256]{2,1,0:T(8,128)(2,1)S(1)}, bf16[4,2048,256]{2,1,0:T(8,128)(2,1)}, u32[]{:S(2)}) copy-start(bf16[4,2048,256]{2,1,0:T(8,128)(2,1)} %fusion.matrix_ref) | copy-start | bytes 12582916
  41.8 9.9 %copy-start.36 = (f32[2048]{0:T(1024)S(1)}, f32[2048]{0:T(1024)}, u32[]{:S(2)}) copy-start(f32[2048]{0:T(1024)} %param.22) | copy-start | bytes 24580
  41.8 9.9 %copy-start.30 = (f32[2048]{0:T(1024)S(1)}, f32[2048]{0:T(1024)}, u32[]{:S(2)}) copy-start(f32[2048]{0:T(1024)} %param.20) | copy-start | bytes 24580
  41.8 10.8 %copy-start.4 = (f32[2048,256]{1,0:T(8,128)S(1)}, f32[2048,256]{1,0:T(8,128)}, u32[]{:S(2)}) copy-start(f32[2048,256]{1,0:T(8,128)} %slip_ref.7) | copy-start | bytes 6291460
  45.7 31.2 %collective-permute-start.10 = (bf16[256,256]{1,0:T(8,128)(2,1)}, bf16[256,256]{1,0:T(8,128)(2,1)}, u32[]{:S(2)}, u32[]{:S(2)}) collective-permute-start(bf16[256,256]{1,0:T(8,128)(2,1)} %get-tuple-element.53), channel_id=1, source_target_pairs={{0,2},{1,3},{2,4},{3,5},{4,6},{5,7},{6,0},{7,1},{8,10},{9,11},{10,... | collective-permute-start | bytes 393224 | tf_op jit(solution)/shard_map/ppermute | solution.py:334
  47.1 29.9 %collective-permute-start.11 = (bf16[256,256]{1,0:T(8,128)(2,1)}, bf16[256,256]{1,0:T(8,128)(2,1)}, u32[]{:S(2)}, u32[]{:S(2)}) collective-permute-start(bf16[256,256]{1,0:T(8,128)(2,1)} %get-tuple-element.54), channel_id=1, source_target_pairs={{0,4},{1,5},{2,6},{3,7},{4,0},{5,1},{6,2},{7,3},{8,12},{9,13},{10,... | collective-permute-start | bytes 393224 | tf_op jit(solution)/shard_map/ppermute | solution.py:334
  50.8 26.1 %collective-permute-start.12 = (bf16[256,256]{1,0:T(8,128)(2,1)}, bf16[256,256]{1,0:T(8,128)(2,1)}, u32[]{:S(2)}, u32[]{:S(2)}) collective-permute-start(bf16[256,256]{1,0:T(8,128)(2,1)} %get-tuple-element.55), channel_id=1, source_target_pairs={{0,6},{1,7},{2,0},{3,1},{4,2},{5,3},{6,4},{7,5},{8,14},{9,15},{10,... | collective-permute-start | bytes 393224 | tf_op jit(solution)/shard_map/ppermute | solution.py:334
  52.6 1.9 %copy-start.5 = (bf16[3,2048,256]{2,1,0:T(8,128)(2,1)S(1)}, bf16[3,2048,256]{2,1,0:T(8,128)(2,1)}, u32[]{:S(2)}) copy-start(bf16[3,2048,256]{2,1,0:T(8,128)(2,1)} %near_ref.3) | copy-start | bytes 9437188
  59.9 17.0 %copy-start.11 = (bf16[32,2048]{1,0:T(8,128)(2,1)S(1)}, bf16[32,2048]{1,0:T(8,128)(2,1)}, u32[]{:S(2)}) copy-start(bf16[32,2048]{1,0:T(8,128)(2,1)} %basis_out_ref.3) | copy-start | bytes 393220
  59.9 17.0 %copy-start.13 = (bf16[32,2048]{1,0:T(8,128)(2,1)S(1)}, bf16[32,2048]{1,0:T(8,128)(2,1)}, u32[]{:S(2)}) copy-start(bf16[32,2048]{1,0:T(8,128)(2,1)} %basis_in_ref.1) | copy-start | bytes 393220
  77.0 16.1 %copy-start.2 = (bf16[4,2048,256]{2,1,0:T(8,128)(2,1)S(1)}, bf16[4,2048,256]{2,1,0:T(8,128)(2,1)}, u32[]{:S(2)}) copy-start(bf16[4,2048,256]{2,1,0:T(8,128)(2,1)} %fusion.matrix_ref) | copy-start | bytes 12582916
  82.2 6.9 %collective-permute-start.15 = (bf16[256,256]{1,0:T(8,128)(2,1)S(1)}, bf16[256,256]{1,0:T(8,128)(2,1)S(1)}, u32[]{:S(2)}, u32[]{:S(2)}) collective-permute-start(bf16[256,256]{1,0:T(8,128)(2,1)S(1)} %get-tuple-element.66.refs_0_), channel_id=1, source_target_pairs={{0,24},{8,0},{16,8},{24,16},{1,25},{9,1},{17,9},{25,17},{2,26},{10... | collective-permute-start | bytes 393224 | tf_op jit(solution)/shard_map/ppermute | solution.py:330
  84.0 7.6 %collective-permute-start.14 = (bf16[256,256]{1,0:T(8,128)(2,1)S(1)}, bf16[256,256]{1,0:T(8,128)(2,1)S(1)}, u32[]{:S(2)}, u32[]{:S(2)}) collective-permute-start(bf16[256,256]{1,0:T(8,128)(2,1)S(1)} %get-tuple-element.66.refs_0_), channel_id=1, source_target_pairs={{0,16},{8,24},{16,0},{24,8},{1,17},{9,25},{17,1},{25,9},{2,18},{10... | collective-permute-start | bytes 393224 | tf_op jit(solution)/shard_map/ppermute | solution.py:330
  84.0 7.6 %collective-permute-start.13 = (bf16[256,256]{1,0:T(8,128)(2,1)S(1)}, bf16[256,256]{1,0:T(8,128)(2,1)S(1)}, u32[]{:S(2)}, u32[]{:S(2)}) collective-permute-start(bf16[256,256]{1,0:T(8,128)(2,1)S(1)} %get-tuple-element.66.refs_0_), channel_id=1, source_target_pairs={{0,8},{8,16},{16,24},{24,0},{1,9},{9,17},{17,25},{25,1},{2,10},{10... | collective-permute-start | bytes 393224 | tf_op jit(solution)/shard_map/ppermute | solution.py:330
  84.7 6.9 %collective-permute-start.17 = (bf16[256,256]{1,0:T(8,128)(2,1)S(1)}, bf16[256,256]{1,0:T(8,128)(2,1)S(1)}, u32[]{:S(2)}, u32[]{:S(2)}) collective-permute-start(bf16[256,256]{1,0:T(8,128)(2,1)S(1)} %get-tuple-element.83), channel_id=1, source_target_pairs={{1,0},{2,1},{3,2},{4,3},{5,4},{6,5},{7,6},{8,7},{9,8},{10,9},{11,1... | collective-permute-start | bytes 393224 | tf_op jit(solution)/shard_map/ppermute | solution.py:343
  86.7 6.5 %collective-permute-start.16 = (bf16[256,256]{1,0:T(8,128)(2,1)S(1)}, bf16[256,256]{1,0:T(8,128)(2,1)S(1)}, u32[]{:S(2)}, u32[]{:S(2)}) collective-permute-start(bf16[256,256]{1,0:T(8,128)(2,1)S(1)} %get-tuple-element.84), channel_id=1, source_target_pairs={{0,1},{1,2},{2,3},{3,4},{4,5},{5,6},{6,7},{7,8},{8,9},{9,10},{10,1... | collective-permute-start | bytes 393224 | tf_op jit(solution)/shard_map/ppermute | solution.py:342
  95.2 2.2 %collective-permute-start.18 = (bf16[1024,256]{1,0:T(8,128)(2,1)S(1)}, bf16[1024,256]{1,0:T(8,128)(2,1)S(1)}, u32[]{:S(2)}, u32[]{:S(2)}) collective-permute-start(bf16[1024,256]{1,0:T(8,128)(2,1)S(1)} %shard_map.193), channel_id=1, source_target_pairs={{0,1},{1,0},{2,3},{3,2},{4,5},{5,4},{6,7},{7,6},{8,9},{9,8},{10,11... | collective-permute-start | bytes 1572872 | tf_op jit(solution)/shard_map/ppermute | solution.py:337
  95.3 10.2 %copy-start.6 = (bf16[3,2048,256]{2,1,0:T(8,128)(2,1)S(1)}, bf16[3,2048,256]{2,1,0:T(8,128)(2,1)}, u32[]{:S(2)}) copy-start(bf16[3,2048,256]{2,1,0:T(8,128)(2,1)} %near_ref.3) | copy-start | bytes 9437188
  95.3 10.2 %copy-start.8 = (f32[2048,256]{1,0:T(8,128)S(1)}, f32[2048,256]{1,0:T(8,128)}, u32[]{:S(2)}) copy-start(f32[2048,256]{1,0:T(8,128)} %state_ref.3) | copy-start | bytes 6291460
  97.5 11.9 %collective-permute-start.19 = (bf16[256,256]{1,0:T(8,128)(2,1)S(1)}, bf16[256,256]{1,0:T(8,128)(2,1)S(1)}, u32[]{:S(2)}, u32[]{:S(2)}) collective-permute-start(bf16[256,256]{1,0:T(8,128)(2,1)S(1)} %get-tuple-element.71), channel_id=1, source_target_pairs={{0,2},{1,3},{2,4},{3,5},{4,6},{5,7},{6,0},{7,1},{8,10},{9,11},{10,... | collective-permute-start | bytes 393224 | tf_op jit(solution)/shard_map/ppermute | solution.py:334
  99.0 15.2 %collective-permute-start.20 = (bf16[256,256]{1,0:T(8,128)(2,1)S(1)}, bf16[256,256]{1,0:T(8,128)(2,1)S(1)}, u32[]{:S(2)}, u32[]{:S(2)}) collective-permute-start(bf16[256,256]{1,0:T(8,128)(2,1)S(1)} %get-tuple-element.72), channel_id=1, source_target_pairs={{0,4},{1,5},{2,6},{3,7},{4,0},{5,1},{6,2},{7,3},{8,12},{9,13},{10,... | collective-permute-start | bytes 393224 | tf_op jit(solution)/shard_map/ppermute | solution.py:334
  105.5 11.5 %collective-permute-start.21 = (bf16[256,256]{1,0:T(8,128)(2,1)S(1)}, bf16[256,256]{1,0:T(8,128)(2,1)S(1)}, u32[]{:S(2)}, u32[]{:S(2)}) collective-permute-start(bf16[256,256]{1,0:T(8,128)(2,1)S(1)} %get-tuple-element.73), channel_id=1, source_target_pairs={{0,6},{1,7},{2,0},{3,1},{4,2},{5,3},{6,4},{7,5},{8,14},{9,15},{10,... | collective-permute-start | bytes 393224 | tf_op jit(solution)/shard_map/ppermute | solution.py:334
  (13 other events, 12.8 us)
where the time goes:
time: 122 us; the launch traced here: 121 us
  Pallas kernels  43 us (35%)
  starting transfers between devices  36 us (30%)
  local copies, waits for them, and re-layouts  20.5 us (17%)
  waiting for transfers between devices  14 us (11%)
  other arithmetic  6.78 us (6%)
  between operations  1.27 us (1%)
    ppermute x9, starting transfers between devices, to_height(): return lax.ppermute(array, 'col', pairs)  19.5 us
    unnamed x79, local copies, waits for them, and re-layouts  18.1 us
    pallas_call x1, Pallas kernels, prepare_first(): pl.pallas_call(prepare_first_kernel, grid=(s.count,), in_specs=[slots, sl...  17 us
    ppermute x9, waiting for transfers between devices, to_height(): return lax.ppermute(array, 'col', pairs)  9.91 us
    pallas_call x4, Pallas kernels, couple(): pl.pallas_call(functools.partial(couple_kernel, sources), grid_spec=grid_...  9.18 us
    ppermute x2, starting transfers between devices, halo(): after = lax.ppermute(rounded[:BS], both, down)  6.02 us
    ppermute x6, starting transfers between devices, to_row(): lax.ppermute(array, 'row', [(i, (i + d) % row_count) for i in range(row_c...  5.55 us
    pallas_call x1, Pallas kernels, finish_first(): pl.pallas_call(functools.partial(finish_first_kernel, len(parts)), grid=(...  5.18 us
  transfers between devices with their start and end apart: 22, of which 5 were waited for; matrix products, arithmetic and copies ran while one was open for 8% of the time, Pallas kernels for 25%

commit v1 on v0

v1 whole, which is shorter than its diff:
```python
import functools

import jax
import jax.numpy as jnp
from jax import lax
from jax.experimental import pallas as pl
from jax.experimental.pallas import tpu as pltpu
from jax.sharding import PartitionSpec as P

BS = 256
R = 32

STEP_SIZE = 0.5
REF_FRICTION = 0.6
LIMIT = 16 * 1024 * 1024
F32 = jnp.float32
BF16 = jnp.bfloat16


def dot(a, b):
    return jnp.dot(a, b, preferred_element_type=F32)


def dot_t(a, b):
    return lax.dot_general(a, b, (((0,), (0,)), ((), ())), preferred_element_type=F32)


VMEM = pl.BlockSpec(memory_space=pltpu.VMEM)
SMEM = pl.BlockSpec(memory_space=pltpu.SMEM)


def call(kernel, outs, *operands, specs=None, **grid):
    return pl.pallas_call(
        kernel,
        in_specs=specs or [VMEM] * len(operands),
        out_shape=outs,
        compiler_params=pltpu.CompilerParams(vmem_limit_bytes=LIMIT),
        **grid,
    )(*operands)


def rows_at(n, size):
    return pl.ds(pl.multiple_of(n * size, size), size)


def project_kernel(slip_ref, basis_ref, coeff_ref, rounded_ref, first_ref, last_ref):
    count = slip_ref.shape[0] // BS

    @pl.loop(0, count)
    def _(n):
        at = rows_at(n, BS)
        rounded = slip_ref[at, :].astype(BF16)
        rounded_ref[at, :] = rounded
        coeff_ref[rows_at(n, R), :] = dot(basis_ref[:, at], rounded).astype(BF16)

    first_ref[...] = rounded_ref[:BS]
    last_ref[...] = rounded_ref[-BS:]


def project(slip, basis_in):
    patches, ens = slip.shape
    edge = jax.ShapeDtypeStruct((BS, ens), BF16)
    return call(
        project_kernel,
        [
            jax.ShapeDtypeStruct((patches // BS * R, ens), BF16),
            jax.ShapeDtypeStruct((patches, ens), BF16),
            edge,
            edge,
        ],
        slip,
        basis_in,
    )


def setup_kernel(
    load_ref, normal_ref, direct_ref, evolution_ref, distance_ref, stiffness_ref, bricks_ref, count_ref, weight_ref,
    now_ref, rate_ref, coeff_ref, numbers_ref, ids_ref, shares_ref, joined_ref,
):
    slots, patches = bricks_ref.shape
    ens = now_ref.shape[1]
    joined_ref[:, :ens] = now_ref[...]
    joined_ref[:, ens:] = rate_ref[...]

    @pl.loop(0, patches // BS)
    def _(n):
        at = rows_at(n, BS)
        evolution = evolution_ref[:, at]
        rows = [
            load_ref[:, at],
            normal_ref[:, at],
            1.0 / direct_ref[:, at],
            1.0 / evolution,
            evolution / distance_ref[:, at],
            stiffness_ref[:, at],
        ]
        rows = rows + rows[:2]
        numbers_ref[at, :] = jnp.concatenate(rows, axis=0).T
        bricks = bricks_ref[:, at]
        slot = lax.broadcasted_iota(jnp.int32, (slots, BS), 0)
        weights = jnp.where(slot < count_ref[:, at], weight_ref[:, at], 0.0)
        merged = jnp.zeros((slots, BS), F32)
        for k in range(slots):
            merged = merged + jnp.where(bricks == bricks[k : k + 1], weights[k : k + 1], 0.0)
        shares = merged / jnp.sum(weights, axis=0, keepdims=True)
        ids_ref[at, :] = bricks.T.astype(jnp.int32).astype(jnp.int16)
        shares_ref[at, :] = shares.T.astype(BF16)


def weights_kernel(ids_ref, shares_ref, matrix_ref):
    patches, slots = ids_ref.shape
    rows = 32

    @pl.loop(0, patches // rows)
    def _(n):
        at = rows_at(n, rows)
        ids, shares = ids_ref[at, :], shares_ref[at, :]
        id_of = [jnp.broadcast_to(ids[:, k : k + 1], (rows, 128)) for k in range(slots)]
        share_of = [jnp.broadcast_to(shares[:, k : k + 1], (rows, 128)) for k in range(slots)]
        lane = lax.broadcasted_iota(jnp.int32, (rows, 128), 1).astype(jnp.int16)
        for left in range(0, matrix_ref.shape[1], 128):
            here = lane + jnp.int16(left)
            tile = jnp.zeros((rows, 128), BF16)
            for k in range(slots):
                tile = jnp.where(id_of[k] == here, share_of[k], tile)
            matrix_ref[at, left : left + 128] = tile


def couple_kernel(sources, heights, where_ref, matrix_ref, *refs):
    coeffs, out_ref = refs[:sources], refs[sources]
    share = coeffs[0].shape[0]

    @pl.loop(0, heights)
    def _(d):
        height = lax.rem(where_ref[0] + d, heights)
        at = rows_at(2 * height + where_ref[1], share)
        total = None
        for step in range(sources):
            term = dot(matrix_ref[where_ref[2 + step], at, :], coeffs[step][...])
            total = term if total is None else total + term
        out_ref[rows_at(d, share), :] = total.astype(out_ref.dtype)


def couple(where, matrix, coeffs, heights, kind):
    share, ens = coeffs[0].shape
    return call(
        functools.partial(couple_kernel, len(coeffs), heights),
        jax.ShapeDtypeStruct((heights * share, ens), kind),
        where,
        matrix,
        *coeffs,
        specs=[SMEM] + [VMEM] * (1 + len(coeffs)),
    )


def chip_sum_kernel(kept_ref, sent_ref, *outs):
    share = outs[0].shape[0]
    for d, out_ref in enumerate(outs):

        @pl.loop(0, share // 32)
        def _(n):
            at = pl.ds(pl.multiple_of(d * share + n * 32, 32), 32)
            out_ref[rows_at(n, 32), :] = (kept_ref[at, :] + sent_ref[at, :].astype(F32)).astype(BF16)


def chip_sum(kept, sent, heights):
    rows, ens = kept.shape
    return list(call(chip_sum_kernel, [jax.ShapeDtypeStruct((rows // heights, ens), BF16)] * heights, kept, sent))


def near_tau(n, slip, numbers, near_ref, rounded_ref, first_ref, last_ref):
    count = rounded_ref.shape[0] // BS
    at = rows_at(n, BS)
    before = jnp.where(n == 0, first_ref[...], rounded_ref[rows_at(jnp.maximum(n - 1, 0), BS), :])
    after = jnp.where(n == count - 1, last_ref[...], rounded_ref[rows_at(jnp.minimum(n + 1, count - 1), BS), :])
    near = dot(near_ref[0, at, :], before) + dot(near_ref[1, at, :], rounded_ref[at, :]) + dot(near_ref[2, at, :], after)
    return numbers[:, 0:1] - numbers[:, 5:6] * slip - near


def prepare_first_kernel(
    matrix_ref, own_ref, other_ref, slip_ref, state_ref, numbers_ref, near_ref, rounded_ref, first_ref,
    last_ref, shift_ref, scale_ref, rest_ref, scale_mid_ref,
):
    half = own_ref.shape[0]
    patches, ens = slip_ref.shape

    @pl.loop(0, patches // BS)
    def _(n):
        at = rows_at(n, BS)
        total = dot(matrix_ref[at, :half], own_ref[...]) + dot(matrix_ref[at, half:], other_ref[...])
        numbers = numbers_ref[at, :]
        normal, inv_direct, inv_evolution, ratio = (numbers[:, k : k + 1] for k in range(1, 5))
        base = total[:, :ens]
        scale = inv_direct / (normal - base)
        scale_ref[at, :] = scale
        scale_mid_ref[at, :] = inv_direct / (normal - (base + STEP_SIZE * total[:, ens:]))
        state = state_ref[at, :]
        tau = near_tau(n, slip_ref[at, :], numbers, near_ref, rounded_ref, first_ref, last_ref)
        shift_ref[at, :] = tau * scale - state * inv_direct
        rest_ref[at, :] = state + (STEP_SIZE * ratio) * jnp.exp((REF_FRICTION - state) * inv_evolution)


def far_speed(n, shift_ref, scale_ref, basis_ref, parts):
    at = rows_at(n, BS)
    levels = rows_at(n, R)
    far = parts[0][levels, :].astype(F32)
    for part in parts[1:]:
        far = far + part[levels, :].astype(F32)
    return jnp.exp(shift_ref[at, :] - scale_ref[at, :] * dot_t(basis_ref[:, at], far.astype(BF16)))


def finish_first_kernel(
    heights, shift_ref, scale_ref, rest_ref, slip_ref, numbers_ref, basis_out_ref, basis_in_ref, *refs
):
    parts = refs[:heights]
    slip_mid_ref, state_mid_ref, rounded_ref, coeff_ref, first_ref, last_ref = refs[heights:]

    @pl.loop(0, slip_ref.shape[0] // BS)
    def _(n):
        at = rows_at(n, BS)
        speed = far_speed(n, shift_ref, scale_ref, basis_out_ref, parts)
        slip_mid = slip_ref[at, :] + STEP_SIZE * speed
        slip_mid_ref[at, :] = slip_mid
        state_mid_ref[at, :] = rest_ref[at, :] - (STEP_SIZE * numbers_ref[at, 4:5]) * speed
        rounded = slip_mid.astype(BF16)
        rounded_ref[at, :] = rounded
        coeff_ref[rows_at(n, R), :] = dot(basis_in_ref[:, at], rounded).astype(BF16)

    first_ref[...] = rounded_ref[:BS]
    last_ref[...] = rounded_ref[-BS:]


def prepare_second_kernel(
    slip_ref, state_ref, slip_mid_ref, state_mid_ref, scale_ref, numbers_ref, near_ref, rounded_ref, first_ref,
    last_ref, shift_ref, slip_rest_ref, rest_ref,
):
    @pl.loop(0, slip_ref.shape[0] // BS)
    def _(n):
        at = rows_at(n, BS)
        numbers = numbers_ref[at, :]
        inv_direct, inv_evolution, ratio = (numbers[:, k : k + 1] for k in range(2, 5))
        slip = slip_mid_ref[at, :]
        state = state_mid_ref[at, :]
        tau = near_tau(n, slip, numbers, near_ref, rounded_ref, first_ref, last_ref)
        shift_ref[at, :] = tau * scale_ref[at, :] - state * inv_direct
        slip_rest_ref[at, :] = 0.5 * (slip_ref[at, :] + slip)
        friction = jnp.exp((REF_FRICTION - state) * inv_evolution)
        rest_ref[at, :] = 0.5 * (state_ref[at, :] + state) + (0.5 * STEP_SIZE * ratio) * friction


def finish_second_kernel(heights, shift_ref, scale_ref, rest_ref, slip_rest_ref, numbers_ref, basis_out_ref, *refs):
    parts, (slip_out_ref, state_out_ref) = refs[:heights], refs[heights:]
    n = pl.program_id(0)
    at = rows_at(n, BS)
    speed = far_speed(n, shift_ref, scale_ref, basis_out_ref, parts)
    slip_out_ref[...] = slip_rest_ref[at, :] + (0.5 * STEP_SIZE) * speed
    state_out_ref[...] = rest_ref[at, :] - (0.5 * STEP_SIZE * numbers_ref[at, 4:5]) * speed


def masked_coupling(coupling, block_rank, row_index, col_index, row_count, col_count):
    rows, sources, width = coupling.shape
    share = width // R
    blocks = rows // R
    receiver = row_index * blocks + jnp.arange(blocks, dtype=jnp.int32)
    source = (
        (jnp.arange(sources, dtype=jnp.int32)[:, None] * col_count + col_index) * share
        + jnp.arange(share, dtype=jnp.int32)[None, :]
    )
    apart = jnp.abs(receiver[:, None, None] - source[None]) > 1
    rank = jnp.where(apart, block_rank, 0)
    rank = jnp.transpose(rank, (1, 0, 2))
    rank_full = jnp.repeat(rank, R, axis=2).reshape(sources, blocks, 1, width)
    level = jnp.maximum(
        jnp.arange(R, dtype=jnp.int32)[:, None], jnp.arange(width, dtype=jnp.int32)[None, :] % R
    )
    keep = level[None, None] < rank_full
    matrix = jnp.transpose(coupling, (1, 0, 2)).reshape(sources, blocks, R, width)
    return jnp.where(keep, matrix, jnp.zeros((), BF16)).reshape(sources, rows, width)


def per_device(
    slip,
    state,
    tau_load,
    normal_stress,
    direct_effect,
    evolution_effect,
    slip_distance,
    self_stiffness,
    near_blocks,
    basis_in,
    basis_out,
    coupling,
    block_rank,
    adj_bricks,
    adj_count,
    adj_weight,
    pressure_now,
    pressure_rate,
):
    row_count = lax.axis_size("row")
    col_count = lax.axis_size("col")
    row_index = lax.axis_index("row")
    col_index = lax.axis_index("col")
    heights = col_count // 2
    height, core = col_index // 2, col_index % 2
    both = ("row", "col")
    devices = row_count * col_count

    def to_row(array, d):
        return lax.ppermute(array, "row", [(i, (i + d) % row_count) for i in range(row_count)])

    def to_height(array, d):
        pairs = [(2 * z + k, 2 * ((z + d) % heights) + k) for z in range(heights) for k in range(2)]
        return lax.ppermute(array, "col", pairs)

    def to_core(array):
        return lax.ppermute(array, "col", [(2 * z + k, 2 * z + 1 - k) for z in range(heights) for k in range(2)])

    def halo(first, last):
        up = [(i, i + 1) for i in range(devices - 1)]
        down = [(j, i) for i, j in up]
        return lax.ppermute(last, both, up), lax.ppermute(first, both, down)

    patches, ens = slip.shape
    slots = adj_bricks.shape[0]
    size = pressure_now.shape[0]
    share = coupling.shape[2]
    owner, within = adj_bricks // size, adj_bricks % size
    away = (height - owner // 2) % heights
    other_core = (owner % 2 != core).astype(jnp.int32)
    live = adj_count[None, :] > jnp.arange(slots, dtype=jnp.int32)[:, None]
    bricks = jnp.where(live, (other_core * heights + away) * size + within, -1).astype(F32)
    masked = masked_coupling(coupling, block_rank, row_index, col_index, row_count, col_count)
    source_rows = [(row_index - d) % row_count for d in range(row_count)]
    own_where = jnp.stack([height, core] + source_rows).astype(jnp.int32)
    pair_where = jnp.stack([height, 1 - core] + source_rows).astype(jnp.int32)

    def far_parts(coeffs):
        sent = to_core(couple(pair_where, masked, coeffs, heights, BF16))
        kept = couple(own_where, masked, coeffs, heights, F32)
        pieces = chip_sum(kept, sent, heights)
        return pieces[:1] + [to_height(pieces[d], d) for d in range(1, heights)]

    def row_coeffs(coeff):
        return [coeff] + [to_row(coeff, d) for d in range(1, row_count)]

    full = jax.ShapeDtypeStruct((patches, ens), F32)
    half = jax.ShapeDtypeStruct((patches, ens), BF16)
    edge = jax.ShapeDtypeStruct((BS, ens), BF16)
    per_patch = [tau_load, normal_stress, direct_effect, evolution_effect, slip_distance, self_stiffness]

    coeff, rounded, first, last = project(slip, basis_in)
    coeffs = row_coeffs(coeff)
    numbers, ids, shares, joined = call(
        setup_kernel,
        [
            jax.ShapeDtypeStruct((patches, 8), F32),
            jax.ShapeDtypeStruct((patches, slots), jnp.int16),
            jax.ShapeDtypeStruct((patches, slots), BF16),
            jax.ShapeDtypeStruct((size, 2 * ens), BF16),
        ],
        *[array[None] for array in per_patch],
        bricks,
        adj_count[None],
        adj_weight,
        pressure_now,
        pressure_rate,
        coeff,
    )
    own = jnp.concatenate([joined] + [to_height(joined, d) for d in range(1, heights)], axis=0)
    other = to_core(own)
    first, last = halo(first, last)
    coeffs, first, last = lax.optimization_barrier((coeffs, first, last))
    parts = far_parts(coeffs)
    matrix = call(
        weights_kernel, jax.ShapeDtypeStruct((patches, 2 * heights * size), BF16), ids, shares
    )
    shift, scale, rest, scale_mid = call(
        prepare_first_kernel, [full] * 4, matrix, own, other, slip, state, numbers, near_blocks, rounded, first, last
    )
    slip_mid, state_mid, rounded, coeff, first, last = call(
        functools.partial(finish_first_kernel, heights),
        [full, full, half, jax.ShapeDtypeStruct((patches // BS * R, ens), BF16), edge, edge],
        shift, scale, rest, slip, numbers, basis_out, basis_in, *parts,
    )
    coeffs = row_coeffs(coeff)
    first, last = halo(first, last)
    coeffs, first, last = lax.optimization_barrier((coeffs, first, last))
    parts = far_parts(coeffs)
    shift, slip_rest, rest = call(
        prepare_second_kernel, [full] * 3,
        slip, state, slip_mid, state_mid, scale_mid, numbers, near_blocks, rounded, first, last,
    )
    slip_out, state_out = call(
        functools.partial(finish_second_kernel, heights),
        [full] * 2,
        shift, scale_mid, rest, slip_rest, numbers, basis_out, *parts,
        grid=(patches // BS,),
        out_specs=[pl.BlockSpec((BS, ens), lambda n: (n, 0))] * 2,
    )
    return (slip_out, state_out)


def solution(mesh):
    in_specs = (
        P(("row", "col"), None),
        P(("row", "col"), None),
        P(("row", "col")),
        P(("row", "col")),
        P(("row", "col")),
        P(("row", "col")),
        P(("row", "col")),
        P(("row", "col")),
        P(None, ("row", "col"), None),
        P(None, ("row", "col")),
        P(None, ("row", "col")),
        P("row", None, "col"),
        P("row", None, "col"),
        P(None, ("row", "col")),
        P(("row", "col")),
        P(None, ("row", "col")),
        P("col", None),
        P("col", None),
    )
    out_specs = (P(("row", "col"), None), P(("row", "col"), None))
    return jax.shard_map(
        per_device, mesh=mesh, in_specs=in_specs, out_specs=out_specs, check_vma=False
    )
```

time: 122 us -> 120 us (0.984)
  the two profiles are of different devices: /device:TPU:12 before, /device:TPU:11 now
where the time goes in v1:
time: 120 us; the launch traced here: 119 us
  Pallas kernels  42.2 us (35%)
  starting transfers between devices  34.9 us (29%)
  local copies, waits for them, and re-layouts  20.4 us (17%)
  waiting for transfers between devices  14.1 us (12%)
  other arithmetic  5.83 us (5%)
    pallas_call x13, Pallas kernels, call(): pl.pallas_call(kernel, in_specs=specs or [VMEM] * len(operands), out_shap...  42.2 us
    unnamed x53, local copies, waits for them, and re-layouts  16.5 us
    ppermute x9, starting transfers between devices, to_height(): return lax.ppermute(array, 'col', pairs)  15 us
    ppermute x4, starting transfers between devices, halo(): return (lax.ppermute(last, both, up), lax.ppermute(first, both, down))  12.8 us
    ppermute x9, waiting for transfers between devices, to_height(): return lax.ppermute(array, 'col', pairs)  8.25 us
    ppermute x4, waiting for transfers between devices, halo(): return (lax.ppermute(last, both, up), lax.ppermute(first, both, down))  5.73 us
    ppermute x6, starting transfers between devices, to_row(): lax.ppermute(array, 'row', [(i, (i + d) % row_count) for i in range(row_c...  5.07 us
    select_n x1, other arithmetic, masked_coupling(): jnp.where(keep, matrix, jnp.zeros((), BF16)).reshape(sources, rows, width)  4.91 us
  transfers between devices with their start and end apart: 22, of which 4 were waited for; matrix products, arithmetic and copies ran while one was open for 11% of the time, Pallas kernels for 26%

profile of v1, /device:TPU:11, one launch (start us, length us, event | category | flops | bytes accessed | tf_op | source)
XLA Modules:
  0.0 118.6 jit_solution(15846977230114685353)
XLA Ops:
  0.6 1.6 %copy-done.3 = f32[2048,256]{1,0:T(8,128)S(1)} copy-done((f32[2048,256]{1,0:T(8,128)S(1)}, f32[2048,256]{1,0:T(8,128)}, u32[]{:S(2)}) %copy-start.3) | copy-done | bytes 2097176
  2.2 0.9 copy-done.8
  3.1 1.9 %shard_map.185 = (bf16[256,256]{1,0:T(8,128)(2,1)S(1)}, bf16[2048,256]{1,0:T(8,128)(2,1)S(1)}, bf16[256,256]{1,0:T(8,128)(2,1)}, bf16[256,256]{1,0:T(8,128)(2,1)}) custom-call(f32[2048,256]{1,0:T(8,128)S(1)} %copy-done.3, bf16[32,2048]{1,0:T(8,128)(2,1)S(1)} %copy-done.8), custom_call_target="tpu_custom_call" | custom-call | tf_op jit(solution)/shard_map/pallas_call | solution.py:33
  5.0 1.2 %collective-permute-start.4 = (bf16[256,256]{1,0:T(8,128)(2,1)S(1)}, bf16[256,256]{1,0:T(8,128)(2,1)S(1)}, u32[]{:S(2)}, u32[]{:S(2)}) collective-permute-start(bf16[256,256]{1,0:T(8,128)(2,1)S(1)} %get-tuple-element.56.coeff_ref.refs_0_), channel_id=1, source_target_pairs={{0,8},{8,16},{16,24},{24,0},{1,9},{9,17},{17,25},{25,1},{2,10},{10... | collective-permute-start | bytes 393224 | tf_op jit(solution)/shard_map/ppermute | solution.py:311
  6.5 1.3 %collective-permute-start.6 = (bf16[256,256]{1,0:T(8,128)(2,1)S(1)}, bf16[256,256]{1,0:T(8,128)(2,1)}, u32[]{:S(2)}, u32[]{:S(2)}) collective-permute-start(bf16[256,256]{1,0:T(8,128)(2,1)S(1)} %get-tuple-element.56.coeff_ref.refs_0_), channel_id=1, source_target_pairs={{0,24},{8,0},{16,8},{24,16},{1,25},{9,1},{17,9},{25,17},{2,26},{10... | collective-permute-start | bytes 393224 | tf_op jit(solution)/shard_map/ppermute | solution.py:311
  7.9 0.8 copy-done.12
  8.8 0.8 copy-done.13
  9.6 0.8 copy-done.14
  11.1 0.7 copy-done.18
  11.8 0.7 copy-done.19
  12.5 0.7 copy-done.20
  13.9 2.0 %shard_map.186 = (f32[2048,8]{1,0:T(8,128)S(1)}, s16[2048,8]{1,0:T(8,128)(2,1)S(1)}, bf16[2048,8]{1,0:T(8,128)(2,1)S(1)}, bf16[128,512]{1,0:T(8,128)(2,1)}) custom-call(f32[1,2048]{1,0:T(1,128)S(1)} %bitcast.25, f32[1,2048]{1,0:T(1,128)S(1)} %bitcast.26, f32[1,2048]{1,0:T(1,128)S(1)} %bitcast.27, f32[1,2048]{1,0:T(1,128)S(1)} %bitcast.28, ...), custom_call_target="tpu_custom_call" | custom-call | tf_op jit(solution)/shard_map/pallas_call | solution.py:33
  15.9 0.8 copy-done.10
  16.7 1.3 %collective-permute-start = (bf16[128,512]{1,0:T(8,128)(2,1)}, bf16[128,512]{1,0:T(8,128)(2,1)}, u32[]{:S(2)}, u32[]{:S(2)}) collective-permute-start(bf16[128,512]{1,0:T(8,128)(2,1)} %get-tuple-element.46), channel_id=1, source_target_pairs={{0,2},{1,3},{2,4},{3,5},{4,6},{5,7},{6,0},{7,1},{8,10},{9,11},{10,... | collective-permute-start | bytes 393224 | tf_op jit(solution)/shard_map/ppermute | solution.py:315
  18.0 4.9 %collective-permute-start.7 = (bf16[256,256]{1,0:T(8,128)(2,1)}, bf16[256,256]{1,0:T(8,128)(2,1)}, u32[]{:S(2)}, u32[]{:S(2)}) collective-permute-start(bf16[256,256]{1,0:T(8,128)(2,1)} %get-tuple-element.49), channel_id=1, source_target_pairs={{0,1},{1,2},{2,3},{3,4},{4,5},{5,6},{6,7},{7,8},{8,9},{9,10},{10,1... | collective-permute-start | bytes 393224 | tf_op jit(solution)/shard_map/ppermute | solution.py:323
  23.1 1.9 %collective-permute-start.8 = (bf16[256,256]{1,0:T(8,128)(2,1)}, bf16[256,256]{1,0:T(8,128)(2,1)}, u32[]{:S(2)}, u32[]{:S(2)}) collective-permute-start(bf16[256,256]{1,0:T(8,128)(2,1)} %get-tuple-element.50), channel_id=1, source_target_pairs={{1,0},{2,1},{3,2},{4,3},{5,4},{6,5},{7,6},{8,7},{9,8},{10,9},{11,1... | collective-permute-start | bytes 393224 | tf_op jit(solution)/shard_map/ppermute | solution.py:323
  25.6 1.8 %collective-permute-start.1 = (bf16[128,512]{1,0:T(8,128)(2,1)}, bf16[128,512]{1,0:T(8,128)(2,1)}, u32[]{:S(2)}, u32[]{:S(2)}) collective-permute-start(bf16[128,512]{1,0:T(8,128)(2,1)} %get-tuple-element.46), channel_id=1, source_target_pairs={{0,4},{1,5},{2,6},{3,7},{4,0},{5,1},{6,2},{7,3},{8,12},{9,13},{10,... | collective-permute-start | bytes 393224 | tf_op jit(solution)/shard_map/ppermute | solution.py:315
  27.4 0.9 constant_dynamic-update-slice_fusion.3
  28.4 0.8 broadcast_in_dim.51
  29.2 1.9 %copy.22 = s32[4,64,256]{2,1,0:T(8,128)} copy(s32[4,64,256]{1,2,0:T(8,128)} %bitcast.32) | data formatting | bytes 524288 | tf_op jit(solution)/shard_map/lt | solution.py:276
  31.1 1.0 lt.73
  32.2 4.9 %fusion.matrix_ref = bf16[4,2048,256]{2,1,0:T(8,128)(2,1)} fusion(bf16[2048,4,256]{2,1,0:T(4,128)(2,1)} %param.29, s32[4,64,256]{2,1,0:T(8,128)S(1)} %copy-done.22, s32[2048,256]{1,0:T(8,128)S(1)} %bitcast.31), kind=kLoop, calls=%fused_computation.1 | loop fusion | flops 4194304 | bytes 10747904 | tf_op jit(solution)/shard_map/jit(_where)/select_n | solution.py:278
  37.2 2.2 %copy-done = bf16[4,2048,256]{2,1,0:T(8,128)(2,1)S(1)} copy-done((bf16[4,2048,256]{2,1,0:T(8,128)(2,1)S(1)}, bf16[4,2048,256]{2,1,0:T(8,128)(2,1)}, u32[]{:S(2)}) %copy-start) | copy-done | bytes 4194328
  39.4 2.9 %shard_map.190 = bf16[1024,256]{1,0:T(8,128)(2,1)} custom-call(s32[6]{0:T(128)S(1)} %stack.40.where_ref, bf16[4,2048,256]{2,1,0:T(8,128)(2,1)S(1)} %copy-done, bf16[256,256]{1,0:T(8,128)(2,1)S(1)} %get-tuple-element.56.coeff_ref.refs_0_, bf16[256,256]{1,0:T(8,128)(2,1)S(1)} %collective-permute-done.4.refs_1_, ...), custom_call_target="tpu_custom_call" | custom-call | tf_op jit(solution)/shard_map/pallas_call | solution.py:33
  42.3 1.9 %collective-permute-start.9 = (bf16[1024,256]{1,0:T(8,128)(2,1)}, bf16[1024,256]{1,0:T(8,128)(2,1)}, u32[]{:S(2)}, u32[]{:S(2)}) collective-permute-start(bf16[1024,256]{1,0:T(8,128)(2,1)} %shard_map.190), channel_id=1, source_target_pairs={{0,1},{1,0},{2,3},{3,2},{4,5},{5,4},{6,7},{7,6},{8,9},{9,8},{10,11... | collective-permute-start | bytes 1572872 | tf_op jit(solution)/shard_map/ppermute | solution.py:318
  44.3 0.9 constant_dynamic-update-slice_fusion.2
  45.2 0.9 constant_dynamic-update-slice_fusion.1
  46.3 2.2 %copy-done.1 = bf16[4,2048,256]{2,1,0:T(8,128)(2,1)S(1)} copy-done((bf16[4,2048,256]{2,1,0:T(8,128)(2,1)S(1)}, bf16[4,2048,256]{2,1,0:T(8,128)(2,1)}, u32[]{:S(2)}) %copy-start.1) | copy-done | bytes 4194328
  48.5 2.3 %shard_map.189.kept_ref = f32[1024,256]{1,0:T(8,128)S(1)} custom-call(s32[6]{0:T(128)S(1)} %stack.38.where_ref, bf16[4,2048,256]{2,1,0:T(8,128)(2,1)S(1)} %copy-done.1, bf16[256,256]{1,0:T(8,128)(2,1)S(1)} %get-tuple-element.56.coeff_ref.refs_0_, bf16[256,256]{1,0:T(8,128)(2,1)S(1)} %collective-permute-done.4.refs_1_, ...), custom_call_target="tpu_custom_call" | custom-call | tf_op jit(solution)/shard_map/pallas_call | solution.py:33
  50.8 1.3 %shard_map.191 = (bf16[256,256]{1,0:T(8,128)(2,1)S(1)}, bf16[256,256]{1,0:T(8,128)(2,1)S(1)}, bf16[256,256]{1,0:T(8,128)(2,1)S(1)}, bf16[256,256]{1,0:T(8,128)(2,1)S(1)}) custom-call(f32[1024,256]{1,0:T(8,128)S(1)} %shard_map.189.kept_ref, bf16[1024,256]{1,0:T(8,128)(2,1)} %collective-permute-done.9.sent_ref), custom_call_target="tpu_custom_call" | custom-call | tf_op jit(solution)/shard_map/pallas_call | solution.py:33
  52.1 1.3 %collective-permute-start.10 = (bf16[256,256]{1,0:T(8,128)(2,1)S(1)}, bf16[256,256]{1,0:T(8,128)(2,1)S(1)}, u32[]{:S(2)}, u32[]{:S(2)}) collective-permute-start(bf16[256,256]{1,0:T(8,128)(2,1)S(1)} %get-tuple-element.61), channel_id=1, source_target_pairs={{0,2},{1,3},{2,4},{3,5},{4,6},{5,7},{6,0},{7,1},{8,10},{9,11},{10,... | collective-permute-start | bytes 393224 | tf_op jit(solution)/shard_map/ppermute | solution.py:315
  53.4 1.8 %collective-permute-start.11 = (bf16[256,256]{1,0:T(8,128)(2,1)S(1)}, bf16[256,256]{1,0:T(8,128)(2,1)S(1)}, u32[]{:S(2)}, u32[]{:S(2)}) collective-permute-start(bf16[256,256]{1,0:T(8,128)(2,1)S(1)} %get-tuple-element.62), channel_id=1, source_target_pairs={{0,4},{1,5},{2,6},{3,7},{4,0},{5,1},{6,2},{7,3},{8,12},{9,13},{10,... | collective-permute-start | bytes 393224 | tf_op jit(solution)/shard_map/ppermute | solution.py:315
  55.2 1.1 collective-permute-start.12
  56.3 12.0 %shard_map.187.matrix_ref = bf16[2048,1024]{1,0:T(8,128)(2,1)S(1)} custom-call(s16[2048,8]{1,0:T(8,128)(2,1)S(1)} %get-tuple-element.44.ids_ref, bf16[2048,8]{1,0:T(8,128)(2,1)S(1)} %copy-done.11), custom_call_target="tpu_custom_call" | custom-call | tf_op jit(solution)/shard_map/pallas_call | solution.py:33
  68.3 5.8 %shard_map.188 = (f32[2048,256]{1,0:T(8,128)S(1)}, f32[2048,256]{1,0:T(8,128)S(1)}, f32[2048,256]{1,0:T(8,128)S(1)}, f32[2048,256]{1,0:T(8,128)S(1)}) custom-call(bf16[2048,1024]{1,0:T(8,128)(2,1)S(1)} %shard_map.187.matrix_ref, bf16[512,512]{1,0:T(8,128)(2,1)S(1)} %constant_dynamic-update-slice_fusion.own_ref, ...), custom_call_target="tpu_custom_call" | custom-call | tf_op jit(solution)/shard_map/pallas_call | solution.py:33
  74.2 3.1 %shard_map.192 = (f32[2048,256]{1,0:T(8,128)S(1)}, f32[2048,256]{1,0:T(8,128)S(1)}, bf16[2048,256]{1,0:T(8,128)(2,1)S(1)}, bf16[256,256]{1,0:T(8,128)(2,1)S(1)},...) custom-call(f32[2048,256]{1,0:T(8,128)S(1)} %get-tuple-element.53.shift_ref, ...), custom_call_target="tpu_custom_call" | custom-call | tf_op jit(solution)/shard_map/pallas_call | solution.py:33
  77.3 2.0 %collective-permute-start.13 = (bf16[256,256]{1,0:T(8,128)(2,1)S(1)}, bf16[256,256]{1,0:T(8,128)(2,1)S(1)}, u32[]{:S(2)}, u32[]{:S(2)}) collective-permute-start(bf16[256,256]{1,0:T(8,128)(2,1)S(1)} %get-tuple-element.76.refs_0_), channel_id=1, source_target_pairs={{0,8},{8,16},{16,24},{24,0},{1,9},{9,17},{17,25},{25,1},{2,10},{10... | collective-permute-start | bytes 393224 | tf_op jit(solution)/shard_map/ppermute | solution.py:311
  79.7 4.1 %collective-permute-start.16 = (bf16[256,256]{1,0:T(8,128)(2,1)S(1)}, bf16[256,256]{1,0:T(8,128)(2,1)S(1)}, u32[]{:S(2)}, u32[]{:S(2)}) collective-permute-start(bf16[256,256]{1,0:T(8,128)(2,1)S(1)} %get-tuple-element.69), channel_id=1, source_target_pairs={{0,1},{1,2},{2,3},{3,4},{4,5},{5,6},{6,7},{7,8},{8,9},{9,10},{10,1... | collective-permute-start | bytes 393224 | tf_op jit(solution)/shard_map/ppermute | solution.py:323
  83.7 1.9 %collective-permute-start.17 = (bf16[256,256]{1,0:T(8,128)(2,1)S(1)}, bf16[256,256]{1,0:T(8,128)(2,1)S(1)}, u32[]{:S(2)}, u32[]{:S(2)}) collective-permute-start(bf16[256,256]{1,0:T(8,128)(2,1)S(1)} %get-tuple-element.70), channel_id=1, source_target_pairs={{1,0},{2,1},{3,2},{4,3},{5,4},{6,5},{7,6},{8,7},{9,8},{10,9},{11,1... | collective-permute-start | bytes 393224 | tf_op jit(solution)/shard_map/ppermute | solution.py:323
  85.7 5.7 %collective-permute-done.17.last_ref = bf16[256,256]{1,0:T(8,128)(2,1)S(1)} collective-permute-done((bf16[256,256]{1,0:T(8,128)(2,1)S(1)}, bf16[256,256]{1,0:T(8,128)(2,1)S(1)}, u32[]{:S(2)}, u32[]{:S(2)}) %collective-permute-start.17) | collective-permute-done | bytes 131104 | tf_op jit(solution)/shard_map/ppermute | solution.py:323
  91.4 1.8 %shard_map.195 = bf16[1024,256]{1,0:T(8,128)(2,1)S(1)} custom-call(s32[6]{0:T(128)S(1)} %stack.40.where_ref, bf16[4,2048,256]{2,1,0:T(8,128)(2,1)S(1)} %copy-done.2, bf16[256,256]{1,0:T(8,128)(2,1)S(1)} %get-tuple-element.76.refs_0_, bf16[256,256]{1,0:T(8,128)(2,1)S(1)} %collective-permute-done.13.refs_1_, ...), custom_call_target="tpu_custom_call" | custom-call | tf_op jit(solution)/shard_map/pallas_call | solution.py:33
  93.3 1.8 %shard_map.194.kept_ref = f32[1024,256]{1,0:T(8,128)S(1)} custom-call(s32[6]{0:T(128)S(1)} %stack.38.where_ref, bf16[4,2048,256]{2,1,0:T(8,128)(2,1)S(1)} %copy-done.2, bf16[256,256]{1,0:T(8,128)(2,1)S(1)} %get-tuple-element.76.refs_0_, bf16[256,256]{1,0:T(8,128)(2,1)S(1)} %collective-permute-done.13.refs_1_, ...), custom_call_target="tpu_custom_call" | custom-call | tf_op jit(solution)/shard_map/pallas_call | solution.py:33
  95.5 6.3 %collective-permute-start.20 = (bf16[256,256]{1,0:T(8,128)(2,1)S(1)}, bf16[256,256]{1,0:T(8,128)(2,1)S(1)}, u32[]{:S(2)}, u32[]{:S(2)}) collective-permute-start(bf16[256,256]{1,0:T(8,128)(2,1)S(1)} %get-tuple-element.82), channel_id=1, source_target_pairs={{0,4},{1,5},{2,6},{3,7},{4,0},{5,1},{6,2},{7,3},{8,12},{9,13},{10,... | collective-permute-start | bytes 393224 | tf_op jit(solution)/shard_map/ppermute | solution.py:315
  101.8 1.4 %collective-permute-start.21 = (bf16[256,256]{1,0:T(8,128)(2,1)S(1)}, bf16[256,256]{1,0:T(8,128)(2,1)S(1)}, u32[]{:S(2)}, u32[]{:S(2)}) collective-permute-start(bf16[256,256]{1,0:T(8,128)(2,1)S(1)} %get-tuple-element.83), channel_id=1, source_target_pairs={{0,6},{1,7},{2,0},{3,1},{4,2},{5,3},{6,4},{7,5},{8,14},{9,15},{10,... | collective-permute-start | bytes 393224 | tf_op jit(solution)/shard_map/ppermute | solution.py:315
  103.2 2.7 %shard_map.193 = (f32[2048,256]{1,0:T(8,128)S(1)}, f32[2048,256]{1,0:T(8,128)S(1)}, f32[2048,256]{1,0:T(8,128)S(1)}) custom-call(f32[2048,256]{1,0:T(8,128)S(1)} %copy-done.4, f32[2048,256]{1,0:T(8,128)S(1)} %copy-done.6, f32[2048,256]{1,0:T(8,128)S(1)} %get-tuple-element.64.slip_mid_ref, f32[2048,256]{1,0:T(8,128)S(1)} %get-tuple-element.65.state_mid_ref, ...), custom_call_target="tpu_custom_call" | custom-call | tf_op jit(solution)/shard_map/pallas_call | solution.py:33
  105.9 4.1 %collective-permute-done.20.refs_2_ = bf16[256,256]{1,0:T(8,128)(2,1)S(1)} collective-permute-done((bf16[256,256]{1,0:T(8,128)(2,1)S(1)}, bf16[256,256]{1,0:T(8,128)(2,1)S(1)}, u32[]{:S(2)}, u32[]{:S(2)}) %collective-permute-start.20) | collective-permute-done | bytes 131104 | tf_op jit(solution)/shard_map/ppermute | solution.py:315
  110.0 4.2 %collective-permute-done.21.refs_3_ = bf16[256,256]{1,0:T(8,128)(2,1)S(1)} collective-permute-done((bf16[256,256]{1,0:T(8,128)(2,1)S(1)}, bf16[256,256]{1,0:T(8,128)(2,1)S(1)}, u32[]{:S(2)}, u32[]{:S(2)}) %collective-permute-start.21) | collective-permute-done | bytes 131104 | tf_op jit(solution)/shard_map/ppermute | solution.py:315
  114.1 4.5 %shard_map.197 = (f32[2048,256]{1,0:T(8,128)}, f32[2048,256]{1,0:T(8,128)}) custom-call(f32[2048,256]{1,0:T(8,128)S(1)} %get-tuple-element.73.shift_ref, f32[2048,256]{1,0:T(8,128)S(1)} %get-tuple-element.66.scale_ref, f32[2048,256]{1,0:T(8,128)S(1)} %get-tuple-element.74.rest_ref, f32[2048,256]{1,0:T(8,128)S(1)} %get-tuple-element.75.slip_rest_ref, ...), custom_call_target="tpu_custom_call" | custom-call | tf_op jit(solution)/shard_map/pallas_call | solution.py:33
  (76 shorter events, 3.8 us)
Async XLA Ops:
  0.6 1.6 %copy-start.3 = (f32[2048,256]{1,0:T(8,128)S(1)}, f32[2048,256]{1,0:T(8,128)}, u32[]{:S(2)}) copy-start(f32[2048,256]{1,0:T(8,128)} %slip_ref.7) | copy-start | bytes 6291460
  2.2 0.9 copy-start.8
  3.1 4.6 %copy-start.15 = (s32[2048]{0:T(1024)S(1)}, s32[2048]{0:T(1024)}, u32[]{:S(2)}) copy-start(s32[2048]{0:T(1024)} %param.32) | copy-start | bytes 24580
  3.1 4.6 %copy-start.23 = (s32[8,2048]{1,0:T(8,128)S(1)}, s32[8,2048]{1,0:T(8,128)}, u32[]{:S(2)}) copy-start(s32[8,2048]{1,0:T(8,128)} %param.31) | copy-start | bytes 196612
  3.1 4.8 %copy-start.16 = (f32[2048]{0:T(1024)S(1)}, f32[2048]{0:T(1024)}, u32[]{:S(2)}) copy-start(f32[2048]{0:T(1024)} %param.20) | copy-start | bytes 24580
  3.1 19.8 %copy-start.24 = (s32[64,4,8]{0,2,1:T(8,128)S(1)}, s32[64,4,8]{0,2,1:T(8,128)}, u32[]{:S(2)}) copy-start(s32[64,4,8]{0,2,1:T(8,128)} %param.30) | copy-start | bytes 24580
  5.0 18.0 %collective-permute-start.4 = (bf16[256,256]{1,0:T(8,128)(2,1)S(1)}, bf16[256,256]{1,0:T(8,128)(2,1)S(1)}, u32[]{:S(2)}, u32[]{:S(2)}) collective-permute-start(bf16[256,256]{1,0:T(8,128)(2,1)S(1)} %get-tuple-element.56.coeff_ref.refs_0_), channel_id=1, source_target_pairs={{0,8},{8,16},{16,24},{24,0},{1,9},{9,17},{17,25},{25,1},{2,10},{10... | collective-permute-start | bytes 393224 | tf_op jit(solution)/shard_map/ppermute | solution.py:311
  6.2 19.4 %collective-permute-start.5 = (bf16[256,256]{1,0:T(8,128)(2,1)S(1)}, bf16[256,256]{1,0:T(8,128)(2,1)S(1)}, u32[]{:S(2)}, u32[]{:S(2)}) collective-permute-start(bf16[256,256]{1,0:T(8,128)(2,1)S(1)} %get-tuple-element.56.coeff_ref.refs_0_), channel_id=1, source_target_pairs={{0,16},{8,24},{16,0},{24,8},{1,17},{9,25},{17,1},{25,9},{2,18},{10... | collective-permute-start | bytes 393224 | tf_op jit(solution)/shard_map/ppermute | solution.py:311
  6.5 30.7 %collective-permute-start.6 = (bf16[256,256]{1,0:T(8,128)(2,1)S(1)}, bf16[256,256]{1,0:T(8,128)(2,1)}, u32[]{:S(2)}, u32[]{:S(2)}) collective-permute-start(bf16[256,256]{1,0:T(8,128)(2,1)S(1)} %get-tuple-element.56.coeff_ref.refs_0_), channel_id=1, source_target_pairs={{0,24},{8,0},{16,8},{24,16},{1,25},{9,1},{17,9},{25,17},{2,26},{10... | collective-permute-start | bytes 393224 | tf_op jit(solution)/shard_map/ppermute | solution.py:311
  7.9 0.8 copy-start.12
  8.8 0.8 copy-start.13
  9.6 0.8 copy-start.14
  10.4 0.7 copy-start.17
  11.1 0.7 copy-start.18
  11.8 0.7 copy-start.19
  12.5 0.7 copy-start.20
  13.2 0.7 copy-start.21
  15.9 0.8 copy-start.10
  16.7 27.6 %collective-permute-start = (bf16[128,512]{1,0:T(8,128)(2,1)}, bf16[128,512]{1,0:T(8,128)(2,1)}, u32[]{:S(2)}, u32[]{:S(2)}) collective-permute-start(bf16[128,512]{1,0:T(8,128)(2,1)} %get-tuple-element.46), channel_id=1, source_target_pairs={{0,2},{1,3},{2,4},{3,5},{4,6},{5,7},{6,0},{7,1},{8,10},{9,11},{10,... | collective-permute-start | bytes 393224 | tf_op jit(solution)/shard_map/ppermute | solution.py:315
  18.0 19.2 %collective-permute-start.7 = (bf16[256,256]{1,0:T(8,128)(2,1)}, bf16[256,256]{1,0:T(8,128)(2,1)}, u32[]{:S(2)}, u32[]{:S(2)}) collective-permute-start(bf16[256,256]{1,0:T(8,128)(2,1)} %get-tuple-element.49), channel_id=1, source_target_pairs={{0,1},{1,2},{2,3},{3,4},{4,5},{5,6},{6,7},{7,8},{8,9},{9,10},{10,1... | collective-permute-start | bytes 393224 | tf_op jit(solution)/shard_map/ppermute | solution.py:323
  23.1 14.2 %collective-permute-start.8 = (bf16[256,256]{1,0:T(8,128)(2,1)}, bf16[256,256]{1,0:T(8,128)(2,1)}, u32[]{:S(2)}, u32[]{:S(2)}) collective-permute-start(bf16[256,256]{1,0:T(8,128)(2,1)} %get-tuple-element.50), channel_id=1, source_target_pairs={{1,0},{2,1},{3,2},{4,3},{5,4},{6,5},{7,6},{8,7},{9,8},{10,9},{11,1... | collective-permute-start | bytes 393224 | tf_op jit(solution)/shard_map/ppermute | solution.py:323
  25.6 19.6 %collective-permute-start.1 = (bf16[128,512]{1,0:T(8,128)(2,1)}, bf16[128,512]{1,0:T(8,128)(2,1)}, u32[]{:S(2)}, u32[]{:S(2)}) collective-permute-start(bf16[128,512]{1,0:T(8,128)(2,1)} %get-tuple-element.46), channel_id=1, source_target_pairs={{0,4},{1,5},{2,6},{3,7},{4,0},{5,1},{6,2},{7,3},{8,12},{9,13},{10,... | collective-permute-start | bytes 393224 | tf_op jit(solution)/shard_map/ppermute | solution.py:315
  31.1 1.1 copy-start.22
  37.2 8.9 %collective-permute-start.2 = (bf16[128,512]{1,0:T(8,128)(2,1)}, bf16[128,512]{1,0:T(8,128)(2,1)S(1)}, u32[]{:S(2)}, u32[]{:S(2)}) collective-permute-start(bf16[128,512]{1,0:T(8,128)(2,1)} %get-tuple-element.46), channel_id=1, source_target_pairs={{0,6},{1,7},{2,0},{3,1},{4,2},{5,3},{6,4},{7,5},{8,14},{9,15},{10,... | collective-permute-start | bytes 393224 | tf_op jit(solution)/shard_map/ppermute | solution.py:315
  37.2 2.2 %copy-start = (bf16[4,2048,256]{2,1,0:T(8,128)(2,1)S(1)}, bf16[4,2048,256]{2,1,0:T(8,128)(2,1)}, u32[]{:S(2)}) copy-start(bf16[4,2048,256]{2,1,0:T(8,128)(2,1)} %fusion.matrix_ref) | copy-start | bytes 12582916
  42.3 8.4 %collective-permute-start.9 = (bf16[1024,256]{1,0:T(8,128)(2,1)}, bf16[1024,256]{1,0:T(8,128)(2,1)}, u32[]{:S(2)}, u32[]{:S(2)}) collective-permute-start(bf16[1024,256]{1,0:T(8,128)(2,1)} %shard_map.190), channel_id=1, source_target_pairs={{0,1},{1,0},{2,3},{3,2},{4,5},{5,4},{6,7},{7,6},{8,9},{9,8},{10,11... | collective-permute-start | bytes 1572872 | tf_op jit(solution)/shard_map/ppermute | solution.py:318
  46.1 22.1 %collective-permute-start.3 = (bf16[512,512]{1,0:T(8,128)(2,1)S(1)}, bf16[512,512]{1,0:T(8,128)(2,1)}, u32[]{:S(2)}, u32[]{:S(2)}) collective-permute-start(bf16[512,512]{1,0:T(8,128)(2,1)S(1)} %constant_dynamic-update-slice_fusion.own_ref), channel_id=1, source_target_pairs={{0,1},{1,0},{2,3},{3,2},{4,5},{5,4},{6,7},{7,6},{8,9},{9,8},{10,11... | collective-permute-start | bytes 1572872 | tf_op jit(solution)/shard_map/ppermute | solution.py:318
  46.3 2.2 %copy-start.1 = (bf16[4,2048,256]{2,1,0:T(8,128)(2,1)S(1)}, bf16[4,2048,256]{2,1,0:T(8,128)(2,1)}, u32[]{:S(2)}) copy-start(bf16[4,2048,256]{2,1,0:T(8,128)(2,1)} %fusion.matrix_ref) | copy-start | bytes 12582916
  48.5 7.8 %copy-start.11 = (bf16[2048,8]{1,0:T(8,128)(2,1)S(1)}, bf16[2048,8]{1,0:T(8,128)(2,1)}, u32[]{:S(2)}) copy-start(bf16[2048,8]{1,0:T(8,128)(2,1)} %copy-done.10) | copy-start | bytes 98308
  48.5 19.8 %copy-start.6 = (f32[2048,256]{1,0:T(8,128)S(1)}, f32[2048,256]{1,0:T(8,128)}, u32[]{:S(2)}) copy-start(f32[2048,256]{1,0:T(8,128)} %state_ref.3) | copy-start | bytes 6291460
  52.1 22.1 %collective-permute-start.10 = (bf16[256,256]{1,0:T(8,128)(2,1)S(1)}, bf16[256,256]{1,0:T(8,128)(2,1)S(1)}, u32[]{:S(2)}, u32[]{:S(2)}) collective-permute-start(bf16[256,256]{1,0:T(8,128)(2,1)S(1)} %get-tuple-element.61), channel_id=1, source_target_pairs={{0,2},{1,3},{2,4},{3,5},{4,6},{5,7},{6,0},{7,1},{8,10},{9,11},{10,... | collective-permute-start | bytes 393224 | tf_op jit(solution)/shard_map/ppermute | solution.py:315
  53.4 20.8 %collective-permute-start.11 = (bf16[256,256]{1,0:T(8,128)(2,1)S(1)}, bf16[256,256]{1,0:T(8,128)(2,1)S(1)}, u32[]{:S(2)}, u32[]{:S(2)}) collective-permute-start(bf16[256,256]{1,0:T(8,128)(2,1)S(1)} %get-tuple-element.62), channel_id=1, source_target_pairs={{0,4},{1,5},{2,6},{3,7},{4,0},{5,1},{6,2},{7,3},{8,12},{9,13},{10,... | collective-permute-start | bytes 393224 | tf_op jit(solution)/shard_map/ppermute | solution.py:315
  55.2 19.0 %collective-permute-start.12 = (bf16[256,256]{1,0:T(8,128)(2,1)S(1)}, bf16[256,256]{1,0:T(8,128)(2,1)S(1)}, u32[]{:S(2)}, u32[]{:S(2)}) collective-permute-start(bf16[256,256]{1,0:T(8,128)(2,1)S(1)} %get-tuple-element.63), channel_id=1, source_target_pairs={{0,6},{1,7},{2,0},{3,1},{4,2},{5,3},{6,4},{7,5},{8,14},{9,15},{10,... | collective-permute-start | bytes 393224 | tf_op jit(solution)/shard_map/ppermute | solution.py:315
  56.3 12.0 %copy-start.4 = (f32[2048,256]{1,0:T(8,128)S(1)}, f32[2048,256]{1,0:T(8,128)}, u32[]{:S(2)}) copy-start(f32[2048,256]{1,0:T(8,128)} %slip_ref.7) | copy-start | bytes 6291460
  56.3 12.0 %copy-start.5 = (bf16[3,2048,256]{2,1,0:T(8,128)(2,1)S(1)}, bf16[3,2048,256]{2,1,0:T(8,128)(2,1)}, u32[]{:S(2)}) copy-start(bf16[3,2048,256]{2,1,0:T(8,128)(2,1)} %near_ref.3) | copy-start | bytes 9437188
  68.3 5.9 %copy-start.7 = (bf16[32,2048]{1,0:T(8,128)(2,1)S(1)}, bf16[32,2048]{1,0:T(8,128)(2,1)}, u32[]{:S(2)}) copy-start(bf16[32,2048]{1,0:T(8,128)(2,1)} %basis_out_ref.3) | copy-start | bytes 393220
  68.3 5.9 %copy-start.9 = (bf16[32,2048]{1,0:T(8,128)(2,1)S(1)}, bf16[32,2048]{1,0:T(8,128)(2,1)}, u32[]{:S(2)}) copy-start(bf16[32,2048]{1,0:T(8,128)(2,1)} %basis_in_ref.1) | copy-start | bytes 393220
  74.2 17.2 %copy-start.2 = (bf16[4,2048,256]{2,1,0:T(8,128)(2,1)S(1)}, bf16[4,2048,256]{2,1,0:T(8,128)(2,1)}, u32[]{:S(2)}) copy-start(bf16[4,2048,256]{2,1,0:T(8,128)(2,1)} %fusion.matrix_ref) | copy-start | bytes 12582916
  77.3 8.4 %collective-permute-start.13 = (bf16[256,256]{1,0:T(8,128)(2,1)S(1)}, bf16[256,256]{1,0:T(8,128)(2,1)S(1)}, u32[]{:S(2)}, u32[]{:S(2)}) collective-permute-start(bf16[256,256]{1,0:T(8,128)(2,1)S(1)} %get-tuple-element.76.refs_0_), channel_id=1, source_target_pairs={{0,8},{8,16},{16,24},{24,0},{1,9},{9,17},{17,25},{25,1},{2,10},{10... | collective-permute-start | bytes 393224 | tf_op jit(solution)/shard_map/ppermute | solution.py:311
  79.3 6.4 %collective-permute-start.14 = (bf16[256,256]{1,0:T(8,128)(2,1)S(1)}, bf16[256,256]{1,0:T(8,128)(2,1)S(1)}, u32[]{:S(2)}, u32[]{:S(2)}) collective-permute-start(bf16[256,256]{1,0:T(8,128)(2,1)S(1)} %get-tuple-element.76.refs_0_), channel_id=1, source_target_pairs={{0,16},{8,24},{16,0},{24,8},{1,17},{9,25},{17,1},{25,9},{2,18},{10... | collective-permute-start | bytes 393224 | tf_op jit(solution)/shard_map/ppermute | solution.py:311
  79.3 6.4 %collective-permute-start.15 = (bf16[256,256]{1,0:T(8,128)(2,1)S(1)}, bf16[256,256]{1,0:T(8,128)(2,1)S(1)}, u32[]{:S(2)}, u32[]{:S(2)}) collective-permute-start(bf16[256,256]{1,0:T(8,128)(2,1)S(1)} %get-tuple-element.76.refs_0_), channel_id=1, source_target_pairs={{0,24},{8,0},{16,8},{24,16},{1,25},{9,1},{17,9},{25,17},{2,26},{10... | collective-permute-start | bytes 393224 | tf_op jit(solution)/shard_map/ppermute | solution.py:311
  79.7 6.0 %collective-permute-start.16 = (bf16[256,256]{1,0:T(8,128)(2,1)S(1)}, bf16[256,256]{1,0:T(8,128)(2,1)S(1)}, u32[]{:S(2)}, u32[]{:S(2)}) collective-permute-start(bf16[256,256]{1,0:T(8,128)(2,1)S(1)} %get-tuple-element.69), channel_id=1, source_target_pairs={{0,1},{1,2},{2,3},{3,4},{4,5},{5,6},{6,7},{7,8},{8,9},{9,10},{10,1... | collective-permute-start | bytes 393224 | tf_op jit(solution)/shard_map/ppermute | solution.py:323
  83.7 7.7 %collective-permute-start.17 = (bf16[256,256]{1,0:T(8,128)(2,1)S(1)}, bf16[256,256]{1,0:T(8,128)(2,1)S(1)}, u32[]{:S(2)}, u32[]{:S(2)}) collective-permute-start(bf16[256,256]{1,0:T(8,128)(2,1)S(1)} %get-tuple-element.70), channel_id=1, source_target_pairs={{1,0},{2,1},{3,2},{4,3},{5,4},{6,5},{7,6},{8,7},{9,8},{10,9},{11,1... | collective-permute-start | bytes 393224 | tf_op jit(solution)/shard_map/ppermute | solution.py:323
  93.2 2.0 %collective-permute-start.18 = (bf16[1024,256]{1,0:T(8,128)(2,1)S(1)}, bf16[1024,256]{1,0:T(8,128)(2,1)S(1)}, u32[]{:S(2)}, u32[]{:S(2)}) collective-permute-start(bf16[1024,256]{1,0:T(8,128)(2,1)S(1)} %shard_map.195), channel_id=1, source_target_pairs={{0,1},{1,0},{2,3},{3,2},{4,5},{5,4},{6,7},{7,6},{8,9},{9,8},{10,11... | collective-permute-start | bytes 1572872 | tf_op jit(solution)/shard_map/ppermute | solution.py:318
  95.4 10.5 %collective-permute-start.19 = (bf16[256,256]{1,0:T(8,128)(2,1)S(1)}, bf16[256,256]{1,0:T(8,128)(2,1)S(1)}, u32[]{:S(2)}, u32[]{:S(2)}) collective-permute-start(bf16[256,256]{1,0:T(8,128)(2,1)S(1)} %get-tuple-element.81), channel_id=1, source_target_pairs={{0,2},{1,3},{2,4},{3,5},{4,6},{5,7},{6,0},{7,1},{8,10},{9,11},{10,... | collective-permute-start | bytes 393224 | tf_op jit(solution)/shard_map/ppermute | solution.py:315
  95.5 14.5 %collective-permute-start.20 = (bf16[256,256]{1,0:T(8,128)(2,1)S(1)}, bf16[256,256]{1,0:T(8,128)(2,1)S(1)}, u32[]{:S(2)}, u32[]{:S(2)}) collective-permute-start(bf16[256,256]{1,0:T(8,128)(2,1)S(1)} %get-tuple-element.82), channel_id=1, source_target_pairs={{0,4},{1,5},{2,6},{3,7},{4,0},{5,1},{6,2},{7,3},{8,12},{9,13},{10,... | collective-permute-start | bytes 393224 | tf_op jit(solution)/shard_map/ppermute | solution.py:315
  101.8 12.3 %collective-permute-start.21 = (bf16[256,256]{1,0:T(8,128)(2,1)S(1)}, bf16[256,256]{1,0:T(8,128)(2,1)S(1)}, u32[]{:S(2)}, u32[]{:S(2)}) collective-permute-start(bf16[256,256]{1,0:T(8,128)(2,1)S(1)} %get-tuple-element.83), channel_id=1, source_target_pairs={{0,6},{1,7},{2,0},{3,1},{4,2},{5,3},{6,4},{7,5},{8,14},{9,15},{10,... | collective-permute-start | bytes 393224 | tf_op jit(solution)/shard_map/ppermute | solution.py:315

commit v2 on v1

--- a/solution.py
+++ b/solution.py
@@ -43,87 +43,152 @@
     return pl.ds(pl.multiple_of(n * size, size), size)
 
 
-def project_kernel(slip_ref, basis_ref, coeff_ref, rounded_ref, first_ref, last_ref):
+HBM = pl.BlockSpec(memory_space=pl.ANY)
+
+
+def in_hbm(*arrays):
+    return [pltpu.with_memory_space_constraint(array, pltpu.HBM) for array in arrays]
+
+
+def start_copies(pairs, sems, first=0):
+    copies = [pltpu.make_async_copy(a, b, sems.at[first + k]) for k, (a, b) in enumerate(pairs)]
+    for copy in copies:
+        copy.start()
+    return copies
+
+
+def project_kernel(slip_hbm, basis_hbm, coeff_ref, rounded_ref, first_ref, last_ref, slip_ref, basis_ref, sems):
     count = slip_ref.shape[0] // BS
-
-    @pl.loop(0, count)
-    def _(n):
-        at = rows_at(n, BS)
+    blocks = [pl.ds(n * BS, BS) for n in range(count)]
+    copies = start_copies(
+        [(basis_hbm, basis_ref)] + [(slip_hbm.at[at, :], slip_ref.at[at, :]) for at in blocks], sems
+    )
+    copies[0].wait()
+    for n, at in enumerate(blocks):
+        copies[1 + n].wait()
         rounded = slip_ref[at, :].astype(BF16)
         rounded_ref[at, :] = rounded
-        coeff_ref[rows_at(n, R), :] = dot(basis_ref[:, at], rounded).astype(BF16)
-
-    first_ref[...] = rounded_ref[:BS]
-    last_ref[...] = rounded_ref[-BS:]
+        if n == 0:
+            first_ref[...] = rounded
+        if n == count - 1:
+            last_ref[...] = rounded
+        coeff_ref[n * R : (n + 1) * R, :] = dot(basis_ref[:, at], rounded).astype(BF16)
 
 
 def project(slip, basis_in):
     patches, ens = slip.shape
+    count = patches // BS
     edge = jax.ShapeDtypeStruct((BS, ens), BF16)
     return call(
         project_kernel,
         [
-            jax.ShapeDtypeStruct((patches // BS * R, ens), BF16),
+            jax.ShapeDtypeStruct((count * R, ens), BF16),
             jax.ShapeDtypeStruct((patches, ens), BF16),
             edge,
             edge,
+            jax.ShapeDtypeStruct((patches, ens), F32),
         ],
-        slip,
-        basis_in,
-    )
-
-
-def setup_kernel(
-    load_ref, normal_ref, direct_ref, evolution_ref, distance_ref, stiffness_ref, bricks_ref, count_ref, weight_ref,
-    now_ref, rate_ref, coeff_ref, numbers_ref, ids_ref, shares_ref, joined_ref,
+        *in_hbm(slip, basis_in),
+        specs=[HBM] * 2,
+        scratch_shapes=[pltpu.VMEM(basis_in.shape, BF16), pltpu.SemaphoreType.DMA((1 + count,))],
+    )
+
+
+def ranks_kernel(
+    col_count, where_ref, rank_hbm, now_hbm, rate_hbm, coeff_ref, wide_ref, joined_ref, rank_ref, sems
+):
+    sources, share, blocks = rank_ref.shape
+    ens = now_hbm.shape[1]
+    copies = start_copies(
+        [
+            (rank_hbm, rank_ref),
+            (now_hbm, joined_ref.at[:, pl.ds(0, ens)]),
+            (rate_hbm, joined_ref.at[:, pl.ds(ens, ens)]),
+        ],
+        sems,
+    )
+    width = share * R
+    column = lax.broadcasted_iota(jnp.int32, (share, width), 1)
+    spread = (lax.div(column, R) == lax.broadcasted_iota(jnp.int32, (share, width), 0)).astype(F32).astype(BF16)
+    level = lax.rem(lax.broadcasted_iota(jnp.int32, (blocks, width), 1), R).astype(F32)
+    receiver = where_ref[0] * blocks + lax.broadcasted_iota(jnp.int32, (share, blocks), 1)
+    copies[0].wait()
+    for source in range(sources):
+        own = (source * col_count + where_ref[1]) * share + lax.broadcasted_iota(jnp.int32, (share, blocks), 0)
+        rank = jnp.where(jnp.abs(receiver - own) > 1, rank_ref[source], 0).astype(F32)
+        wide = dot_t(rank.astype(BF16), spread)
+        wide_ref[source] = jnp.where(level < wide, wide, 0.0)
+    copies[1].wait()
+    copies[2].wait()
+
+
+def side_by_side_kernel(*refs):
+    pieces, out_ref = refs[:-1], refs[-1]
+    size = pieces[0].shape[0]
+    for k, piece in enumerate(pieces):
+        out_ref[k * size : (k + 1) * size, :] = piece[...]
+
+
+def weights_kernel(
+    heights, size, where_ref, load_hbm, normal_hbm, direct_hbm, evolution_hbm, distance_hbm, stiffness_hbm,
+    count_hbm, bricks_hbm, weight_hbm, near_hbm, state_hbm, after_ref, numbers_ref, matrix_ref, near_ref, state_ref,
+    vectors, count_ref, bricks_ref, weight_ref, id_wide, share_wide, sems,
 ):
     slots, patches = bricks_ref.shape
-    ens = now_ref.shape[1]
-    joined_ref[:, :ens] = now_ref[...]
-    joined_ref[:, ens:] = rate_ref[...]
+    sources = [load_hbm, normal_hbm, direct_hbm, evolution_hbm, distance_hbm, stiffness_hbm]
+    small = [(source, vectors.at[k]) for k, source in enumerate(sources)]
+    small = small + [(count_hbm, count_ref), (bricks_hbm, bricks_ref), (weight_hbm, weight_ref)]
+    copies = start_copies(small, sems)
+    large = start_copies([(near_hbm, near_ref), (state_hbm, state_ref)], sems, len(small))
+    height, core = where_ref[0].astype(F32), where_ref[1].astype(F32)
+    lanes = 128
+    column = lax.div(lax.broadcasted_iota(jnp.int32, (slots, slots * lanes), 1), lanes)
+    spread = (column == lax.broadcasted_iota(jnp.int32, (slots, slots * lanes), 0)).astype(F32).astype(BF16)
+    spread_both = jnp.concatenate([spread, spread], axis=0)
+    for copy in copies:
+        copy.wait()
 
     @pl.loop(0, patches // BS)
     def _(n):
         at = rows_at(n, BS)
-        evolution = evolution_ref[:, at]
-        rows = [
-            load_ref[:, at],
-            normal_ref[:, at],
-            1.0 / direct_ref[:, at],
-            1.0 / evolution,
-            evolution / distance_ref[:, at],
-            stiffness_ref[:, at],
-        ]
-        rows = rows + rows[:2]
+        load, normal, direct, evolution, distance, stiffness = (vectors[k, :, at] for k in range(6))
+        rows = [load, normal, 1.0 / direct, 1.0 / evolution, evolution / distance, stiffness, load, normal]
         numbers_ref[at, :] = jnp.concatenate(rows, axis=0).T
-        bricks = bricks_ref[:, at]
-        slot = lax.broadcasted_iota(jnp.int32, (slots, BS), 0)
-        weights = jnp.where(slot < count_ref[:, at], weight_ref[:, at], 0.0)
+        bricks = bricks_ref[:, at].astype(F32)
+        live = lax.broadcasted_iota(jnp.int32, (slots, BS), 0) < count_ref[:, at]
+        weights = jnp.where(live, weight_ref[:, at], 0.0)
         merged = jnp.zeros((slots, BS), F32)
         for k in range(slots):
             merged = merged + jnp.where(bricks == bricks[k : k + 1], weights[k : k + 1], 0.0)
         shares = merged / jnp.sum(weights, axis=0, keepdims=True)
-        ids_ref[at, :] = bricks.T.astype(jnp.int32).astype(jnp.int16)
-        shares_ref[at, :] = shares.T.astype(BF16)
-
-
-def weights_kernel(ids_ref, shares_ref, matrix_ref):
-    patches, slots = ids_ref.shape
-    rows = 32
-
-    @pl.loop(0, patches // rows)
-    def _(n):
-        at = rows_at(n, rows)
-        ids, shares = ids_ref[at, :], shares_ref[at, :]
-        id_of = [jnp.broadcast_to(ids[:, k : k + 1], (rows, 128)) for k in range(slots)]
-        share_of = [jnp.broadcast_to(shares[:, k : k + 1], (rows, 128)) for k in range(slots)]
-        lane = lax.broadcasted_iota(jnp.int32, (rows, 128), 1).astype(jnp.int16)
-        for left in range(0, matrix_ref.shape[1], 128):
-            here = lane + jnp.int16(left)
-            tile = jnp.zeros((rows, 128), BF16)
-            for k in range(slots):
-                tile = jnp.where(id_of[k] == here, share_of[k], tile)
-            matrix_ref[at, left : left + 128] = tile
+        owner = jnp.floor((bricks + 0.5) * (1.0 / size))
+        chip = jnp.floor(owner * 0.5 + 0.25)
+        away = height - chip
+        away = jnp.where(away < 0, away + heights, away)
+        other = jnp.where(owner - 2.0 * chip == core, 0.0, float(heights))
+        place = jnp.where(live, (other + away - owner) * size + bricks, -1.0)
+        high = jnp.floor((place + 0.5) * (1.0 / lanes)) * lanes
+        place_both = jnp.concatenate([high, place - high], axis=0).astype(BF16)
+        id_wide[...] = dot_t(place_both, spread_both)
+        share_wide[...] = dot_t(shares.astype(BF16), spread)
+        group = 16
+
+        @pl.loop(0, BS // group, unroll=2)
+        def _(m):
+            part = rows_at(m, group)
+            to = pl.ds(pl.multiple_of(n * BS + m * group, group), group)
+            ids = [id_wide[part, k * lanes : (k + 1) * lanes] for k in range(slots)]
+            values = [share_wide[part, k * lanes : (k + 1) * lanes] for k in range(slots)]
+            lane = lax.broadcasted_iota(jnp.int32, (group, lanes), 1).astype(F32)
+            for left in range(0, matrix_ref.shape[1], lanes):
+                here = lane + float(left)
+                tile = jnp.zeros((group, lanes), F32)
+                for k in range(slots):
+                    tile = jnp.where(ids[k] == here, values[k], tile)
+                matrix_ref[to, left : left + lanes] = tile.astype(BF16)
+
+    for copy in large:
+        copy.wait()
 
 
 def couple_kernel(sources, heights, where_ref, matrix_ref, *refs):
@@ -257,25 +322,13 @@
     state_out_ref[...] = rest_ref[at, :] - (0.5 * STEP_SIZE * numbers_ref[at, 4:5]) * speed
 
 
-def masked_coupling(coupling, block_rank, row_index, col_index, row_count, col_count):
+def masked_coupling(coupling, wide):
     rows, sources, width = coupling.shape
-    share = width // R
     blocks = rows // R
-    receiver = row_index * blocks + jnp.arange(blocks, dtype=jnp.int32)
-    source = (
-        (jnp.arange(sources, dtype=jnp.int32)[:, None] * col_count + col_index) * share
-        + jnp.arange(share, dtype=jnp.int32)[None, :]
-    )
-    apart = jnp.abs(receiver[:, None, None] - source[None]) > 1
-    rank = jnp.where(apart, block_rank, 0)
-    rank = jnp.transpose(rank, (1, 0, 2))
-    rank_full = jnp.repeat(rank, R, axis=2).reshape(sources, blocks, 1, width)
-    level = jnp.maximum(
-        jnp.arange(R, dtype=jnp.int32)[:, None], jnp.arange(width, dtype=jnp.int32)[None, :] % R
-    )
-    keep = level[None, None] < rank_full
+    keep = jnp.arange(R, dtype=jnp.int32).astype(F32)[None, None, :, None] < wide[:, :, None, :]
     matrix = jnp.transpose(coupling, (1, 0, 2)).reshape(sources, blocks, R, width)
-    return jnp.where(keep, matrix, jnp.zeros((), BF16)).reshape(sources, rows, width)
+    masked = jnp.where(keep, matrix, jnp.zeros((), BF16)).reshape(sources, rows, width)
+    return pltpu.with_memory_space_constraint(masked, pltpu.VMEM)
 
 
 def per_device(
@@ -326,21 +379,17 @@
     slots = adj_bricks.shape[0]
     size = pressure_now.shape[0]
     share = coupling.shape[2]
-    owner, within = adj_bricks // size, adj_bricks % size
-    away = (height - owner // 2) % heights
-    other_core = (owner % 2 != core).astype(jnp.int32)
-    live = adj_count[None, :] > jnp.arange(slots, dtype=jnp.int32)[:, None]
-    bricks = jnp.where(live, (other_core * heights + away) * size + within, -1).astype(F32)
-    masked = masked_coupling(coupling, block_rank, row_index, col_index, row_count, col_count)
     source_rows = [(row_index - d) % row_count for d in range(row_count)]
     own_where = jnp.stack([height, core] + source_rows).astype(jnp.int32)
     pair_where = jnp.stack([height, 1 - core] + source_rows).astype(jnp.int32)
 
-    def far_parts(coeffs):
+    def far_parts(coeffs, first, last):
         sent = to_core(couple(pair_where, masked, coeffs, heights, BF16))
         kept = couple(own_where, masked, coeffs, heights, F32)
         pieces = chip_sum(kept, sent, heights)
-        return pieces[:1] + [to_height(pieces[d], d) for d in range(1, heights)]
+        pieces, first, last = lax.optimization_barrier((pieces, first, last))
+        parts = pieces[:1] + [to_height(pieces[d], d) for d in range(1, heights)]
+        return parts, *halo(first, last)
 
     def row_coeffs(coeff):
         return [coeff] + [to_row(coeff, d) for d in range(1, row_count)]
@@ -350,34 +399,55 @@
     edge = jax.ShapeDtypeStruct((BS, ens), BF16)
     per_patch = [tau_load, normal_stress, direct_effect, evolution_effect, slip_distance, self_stiffness]
 
-    coeff, rounded, first, last = project(slip, basis_in)
+    coeff, rounded, first, last, slip = project(slip, basis_in)
     coeffs = row_coeffs(coeff)
-    numbers, ids, shares, joined = call(
-        setup_kernel,
+    ranks = jnp.transpose(block_rank, (1, 2, 0))
+    place = jnp.stack([row_index, col_index]).astype(jnp.int32)
+    wide, joined = call(
+        functools.partial(ranks_kernel, col_count),
+        [
+            jax.ShapeDtypeStruct((ranks.shape[0], ranks.shape[2], share), F32),
+            jax.ShapeDtypeStruct((size, 2 * ens), BF16),
+        ],
+        place,
+        *in_hbm(ranks, pressure_now, pressure_rate),
+        coeff,
+        specs=[SMEM] + [HBM] * 3 + [VMEM],
+        scratch_shapes=[pltpu.VMEM(ranks.shape, jnp.int32), pltpu.SemaphoreType.DMA((3,))],
+    )
+    own = call(
+        side_by_side_kernel,
+        jax.ShapeDtypeStruct((heights * size, 2 * ens), BF16),
+        joined,
+        *[to_height(joined, d) for d in range(1, heights)],
+    )
+    other = to_core(own)
+    masked = masked_coupling(coupling, wide)
+    parts, before, after = far_parts(coeffs, first, last)
+    numbers, matrix, near, state = call(
+        functools.partial(weights_kernel, heights, size),
         [
             jax.ShapeDtypeStruct((patches, 8), F32),
-            jax.ShapeDtypeStruct((patches, slots), jnp.int16),
-            jax.ShapeDtypeStruct((patches, slots), BF16),
-            jax.ShapeDtypeStruct((size, 2 * ens), BF16),
+            jax.ShapeDtypeStruct((patches, 2 * heights * size), BF16),
+            jax.ShapeDtypeStruct(near_blocks.shape, BF16),
+            full,
         ],
-        *[array[None] for array in per_patch],
-        bricks,
-        adj_count[None],
-        adj_weight,
-        pressure_now,
-        pressure_rate,
-        coeff,
-    )
-    own = jnp.concatenate([joined] + [to_height(joined, d) for d in range(1, heights)], axis=0)
-    other = to_core(own)
-    first, last = halo(first, last)
-    coeffs, first, last = lax.optimization_barrier((coeffs, first, last))
-    parts = far_parts(coeffs)
-    matrix = call(
-        weights_kernel, jax.ShapeDtypeStruct((patches, 2 * heights * size), BF16), ids, shares
+        jnp.stack([height, core]).astype(jnp.int32),
+        *in_hbm(*[array[None] for array in per_patch], adj_count[None], adj_bricks, adj_weight, near_blocks, state),
+        parts[0],
+        specs=[SMEM] + [HBM] * 11 + [VMEM],
+        scratch_shapes=[
+            pltpu.VMEM((6, 1, patches), F32),
+            pltpu.VMEM((1, patches), jnp.int32),
+            pltpu.VMEM(adj_bricks.shape, jnp.int32),
+            pltpu.VMEM(adj_weight.shape, F32),
+            pltpu.VMEM((BS, slots * 128), F32),
+            pltpu.VMEM((BS, slots * 128), F32),
+            pltpu.SemaphoreType.DMA((11,)),
+        ],
     )
     shift, scale, rest, scale_mid = call(
-        prepare_first_kernel, [full] * 4, matrix, own, other, slip, state, numbers, near_blocks, rounded, first, last
+        prepare_first_kernel, [full] * 4, matrix, own, other, slip, state, numbers, near, rounded, before, after
     )
     slip_mid, state_mid, rounded, coeff, first, last = call(
         functools.partial(finish_first_kernel, heights),
@@ -385,12 +455,10 @@
         shift, scale, rest, slip, numbers, basis_out, basis_in, *parts,
     )
     coeffs = row_coeffs(coeff)
-    first, last = halo(first, last)
-    coeffs, first, last = lax.optimization_barrier((coeffs, first, last))
-    parts = far_parts(coeffs)
+    parts, before, after = far_parts(coeffs, first, last)
     shift, slip_rest, rest = call(
         prepare_second_kernel, [full] * 3,
-        slip, state, slip_mid, state_mid, scale_mid, numbers, near_blocks, rounded, first, last,
+        slip, state, slip_mid, state_mid, scale_mid, numbers, near, rounded, before, after,
     )
     slip_out, state_out = call(
         functools.partial(finish_second_kernel, heights),

time: 120 us -> 104 us (0.87)
  the two profiles are of different devices: /device:TPU:11 before, /device:TPU:0 now
where the time goes in v2:
time: 104 us
  Pallas kernels  40.8 us (39%)
  starting transfers between devices  36.5 us (35%)
  waiting for transfers between devices  13.1 us (13%)
  local copies, waits for them, and re-layouts  7.84 us (8%)
  other arithmetic  4.62 us (4%)
    pallas_call x14, Pallas kernels, call(): pl.pallas_call(kernel, in_specs=specs or [VMEM] * len(operands), out_shap...  40.8 us
    ppermute x9, starting transfers between devices, to_height(): return lax.ppermute(array, 'col', pairs)  18.7 us
    ppermute x6, starting transfers between devices, to_row(): lax.ppermute(array, 'row', [(i, (i + d) % row_count) for i in range(row_c...  10.3 us
    unnamed x26, local copies, waits for them, and re-layouts  7.59 us
    ppermute x4, starting transfers between devices, halo(): return (lax.ppermute(last, both, up), lax.ppermute(first, both, down))  7.18 us
    ppermute x9, waiting for transfers between devices, to_height(): return lax.ppermute(array, 'col', pairs)  7.1 us
    ppermute x6, waiting for transfers between devices, to_row(): lax.ppermute(array, 'row', [(i, (i + d) % row_count) for i in range(row_c...  5.87 us
    select_n x1, other arithmetic, masked_coupling(): jnp.where(keep, matrix, jnp.zeros((), BF16)).reshape(sources, rows, width)  4.47 us
  transfers between devices with their start and end apart: 22, of which 7 were waited for; matrix products, arithmetic and copies ran while one was open for 5% of the time, Pallas kernels for 28%

profile of v2, /device:TPU:0, one launch (start us, length us, event | category | flops | bytes accessed | tf_op | source)
XLA Modules:
  0.0 103.8 jit_solution(279582108729718992)
XLA Ops:
  0.6 2.4 %shard_map.185 = (bf16[256,256]{1,0:T(8,128)(2,1)S(1)}, bf16[2048,256]{1,0:T(8,128)(2,1)S(1)}, bf16[256,256]{1,0:T(8,128)(2,1)S(1)}, bf16[256,256]{1,0:T(8,128)(2,1)S(1)}, f32[2048,256]{1,0:T(8,128)S(1)}) custom-call(f32[2048,256]{1,0:T(8,128)} %slip_hbm.1, bf16[32,2048]{1,0:T(8,128)(2,1)} %basis_in_ref.1), custom_call_target="tpu_custom_call" | custom-call | tf_op jit(solution)/shard_map/pallas_call | solution.py:33
  3.0 1.0 copy-done.3
  4.0 0.6 copy-done.9
  4.6 0.7 copy-done.11
  5.3 3.9 %collective-permute-start.2 = (bf16[256,256]{1,0:T(8,128)(2,1)S(1)}, bf16[256,256]{1,0:T(8,128)(2,1)S(1)}, u32[]{:S(2)}, u32[]{:S(2)}) collective-permute-start(bf16[256,256]{1,0:T(8,128)(2,1)S(1)} %get-tuple-element.47.coeff_ref.refs_0_), channel_id=1, source_target_pairs={{0,24},{8,0},{16,8},{24,16},{1,25},{9,1},{17,9},{25,17},{2,26},{10... | collective-permute-start | bytes 393224 | tf_op jit(solution)/shard_map/ppermute | solution.py:364
  9.2 0.5 collective-permute-start.1
  9.7 0.6 collective-permute-start
  10.3 0.1 pad_add_fusion.1.where_ref
  10.4 1.5 %shard_map.186 = (f32[4,64,256]{2,1,0:T(8,128)S(1)}, bf16[128,512]{1,0:T(8,128)(2,1)S(1)}) custom-call(s32[2]{0:T(128)S(1)} %pad_add_fusion.1.where_ref, s32[4,8,64]{2,1,0:T(8,128)} %bitcast.23, bf16[128,256]{1,0:T(8,128)(2,1)} %now_hbm.1, bf16[128,256]{1,0:T(8,128)(2,1)} %rate_hbm.1, bf16[256,256]{1,0:T(8,128)(2,1)S(1)} %get-tuple-element.47.coeff_ref.refs_0_), custom_call_target="tpu_custom_call" | custom-call | tf_op jit(solution)/shard_map/pallas_call | solution.py:33
  11.9 3.7 %collective-permute-start.6 = (bf16[128,512]{1,0:T(8,128)(2,1)S(1)}, bf16[128,512]{1,0:T(8,128)(2,1)S(1)}, u32[]{:S(2)}, u32[]{:S(2)}) collective-permute-start(bf16[128,512]{1,0:T(8,128)(2,1)S(1)} %get-tuple-element.58.refs_0_), channel_id=1, source_target_pairs={{0,6},{1,7},{2,0},{3,1},{4,2},{5,3},{6,4},{7,5},{8,14},{9,15},{10,... | collective-permute-start | bytes 393224 | tf_op jit(solution)/shard_map/ppermute | solution.py:368
  15.5 1.0 collective-permute-start.4
  16.6 4.5 %fusion.matrix_ref = bf16[4,2048,256]{2,1,0:T(8,128)(2,1)} fusion(bf16[2048,4,256]{2,1,0:T(4,128)(2,1)} %param.29, f32[4,64,256]{2,1,0:T(8,128)S(1)} %get-tuple-element.48, f32[2048]{0:T(1024)S(1)} %lt.48), kind=kLoop, calls=%fused_computation.1 | loop fusion | flops 4194304 | bytes 8658944 | tf_op jit(solution)/shard_map/jit(_where)/select_n | solution.py:330
  21.1 0.1 stack.58.where_ref
  21.2 2.2 %copy-done = bf16[4,2048,256]{2,1,0:T(8,128)(2,1)S(1)} copy-done((bf16[4,2048,256]{2,1,0:T(8,128)(2,1)S(1)}, bf16[4,2048,256]{2,1,0:T(8,128)(2,1)}, u32[]{:S(2)}) %copy-start) | copy-done | bytes 4194328
  23.4 2.6 %shard_map.188 = bf16[1024,256]{1,0:T(8,128)(2,1)} custom-call(s32[6]{0:T(128)S(1)} %stack.58.where_ref, bf16[4,2048,256]{2,1,0:T(8,128)(2,1)S(1)} %copy-done, bf16[256,256]{1,0:T(8,128)(2,1)S(1)} %get-tuple-element.47.coeff_ref.refs_0_, bf16[256,256]{1,0:T(8,128)(2,1)S(1)} %collective-permute-done.refs_1_, ...), custom_call_target="tpu_custom_call" | custom-call | tf_op jit(solution)/shard_map/pallas_call | solution.py:33
  26.0 0.4 collective-permute-done.5.refs_2_
  26.4 0.2 collective-permute-start.7
  26.6 0.1 stack.53.where_ref
  26.7 2.2 %copy-done.1 = bf16[4,2048,256]{2,1,0:T(8,128)(2,1)S(1)} copy-done((bf16[4,2048,256]{2,1,0:T(8,128)(2,1)S(1)}, bf16[4,2048,256]{2,1,0:T(8,128)(2,1)}, u32[]{:S(2)}) %copy-start.1) | copy-done | bytes 4194328
  28.9 0.9 copy-done.8
  29.8 1.8 %shard_map.187.kept_ref = f32[1024,256]{1,0:T(8,128)S(1)} custom-call(s32[6]{0:T(128)S(1)} %stack.53.where_ref, bf16[4,2048,256]{2,1,0:T(8,128)(2,1)S(1)} %copy-done.1, bf16[256,256]{1,0:T(8,128)(2,1)S(1)} %get-tuple-element.47.coeff_ref.refs_0_, bf16[256,256]{1,0:T(8,128)(2,1)S(1)} %copy-done.8, bf16[256,256]{1,0:T(8,128)(2,1)S(1)} %collective-permute-done.1.refs_2_, ...), custom_call_target="tpu_custom_call" | custom-call | tf_op jit(solution)/shard_map/pallas_call | solution.py:33
  31.6 1.3 %shard_map.189 = (bf16[256,256]{1,0:T(8,128)(2,1)S(1)}, bf16[256,256]{1,0:T(8,128)(2,1)S(1)}, bf16[256,256]{1,0:T(8,128)(2,1)S(1)}, bf16[256,256]{1,0:T(8,128)(2,1)S(1)}) custom-call(f32[1024,256]{1,0:T(8,128)S(1)} %shard_map.187.kept_ref, bf16[1024,256]{1,0:T(8,128)(2,1)} %collective-permute-done.3.sent_ref), custom_call_target="tpu_custom_call" | custom-call | tf_op jit(solution)/shard_map/pallas_call | solution.py:33
  32.9 2.3 %collective-permute-start.8 = (bf16[256,256]{1,0:T(8,128)(2,1)S(1)}, bf16[256,256]{1,0:T(8,128)(2,1)S(1)}, u32[]{:S(2)}, u32[]{:S(2)}) collective-permute-start(bf16[256,256]{1,0:T(8,128)(2,1)S(1)} %copy-done.12), channel_id=1, source_target_pairs={{0,1},{1,2},{2,3},{3,4},{4,5},{5,6},{6,7},{7,8},{8,9},{9,10},{10,1... | collective-permute-start | bytes 393224 | tf_op jit(solution)/shard_map/ppermute | solution.py:376
  35.2 1.3 %collective-permute-start.9 = (bf16[256,256]{1,0:T(8,128)(2,1)S(1)}, bf16[256,256]{1,0:T(8,128)(2,1)S(1)}, u32[]{:S(2)}, u32[]{:S(2)}) collective-permute-start(bf16[256,256]{1,0:T(8,128)(2,1)S(1)} %copy-done.10), channel_id=1, source_target_pairs={{1,0},{2,1},{3,2},{4,3},{5,4},{6,5},{7,6},{8,7},{9,8},{10,9},{11,1... | collective-permute-start | bytes 393224 | tf_op jit(solution)/shard_map/ppermute | solution.py:376
  36.5 4.5 %collective-permute-start.10 = (bf16[256,256]{1,0:T(8,128)(2,1)S(1)}, bf16[256,256]{1,0:T(8,128)(2,1)S(1)}, u32[]{:S(2)}, u32[]{:S(2)}) collective-permute-start(bf16[256,256]{1,0:T(8,128)(2,1)S(1)} %get-tuple-element.67), channel_id=1, source_target_pairs={{0,2},{1,3},{2,4},{3,5},{4,6},{5,7},{6,0},{7,1},{8,10},{9,11},{10,... | collective-permute-start | bytes 393224 | tf_op jit(solution)/shard_map/ppermute | solution.py:368
  41.0 0.9 collective-permute-start.11
  41.9 1.7 %collective-permute-start.12 = (bf16[256,256]{1,0:T(8,128)(2,1)S(1)}, bf16[256,256]{1,0:T(8,128)(2,1)S(1)}, u32[]{:S(2)}, u32[]{:S(2)}) collective-permute-start(bf16[256,256]{1,0:T(8,128)(2,1)S(1)} %get-tuple-element.69), channel_id=1, source_target_pairs={{0,6},{1,7},{2,0},{3,1},{4,2},{5,3},{6,4},{7,5},{8,14},{9,15},{10,... | collective-permute-start | bytes 393224 | tf_op jit(solution)/shard_map/ppermute | solution.py:368
  43.6 12.6 %shard_map.190 = (f32[2048,8]{1,0:T(8,128)S(1)}, bf16[2048,1024]{1,0:T(8,128)(2,1)S(1)}, bf16[3,2048,256]{2,1,0:T(8,128)(2,1)S(1)}, f32[2048,256]{1,0:T(8,128)S(1)}) custom-call(s32[2]{0:T(128)S(1)} %pad_add_fusion.where_ref, f32[1,2048]{1,0:T(1,128)} %bitcast.24, f32[1,2048]{1,0:T(1,128)} %bitcast.25, f32[1,2048]{1,0:T(1,128)} %bitcast.26, ...), custom_call_target="tpu_custom_call" | custom-call | tf_op jit(solution)/shard_map/pallas_call | solution.py:33
  56.3 4.6 %shard_map.192 = (f32[2048,256]{1,0:T(8,128)S(1)}, f32[2048,256]{1,0:T(8,128)S(1)}, f32[2048,256]{1,0:T(8,128)S(1)}, f32[2048,256]{1,0:T(8,128)S(1)}) custom-call(bf16[2048,1024]{1,0:T(8,128)(2,1)S(1)} %get-tuple-element.57.matrix_ref, bf16[512,512]{1,0:T(8,128)(2,1)S(1)} %shard_map.191.own_ref, bf16[512,512]{1,0:T(8,128)(2,1)S(1)} %collective-permute-done.7.other_ref, ...), custom_call_target="tpu_custom_call" | custom-call | tf_op jit(solution)/shard_map/pallas_call | solution.py:33
  61.0 3.1 %shard_map.193 = (f32[2048,256]{1,0:T(8,128)S(1)}, f32[2048,256]{1,0:T(8,128)S(1)}, bf16[2048,256]{1,0:T(8,128)(2,1)S(1)}, bf16[256,256]{1,0:T(8,128)(2,1)S(1)},...) custom-call(f32[2048,256]{1,0:T(8,128)S(1)} %get-tuple-element.64.shift_ref, ...), custom_call_target="tpu_custom_call" | custom-call | tf_op jit(solution)/shard_map/pallas_call | solution.py:33
  64.1 3.8 %collective-permute-start.15 = (bf16[256,256]{1,0:T(8,128)(2,1)S(1)}, bf16[256,256]{1,0:T(8,128)(2,1)S(1)}, u32[]{:S(2)}, u32[]{:S(2)}) collective-permute-start(bf16[256,256]{1,0:T(8,128)(2,1)S(1)} %get-tuple-element.74.refs_0_), channel_id=1, source_target_pairs={{0,24},{8,0},{16,8},{24,16},{1,25},{9,1},{17,9},{25,17},{2,26},{10... | collective-permute-start | bytes 393224 | tf_op jit(solution)/shard_map/ppermute | solution.py:364
  67.9 1.5 %collective-permute-start.14 = (bf16[256,256]{1,0:T(8,128)(2,1)S(1)}, bf16[256,256]{1,0:T(8,128)(2,1)S(1)}, u32[]{:S(2)}, u32[]{:S(2)}) collective-permute-start(bf16[256,256]{1,0:T(8,128)(2,1)S(1)} %get-tuple-element.74.refs_0_), channel_id=1, source_target_pairs={{0,16},{8,24},{16,0},{24,8},{1,17},{9,25},{17,1},{25,9},{2,18},{10... | collective-permute-start | bytes 393224 | tf_op jit(solution)/shard_map/ppermute | solution.py:364
  69.4 2.4 %collective-permute-done.15.refs_3_ = bf16[256,256]{1,0:T(8,128)(2,1)S(1)} collective-permute-done((bf16[256,256]{1,0:T(8,128)(2,1)S(1)}, bf16[256,256]{1,0:T(8,128)(2,1)S(1)}, u32[]{:S(2)}, u32[]{:S(2)}) %collective-permute-start.15) | collective-permute-done | bytes 131104 | tf_op jit(solution)/shard_map/ppermute | solution.py:364
  71.8 1.5 %collective-permute-done.14.refs_2_ = bf16[256,256]{1,0:T(8,128)(2,1)S(1)} collective-permute-done((bf16[256,256]{1,0:T(8,128)(2,1)S(1)}, bf16[256,256]{1,0:T(8,128)(2,1)S(1)}, u32[]{:S(2)}, u32[]{:S(2)}) %collective-permute-start.14) | collective-permute-done | bytes 131104 | tf_op jit(solution)/shard_map/ppermute | solution.py:364
  73.3 2.0 %collective-permute-done.13.refs_1_ = bf16[256,256]{1,0:T(8,128)(2,1)S(1)} collective-permute-done((bf16[256,256]{1,0:T(8,128)(2,1)S(1)}, bf16[256,256]{1,0:T(8,128)(2,1)S(1)}, u32[]{:S(2)}, u32[]{:S(2)}) %collective-permute-start.13) | collective-permute-done | bytes 131104 | tf_op jit(solution)/shard_map/ppermute | solution.py:364
  75.3 1.8 %shard_map.195 = bf16[1024,256]{1,0:T(8,128)(2,1)S(1)} custom-call(s32[6]{0:T(128)S(1)} %stack.58.where_ref, bf16[4,2048,256]{2,1,0:T(8,128)(2,1)S(1)} %copy-done.2, bf16[256,256]{1,0:T(8,128)(2,1)S(1)} %get-tuple-element.74.refs_0_, bf16[256,256]{1,0:T(8,128)(2,1)S(1)} %collective-permute-done.13.refs_1_, ...), custom_call_target="tpu_custom_call" | custom-call | tf_op jit(solution)/shard_map/pallas_call | solution.py:33
  77.1 1.8 %shard_map.194.kept_ref = f32[1024,256]{1,0:T(8,128)S(1)} custom-call(s32[6]{0:T(128)S(1)} %stack.53.where_ref, bf16[4,2048,256]{2,1,0:T(8,128)(2,1)S(1)} %copy-done.2, bf16[256,256]{1,0:T(8,128)(2,1)S(1)} %get-tuple-element.74.refs_0_, bf16[256,256]{1,0:T(8,128)(2,1)S(1)} %collective-permute-done.13.refs_1_, ...), custom_call_target="tpu_custom_call" | custom-call | tf_op jit(solution)/shard_map/pallas_call | solution.py:33
  78.9 0.1 collective-permute-done.16.sent_ref
  79.0 0.3 shard_map.196
  79.3 2.3 %collective-permute-start.17 = (bf16[256,256]{1,0:T(8,128)(2,1)S(1)}, bf16[256,256]{1,0:T(8,128)(2,1)S(1)}, u32[]{:S(2)}, u32[]{:S(2)}) collective-permute-start(bf16[256,256]{1,0:T(8,128)(2,1)S(1)} %get-tuple-element.81), channel_id=1, source_target_pairs={{0,1},{1,2},{2,3},{3,4},{4,5},{5,6},{6,7},{7,8},{8,9},{9,10},{10,1... | collective-permute-start | bytes 393224 | tf_op jit(solution)/shard_map/ppermute | solution.py:376
  81.6 1.3 %collective-permute-start.18 = (bf16[256,256]{1,0:T(8,128)(2,1)S(1)}, bf16[256,256]{1,0:T(8,128)(2,1)S(1)}, u32[]{:S(2)}, u32[]{:S(2)}) collective-permute-start(bf16[256,256]{1,0:T(8,128)(2,1)S(1)} %get-tuple-element.82), channel_id=1, source_target_pairs={{1,0},{2,1},{3,2},{4,3},{5,4},{6,5},{7,6},{8,7},{9,8},{10,9},{11,1... | collective-permute-start | bytes 393224 | tf_op jit(solution)/shard_map/ppermute | solution.py:376
  82.9 2.6 %collective-permute-start.19 = (bf16[256,256]{1,0:T(8,128)(2,1)S(1)}, bf16[256,256]{1,0:T(8,128)(2,1)S(1)}, u32[]{:S(2)}, u32[]{:S(2)}) collective-permute-start(bf16[256,256]{1,0:T(8,128)(2,1)S(1)} %get-tuple-element.87), channel_id=1, source_target_pairs={{0,2},{1,3},{2,4},{3,5},{4,6},{5,7},{6,0},{7,1},{8,10},{9,11},{10,... | collective-permute-start | bytes 393224 | tf_op jit(solution)/shard_map/ppermute | solution.py:368
  85.5 1.7 %collective-permute-start.20 = (bf16[256,256]{1,0:T(8,128)(2,1)S(1)}, bf16[256,256]{1,0:T(8,128)(2,1)S(1)}, u32[]{:S(2)}, u32[]{:S(2)}) collective-permute-start(bf16[256,256]{1,0:T(8,128)(2,1)S(1)} %get-tuple-element.88), channel_id=1, source_target_pairs={{0,4},{1,5},{2,6},{3,7},{4,0},{5,1},{6,2},{7,3},{8,12},{9,13},{10,... | collective-permute-start | bytes 393224 | tf_op jit(solution)/shard_map/ppermute | solution.py:368
  87.3 2.6 %collective-permute-start.21 = (bf16[256,256]{1,0:T(8,128)(2,1)S(1)}, bf16[256,256]{1,0:T(8,128)(2,1)S(1)}, u32[]{:S(2)}, u32[]{:S(2)}) collective-permute-start(bf16[256,256]{1,0:T(8,128)(2,1)S(1)} %get-tuple-element.89), channel_id=1, source_target_pairs={{0,6},{1,7},{2,0},{3,1},{4,2},{5,3},{6,4},{7,5},{8,14},{9,15},{10,... | collective-permute-start | bytes 393224 | tf_op jit(solution)/shard_map/ppermute | solution.py:368
  89.9 2.7 %shard_map.197 = (f32[2048,256]{1,0:T(8,128)S(1)}, f32[2048,256]{1,0:T(8,128)S(1)}, f32[2048,256]{1,0:T(8,128)S(1)}) custom-call(f32[2048,256]{1,0:T(8,128)S(1)} %get-tuple-element.46.slip_ref, f32[2048,256]{1,0:T(8,128)S(1)} %get-tuple-element.56.state_ref, f32[2048,256]{1,0:T(8,128)S(1)} %get-tuple-element.70.slip_mid_ref, ...), custom_call_target="tpu_custom_call" | custom-call | tf_op jit(solution)/shard_map/pallas_call | solution.py:33
  92.6 0.9 collective-permute-done.19.refs_1_
  93.5 5.8 %collective-permute-done.20.refs_2_ = bf16[256,256]{1,0:T(8,128)(2,1)S(1)} collective-permute-done((bf16[256,256]{1,0:T(8,128)(2,1)S(1)}, bf16[256,256]{1,0:T(8,128)(2,1)S(1)}, u32[]{:S(2)}, u32[]{:S(2)}) %collective-permute-start.20) | collective-permute-done | bytes 131104 | tf_op jit(solution)/shard_map/ppermute | solution.py:368
  99.3 4.5 %shard_map.198 = (f32[2048,256]{1,0:T(8,128)}, f32[2048,256]{1,0:T(8,128)}) custom-call(f32[2048,256]{1,0:T(8,128)S(1)} %get-tuple-element.83.shift_ref, f32[2048,256]{1,0:T(8,128)S(1)} %get-tuple-element.72.scale_ref, f32[2048,256]{1,0:T(8,128)S(1)} %get-tuple-element.84.rest_ref, f32[2048,256]{1,0:T(8,128)S(1)} %get-tuple-element.85.slip_rest_ref, ...), custom_call_target="tpu_custom_call" | custom-call | tf_op jit(solution)/shard_map/pallas_call | solution.py:33
  (44 shorter events, 0.4 us)
Async XLA Ops:
  3.0 1.0 copy-start.3
  4.0 0.6 copy-start.9
  4.6 0.7 copy-start.11
  5.3 10.3 %collective-permute-start.2 = (bf16[256,256]{1,0:T(8,128)(2,1)S(1)}, bf16[256,256]{1,0:T(8,128)(2,1)S(1)}, u32[]{:S(2)}, u32[]{:S(2)}) collective-permute-start(bf16[256,256]{1,0:T(8,128)(2,1)S(1)} %get-tuple-element.47.coeff_ref.refs_0_), channel_id=1, source_target_pairs={{0,24},{8,0},{16,8},{24,16},{1,25},{9,1},{17,9},{25,17},{2,26},{10... | collective-permute-start | bytes 393224 | tf_op jit(solution)/shard_map/ppermute | solution.py:364
  9.2 12.0 %collective-permute-start.1 = (bf16[256,256]{1,0:T(8,128)(2,1)S(1)}, bf16[256,256]{1,0:T(8,128)(2,1)S(1)}, u32[]{:S(2)}, u32[]{:S(2)}) collective-permute-start(bf16[256,256]{1,0:T(8,128)(2,1)S(1)} %get-tuple-element.47.coeff_ref.refs_0_), channel_id=1, source_target_pairs={{0,16},{8,24},{16,0},{24,8},{1,17},{9,25},{17,1},{25,9},{2,18},{10... | collective-permute-start | bytes 393224 | tf_op jit(solution)/shard_map/ppermute | solution.py:364
  9.7 11.5 %collective-permute-start = (bf16[256,256]{1,0:T(8,128)(2,1)S(1)}, bf16[256,256]{1,0:T(8,128)(2,1)S(1)}, u32[]{:S(2)}, u32[]{:S(2)}) collective-permute-start(bf16[256,256]{1,0:T(8,128)(2,1)S(1)} %get-tuple-element.47.coeff_ref.refs_0_), channel_id=1, source_target_pairs={{0,8},{8,16},{16,24},{24,0},{1,9},{9,17},{17,25},{25,1},{2,10},{10... | collective-permute-start | bytes 393224 | tf_op jit(solution)/shard_map/ppermute | solution.py:364
  11.9 14.1 %collective-permute-start.6 = (bf16[128,512]{1,0:T(8,128)(2,1)S(1)}, bf16[128,512]{1,0:T(8,128)(2,1)S(1)}, u32[]{:S(2)}, u32[]{:S(2)}) collective-permute-start(bf16[128,512]{1,0:T(8,128)(2,1)S(1)} %get-tuple-element.58.refs_0_), channel_id=1, source_target_pairs={{0,6},{1,7},{2,0},{3,1},{4,2},{5,3},{6,4},{7,5},{8,14},{9,15},{10,... | collective-permute-start | bytes 393224 | tf_op jit(solution)/shard_map/ppermute | solution.py:368
  15.5 10.8 %collective-permute-start.5 = (bf16[128,512]{1,0:T(8,128)(2,1)S(1)}, bf16[128,512]{1,0:T(8,128)(2,1)S(1)}, u32[]{:S(2)}, u32[]{:S(2)}) collective-permute-start(bf16[128,512]{1,0:T(8,128)(2,1)S(1)} %get-tuple-element.58.refs_0_), channel_id=1, source_target_pairs={{0,4},{1,5},{2,6},{3,7},{4,0},{5,1},{6,2},{7,3},{8,12},{9,13},{10,... | collective-permute-start | bytes 393224 | tf_op jit(solution)/shard_map/ppermute | solution.py:368
  15.5 10.8 %collective-permute-start.4 = (bf16[128,512]{1,0:T(8,128)(2,1)S(1)}, bf16[128,512]{1,0:T(8,128)(2,1)S(1)}, u32[]{:S(2)}, u32[]{:S(2)}) collective-permute-start(bf16[128,512]{1,0:T(8,128)(2,1)S(1)} %get-tuple-element.58.refs_0_), channel_id=1, source_target_pairs={{0,2},{1,3},{2,4},{3,5},{4,6},{5,7},{6,0},{7,1},{8,10},{9,11},{10,... | collective-permute-start | bytes 393224 | tf_op jit(solution)/shard_map/ppermute | solution.py:368
  21.2 2.2 %copy-start = (bf16[4,2048,256]{2,1,0:T(8,128)(2,1)S(1)}, bf16[4,2048,256]{2,1,0:T(8,128)(2,1)}, u32[]{:S(2)}) copy-start(bf16[4,2048,256]{2,1,0:T(8,128)(2,1)} %fusion.matrix_ref) | copy-start | bytes 12582916
  23.4 2.6 %copy-start.7 = (bf16[256,256]{1,0:T(8,128)(2,1)}, bf16[256,256]{1,0:T(8,128)(2,1)S(1)}, u32[]{:S(2)}) copy-start(bf16[256,256]{1,0:T(8,128)(2,1)S(1)} %collective-permute-done.refs_1_) | copy-start | bytes 393220
  25.9 5.6 %collective-permute-start.3 = (bf16[1024,256]{1,0:T(8,128)(2,1)}, bf16[1024,256]{1,0:T(8,128)(2,1)}, u32[]{:S(2)}, u32[]{:S(2)}) collective-permute-start(bf16[1024,256]{1,0:T(8,128)(2,1)} %shard_map.188), channel_id=1, source_target_pairs={{0,1},{1,0},{2,3},{3,2},{4,5},{5,4},{6,7},{7,6},{8,9},{9,8},{10,11... | collective-permute-start | bytes 1572872 | tf_op jit(solution)/shard_map/ppermute | solution.py:371
  26.4 15.5 %collective-permute-start.7 = (bf16[512,512]{1,0:T(8,128)(2,1)S(1)}, bf16[512,512]{1,0:T(8,128)(2,1)S(1)}, u32[]{:S(2)}, u32[]{:S(2)}) collective-permute-start(bf16[512,512]{1,0:T(8,128)(2,1)S(1)} %shard_map.191.own_ref), channel_id=1, source_target_pairs={{0,1},{1,0},{2,3},{3,2},{4,5},{5,4},{6,7},{7,6},{8,9},{9,8},{10,11... | collective-permute-start | bytes 1572872 | tf_op jit(solution)/shard_map/ppermute | solution.py:371
  26.7 2.2 %copy-start.1 = (bf16[4,2048,256]{2,1,0:T(8,128)(2,1)S(1)}, bf16[4,2048,256]{2,1,0:T(8,128)(2,1)}, u32[]{:S(2)}) copy-start(bf16[4,2048,256]{2,1,0:T(8,128)(2,1)} %fusion.matrix_ref) | copy-start | bytes 12582916
  28.9 0.9 copy-start.8
  29.8 3.1 %copy-start.12 = (bf16[256,256]{1,0:T(8,128)(2,1)S(1)}, bf16[256,256]{1,0:T(8,128)(2,1)}, u32[]{:S(2)}) copy-start(bf16[256,256]{1,0:T(8,128)(2,1)} %copy-done.11) | copy-start | bytes 393220
  29.8 5.4 %copy-start.10 = (bf16[256,256]{1,0:T(8,128)(2,1)S(1)}, bf16[256,256]{1,0:T(8,128)(2,1)}, u32[]{:S(2)}) copy-start(bf16[256,256]{1,0:T(8,128)(2,1)} %copy-done.9) | copy-start | bytes 393220
  32.9 23.4 %collective-permute-start.8 = (bf16[256,256]{1,0:T(8,128)(2,1)S(1)}, bf16[256,256]{1,0:T(8,128)(2,1)S(1)}, u32[]{:S(2)}, u32[]{:S(2)}) collective-permute-start(bf16[256,256]{1,0:T(8,128)(2,1)S(1)} %copy-done.12), channel_id=1, source_target_pairs={{0,1},{1,2},{2,3},{3,4},{4,5},{5,6},{6,7},{7,8},{8,9},{9,10},{10,1... | collective-permute-start | bytes 393224 | tf_op jit(solution)/shard_map/ppermute | solution.py:376
  35.2 21.1 %collective-permute-start.9 = (bf16[256,256]{1,0:T(8,128)(2,1)S(1)}, bf16[256,256]{1,0:T(8,128)(2,1)S(1)}, u32[]{:S(2)}, u32[]{:S(2)}) collective-permute-start(bf16[256,256]{1,0:T(8,128)(2,1)S(1)} %copy-done.10), channel_id=1, source_target_pairs={{1,0},{2,1},{3,2},{4,3},{5,4},{6,5},{7,6},{8,7},{9,8},{10,9},{11,1... | collective-permute-start | bytes 393224 | tf_op jit(solution)/shard_map/ppermute | solution.py:376
  36.5 24.4 %collective-permute-start.10 = (bf16[256,256]{1,0:T(8,128)(2,1)S(1)}, bf16[256,256]{1,0:T(8,128)(2,1)S(1)}, u32[]{:S(2)}, u32[]{:S(2)}) collective-permute-start(bf16[256,256]{1,0:T(8,128)(2,1)S(1)} %get-tuple-element.67), channel_id=1, source_target_pairs={{0,2},{1,3},{2,4},{3,5},{4,6},{5,7},{6,0},{7,1},{8,10},{9,11},{10,... | collective-permute-start | bytes 393224 | tf_op jit(solution)/shard_map/ppermute | solution.py:368
  41.0 19.9 %collective-permute-start.11 = (bf16[256,256]{1,0:T(8,128)(2,1)S(1)}, bf16[256,256]{1,0:T(8,128)(2,1)S(1)}, u32[]{:S(2)}, u32[]{:S(2)}) collective-permute-start(bf16[256,256]{1,0:T(8,128)(2,1)S(1)} %get-tuple-element.68), channel_id=1, source_target_pairs={{0,4},{1,5},{2,6},{3,7},{4,0},{5,1},{6,2},{7,3},{8,12},{9,13},{10,... | collective-permute-start | bytes 393224 | tf_op jit(solution)/shard_map/ppermute | solution.py:368
  41.9 19.1 %collective-permute-start.12 = (bf16[256,256]{1,0:T(8,128)(2,1)S(1)}, bf16[256,256]{1,0:T(8,128)(2,1)S(1)}, u32[]{:S(2)}, u32[]{:S(2)}) collective-permute-start(bf16[256,256]{1,0:T(8,128)(2,1)S(1)} %get-tuple-element.69), channel_id=1, source_target_pairs={{0,6},{1,7},{2,0},{3,1},{4,2},{5,3},{6,4},{7,5},{8,14},{9,15},{10,... | collective-permute-start | bytes 393224 | tf_op jit(solution)/shard_map/ppermute | solution.py:368
  43.6 12.6 %copy-start.4 = (bf16[2048,256]{1,0:T(8,128)(2,1)S(1)}, bf16[2048,256]{1,0:T(8,128)(2,1)}, u32[]{:S(2)}) copy-start(bf16[2048,256]{1,0:T(8,128)(2,1)} %copy-done.3) | copy-start | bytes 3145732
  56.3 4.7 %copy-start.5 = (bf16[32,2048]{1,0:T(8,128)(2,1)S(1)}, bf16[32,2048]{1,0:T(8,128)(2,1)}, u32[]{:S(2)}) copy-start(bf16[32,2048]{1,0:T(8,128)(2,1)} %basis_out_ref.3) | copy-start | bytes 393220
  56.3 4.7 %copy-start.6 = (bf16[32,2048]{1,0:T(8,128)(2,1)S(1)}, bf16[32,2048]{1,0:T(8,128)(2,1)}, u32[]{:S(2)}) copy-start(bf16[32,2048]{1,0:T(8,128)(2,1)} %basis_in_ref.1) | copy-start | bytes 393220
  61.0 14.3 %copy-start.2 = (bf16[4,2048,256]{2,1,0:T(8,128)(2,1)S(1)}, bf16[4,2048,256]{2,1,0:T(8,128)(2,1)}, u32[]{:S(2)}) copy-start(bf16[4,2048,256]{2,1,0:T(8,128)(2,1)} %fusion.matrix_ref) | copy-start | bytes 12582916
  64.1 7.7 %collective-permute-start.15 = (bf16[256,256]{1,0:T(8,128)(2,1)S(1)}, bf16[256,256]{1,0:T(8,128)(2,1)S(1)}, u32[]{:S(2)}, u32[]{:S(2)}) collective-permute-start(bf16[256,256]{1,0:T(8,128)(2,1)S(1)} %get-tuple-element.74.refs_0_), channel_id=1, source_target_pairs={{0,24},{8,0},{16,8},{24,16},{1,25},{9,1},{17,9},{25,17},{2,26},{10... | collective-permute-start | bytes 393224 | tf_op jit(solution)/shard_map/ppermute | solution.py:364
  67.9 5.4 %collective-permute-start.14 = (bf16[256,256]{1,0:T(8,128)(2,1)S(1)}, bf16[256,256]{1,0:T(8,128)(2,1)S(1)}, u32[]{:S(2)}, u32[]{:S(2)}) collective-permute-start(bf16[256,256]{1,0:T(8,128)(2,1)S(1)} %get-tuple-element.74.refs_0_), channel_id=1, source_target_pairs={{0,16},{8,24},{16,0},{24,8},{1,17},{9,25},{17,1},{25,9},{2,18},{10... | collective-permute-start | bytes 393224 | tf_op jit(solution)/shard_map/ppermute | solution.py:364
  69.4 5.9 %collective-permute-start.13 = (bf16[256,256]{1,0:T(8,128)(2,1)S(1)}, bf16[256,256]{1,0:T(8,128)(2,1)S(1)}, u32[]{:S(2)}, u32[]{:S(2)}) collective-permute-start(bf16[256,256]{1,0:T(8,128)(2,1)S(1)} %get-tuple-element.74.refs_0_), channel_id=1, source_target_pairs={{0,8},{8,16},{16,24},{24,0},{1,9},{9,17},{17,25},{25,1},{2,10},{10... | collective-permute-start | bytes 393224 | tf_op jit(solution)/shard_map/ppermute | solution.py:364
  77.1 2.0 %collective-permute-start.16 = (bf16[1024,256]{1,0:T(8,128)(2,1)S(1)}, bf16[1024,256]{1,0:T(8,128)(2,1)S(1)}, u32[]{:S(2)}, u32[]{:S(2)}) collective-permute-start(bf16[1024,256]{1,0:T(8,128)(2,1)S(1)} %shard_map.195), channel_id=1, source_target_pairs={{0,1},{1,0},{2,3},{3,2},{4,5},{5,4},{6,7},{7,6},{8,9},{9,8},{10,11... | collective-permute-start | bytes 1572872 | tf_op jit(solution)/shard_map/ppermute | solution.py:371
  79.3 10.6 %collective-permute-start.17 = (bf16[256,256]{1,0:T(8,128)(2,1)S(1)}, bf16[256,256]{1,0:T(8,128)(2,1)S(1)}, u32[]{:S(2)}, u32[]{:S(2)}) collective-permute-start(bf16[256,256]{1,0:T(8,128)(2,1)S(1)} %get-tuple-element.81), channel_id=1, source_target_pairs={{0,1},{1,2},{2,3},{3,4},{4,5},{5,6},{6,7},{7,8},{8,9},{9,10},{10,1... | collective-permute-start | bytes 393224 | tf_op jit(solution)/shard_map/ppermute | solution.py:376
  81.6 8.3 %collective-permute-start.18 = (bf16[256,256]{1,0:T(8,128)(2,1)S(1)}, bf16[256,256]{1,0:T(8,128)(2,1)S(1)}, u32[]{:S(2)}, u32[]{:S(2)}) collective-permute-start(bf16[256,256]{1,0:T(8,128)(2,1)S(1)} %get-tuple-element.82), channel_id=1, source_target_pairs={{1,0},{2,1},{3,2},{4,3},{5,4},{6,5},{7,6},{8,7},{9,8},{10,9},{11,1... | collective-permute-start | bytes 393224 | tf_op jit(solution)/shard_map/ppermute | solution.py:376
  82.9 10.6 %collective-permute-start.19 = (bf16[256,256]{1,0:T(8,128)(2,1)S(1)}, bf16[256,256]{1,0:T(8,128)(2,1)S(1)}, u32[]{:S(2)}, u32[]{:S(2)}) collective-permute-start(bf16[256,256]{1,0:T(8,128)(2,1)S(1)} %get-tuple-element.87), channel_id=1, source_target_pairs={{0,2},{1,3},{2,4},{3,5},{4,6},{5,7},{6,0},{7,1},{8,10},{9,11},{10,... | collective-permute-start | bytes 393224 | tf_op jit(solution)/shard_map/ppermute | solution.py:368
  85.5 13.8 %collective-permute-start.20 = (bf16[256,256]{1,0:T(8,128)(2,1)S(1)}, bf16[256,256]{1,0:T(8,128)(2,1)S(1)}, u32[]{:S(2)}, u32[]{:S(2)}) collective-permute-start(bf16[256,256]{1,0:T(8,128)(2,1)S(1)} %get-tuple-element.88), channel_id=1, source_target_pairs={{0,4},{1,5},{2,6},{3,7},{4,0},{5,1},{6,2},{7,3},{8,12},{9,13},{10,... | collective-permute-start | bytes 393224 | tf_op jit(solution)/shard_map/ppermute | solution.py:368
  87.3 12.0 %collective-permute-start.21 = (bf16[256,256]{1,0:T(8,128)(2,1)S(1)}, bf16[256,256]{1,0:T(8,128)(2,1)S(1)}, u32[]{:S(2)}, u32[]{:S(2)}) collective-permute-start(bf16[256,256]{1,0:T(8,128)(2,1)S(1)} %get-tuple-element.89), channel_id=1, source_target_pairs={{0,6},{1,7},{2,0},{3,1},{4,2},{5,3},{6,4},{7,5},{8,14},{9,15},{10,... | collective-permute-start | bytes 393224 | tf_op jit(solution)/shard_map/ppermute | solution.py:368

commit v3 on v2

--- a/solution.py
+++ b/solution.py
@@ -95,7 +95,7 @@
 
 
 def ranks_kernel(
-    col_count, where_ref, rank_hbm, now_hbm, rate_hbm, coeff_ref, wide_ref, joined_ref, rank_ref, sems
+    col_count, where_ref, rank_hbm, now_hbm, rate_hbm, wide_ref, joined_ref, rank_ref, sems
 ):
     sources, share, blocks = rank_ref.shape
     ens = now_hbm.shape[1]
@@ -129,31 +129,57 @@
         out_ref[k * size : (k + 1) * size, :] = piece[...]
 
 
-def weights_kernel(
+def fill_numbers(vectors, numbers_ref):
+    @pl.loop(0, numbers_ref.shape[0] // BS)
+    def _(n):
+        at = rows_at(n, BS)
+        load, normal, direct, evolution, distance, stiffness = (vectors[k, :, at] for k in range(6))
+        rows = [load, normal, 1.0 / direct, 1.0 / evolution, evolution / distance, stiffness, load, normal]
+        numbers_ref[at, :] = jnp.concatenate(rows, axis=0).T
+
+
+def weights_first_kernel(
     heights, size, where_ref, load_hbm, normal_hbm, direct_hbm, evolution_hbm, distance_hbm, stiffness_hbm,
-    count_hbm, bricks_hbm, weight_hbm, near_hbm, state_hbm, after_ref, numbers_ref, matrix_ref, near_ref, state_ref,
+    count_hbm, bricks_hbm, weight_hbm, after_ref, numbers_ref, matrix_ref,
     vectors, count_ref, bricks_ref, weight_ref, id_wide, share_wide, sems,
 ):
-    slots, patches = bricks_ref.shape
     sources = [load_hbm, normal_hbm, direct_hbm, evolution_hbm, distance_hbm, stiffness_hbm]
     small = [(source, vectors.at[k]) for k, source in enumerate(sources)]
     small = small + [(count_hbm, count_ref), (bricks_hbm, bricks_ref), (weight_hbm, weight_ref)]
+    for copy in start_copies(small, sems):
+        copy.wait()
+    fill_numbers(vectors, numbers_ref)
+    fill_weights(heights, size, 0, where_ref, count_ref, bricks_ref, weight_ref, matrix_ref, id_wide, share_wide)
+
+
+def weights_second_kernel(
+    heights, size, where_ref, count_hbm, bricks_hbm, weight_hbm, near_hbm, state_hbm, after_ref,
+    matrix_ref, near_ref, state_ref, count_ref, bricks_ref, weight_ref, id_wide, share_wide, sems,
+):
+    small = [(count_hbm, count_ref), (bricks_hbm, bricks_ref), (weight_hbm, weight_ref)]
     copies = start_copies(small, sems)
     large = start_copies([(near_hbm, near_ref), (state_hbm, state_ref)], sems, len(small))
+    for copy in copies:
+        copy.wait()
+    half = bricks_ref.shape[1] // 2
+    fill_weights(heights, size, half, where_ref, count_ref, bricks_ref, weight_ref, matrix_ref, id_wide, share_wide)
+    for copy in large:
+        copy.wait()
+
+
+def fill_weights(
+    heights, size, start, where_ref, count_ref, bricks_ref, weight_ref, matrix_ref, id_wide, share_wide
+):
+    slots = bricks_ref.shape[0]
     height, core = where_ref[0].astype(F32), where_ref[1].astype(F32)
     lanes = 128
     column = lax.div(lax.broadcasted_iota(jnp.int32, (slots, slots * lanes), 1), lanes)
     spread = (column == lax.broadcasted_iota(jnp.int32, (slots, slots * lanes), 0)).astype(F32).astype(BF16)
     spread_both = jnp.concatenate([spread, spread], axis=0)
-    for copy in copies:
-        copy.wait()
-
-    @pl.loop(0, patches // BS)
+
+    @pl.loop(0, matrix_ref.shape[0] // BS)
     def _(n):
-        at = rows_at(n, BS)
-        load, normal, direct, evolution, distance, stiffness = (vectors[k, :, at] for k in range(6))
-        rows = [load, normal, 1.0 / direct, 1.0 / evolution, evolution / distance, stiffness, load, normal]
-        numbers_ref[at, :] = jnp.concatenate(rows, axis=0).T
+        at = pl.ds(pl.multiple_of(start + n * BS, BS), BS)
         bricks = bricks_ref[:, at].astype(F32)
         live = lax.broadcasted_iota(jnp.int32, (slots, BS), 0) < count_ref[:, at]
         weights = jnp.where(live, weight_ref[:, at], 0.0)
@@ -187,35 +213,40 @@
                     tile = jnp.where(ids[k] == here, values[k], tile)
                 matrix_ref[to, left : left + lanes] = tile.astype(BF16)
 
-    for copy in large:
-        copy.wait()
-
-
-def couple_kernel(sources, heights, where_ref, matrix_ref, *refs):
+
+def couple_kernel(sources, where_ref, matrix_ref, *refs):
     coeffs, out_ref = refs[:sources], refs[sources]
-    share = coeffs[0].shape[0]
-
-    @pl.loop(0, heights)
-    def _(d):
-        height = lax.rem(where_ref[0] + d, heights)
-        at = rows_at(2 * height + where_ref[1], share)
-        total = None
-        for step in range(sources):
-            term = dot(matrix_ref[where_ref[2 + step], at, :], coeffs[step][...])
-            total = term if total is None else total + term
-        out_ref[rows_at(d, share), :] = total.astype(out_ref.dtype)
+    total = None
+    for step in range(sources):
+        term = dot(matrix_ref[where_ref[2 + step]], coeffs[step][...])
+        total = term if total is None else total + term
+    out_ref[...] = total.astype(out_ref.dtype)
 
 
 def couple(where, matrix, coeffs, heights, kind):
+    sources, rows, width = matrix.shape
     share, ens = coeffs[0].shape
-    return call(
-        functools.partial(couple_kernel, len(coeffs), heights),
-        jax.ShapeDtypeStruct((heights * share, ens), kind),
-        where,
-        matrix,
-        *coeffs,
-        specs=[SMEM] + [VMEM] * (1 + len(coeffs)),
-    )
+    return pl.pallas_call(
+        functools.partial(couple_kernel, sources),
+        grid_spec=pltpu.PrefetchScalarGridSpec(
+            num_scalar_prefetch=1,
+            grid=(heights,),
+            in_specs=[
+                pl.BlockSpec(
+                    (sources, share, width), lambda d, w: (0, 2 * lax.rem(w[0] + d, heights) + w[1], 0)
+                )
+            ]
+            + [VMEM] * sources,
+            out_specs=pl.BlockSpec((share, ens), lambda d, w: (d, 0)),
+        ),
+        out_shape=jax.ShapeDtypeStruct((heights * share, ens), kind),
+        compiler_params=pltpu.CompilerParams(vmem_limit_bytes=LIMIT),
+    )(where, *in_hbm(matrix), *coeffs)
+
+
+def edges_kernel(first_ref, last_ref, after_ref, first_out, last_out):
+    first_out[...] = first_ref[...]
+    last_out[...] = last_ref[...]
 
 
 def chip_sum_kernel(kept_ref, sent_ref, *outs):
@@ -243,16 +274,16 @@
 
 
 def prepare_first_kernel(
-    matrix_ref, own_ref, other_ref, slip_ref, state_ref, numbers_ref, near_ref, rounded_ref, first_ref,
+    low_ref, high_ref, own_ref, other_ref, slip_ref, state_ref, numbers_ref, near_ref, rounded_ref, first_ref,
     last_ref, shift_ref, scale_ref, rest_ref, scale_mid_ref,
 ):
     half = own_ref.shape[0]
-    patches, ens = slip_ref.shape
-
-    @pl.loop(0, patches // BS)
-    def _(n):
-        at = rows_at(n, BS)
-        total = dot(matrix_ref[at, :half], own_ref[...]) + dot(matrix_ref[at, half:], other_ref[...])
+    ens = slip_ref.shape[1]
+    blocks = low_ref.shape[0] // BS
+
+    def block(matrix_ref, m, n):
+        at, own_at = rows_at(n, BS), rows_at(m, BS)
+        total = dot(matrix_ref[own_at, :half], own_ref[...]) + dot(matrix_ref[own_at, half:], other_ref[...])
         numbers = numbers_ref[at, :]
         normal, inv_direct, inv_evolution, ratio = (numbers[:, k : k + 1] for k in range(1, 5))
         base = total[:, :ens]
@@ -263,6 +294,14 @@
         tau = near_tau(n, slip_ref[at, :], numbers, near_ref, rounded_ref, first_ref, last_ref)
         shift_ref[at, :] = tau * scale - state * inv_direct
         rest_ref[at, :] = state + (STEP_SIZE * ratio) * jnp.exp((REF_FRICTION - state) * inv_evolution)
+
+    @pl.loop(0, blocks)
+    def _(m):
+        block(low_ref, m, m)
+
+    @pl.loop(0, blocks)
+    def _(m):
+        block(high_ref, m, blocks + m)
 
 
 def far_speed(n, shift_ref, scale_ref, basis_ref, parts):
@@ -327,8 +366,7 @@
     blocks = rows // R
     keep = jnp.arange(R, dtype=jnp.int32).astype(F32)[None, None, :, None] < wide[:, :, None, :]
     matrix = jnp.transpose(coupling, (1, 0, 2)).reshape(sources, blocks, R, width)
-    masked = jnp.where(keep, matrix, jnp.zeros((), BF16)).reshape(sources, rows, width)
-    return pltpu.with_memory_space_constraint(masked, pltpu.VMEM)
+    return jnp.where(keep, matrix, jnp.zeros((), BF16)).reshape(sources, rows, width)
 
 
 def per_device(
@@ -387,7 +425,7 @@
         sent = to_core(couple(pair_where, masked, coeffs, heights, BF16))
         kept = couple(own_where, masked, coeffs, heights, F32)
         pieces = chip_sum(kept, sent, heights)
-        pieces, first, last = lax.optimization_barrier((pieces, first, last))
+        first, last = call(edges_kernel, [edge, edge], first, last, pieces[0])
         parts = pieces[:1] + [to_height(pieces[d], d) for d in range(1, heights)]
         return parts, *halo(first, last)
 
@@ -399,8 +437,6 @@
     edge = jax.ShapeDtypeStruct((BS, ens), BF16)
     per_patch = [tau_load, normal_stress, direct_effect, evolution_effect, slip_distance, self_stiffness]
 
-    coeff, rounded, first, last, slip = project(slip, basis_in)
-    coeffs = row_coeffs(coeff)
     ranks = jnp.transpose(block_rank, (1, 2, 0))
     place = jnp.stack([row_index, col_index]).astype(jnp.int32)
     wide, joined = call(
@@ -411,8 +447,7 @@
         ],
         place,
         *in_hbm(ranks, pressure_now, pressure_rate),
-        coeff,
-        specs=[SMEM] + [HBM] * 3 + [VMEM],
+        specs=[SMEM] + [HBM] * 3,
         scratch_shapes=[pltpu.VMEM(ranks.shape, jnp.int32), pltpu.SemaphoreType.DMA((3,))],
     )
     own = call(
@@ -423,31 +458,41 @@
     )
     other = to_core(own)
     masked = masked_coupling(coupling, wide)
+    masked, slip = lax.optimization_barrier((masked, slip))
+    coeff, rounded, first, last, slip = project(slip, basis_in)
+    coeffs = row_coeffs(coeff)
+    place = jnp.stack([height, core]).astype(jnp.int32)
+    brick_lists = [adj_count[None], adj_bricks, adj_weight]
+    part = jax.ShapeDtypeStruct((patches // 2, 2 * heights * size), BF16)
+    list_scratch = [
+        pltpu.VMEM((1, patches), jnp.int32),
+        pltpu.VMEM(adj_bricks.shape, jnp.int32),
+        pltpu.VMEM(adj_weight.shape, F32),
+        pltpu.VMEM((BS, slots * 128), F32),
+        pltpu.VMEM((BS, slots * 128), F32),
+    ]
+    numbers, low = call(
+        functools.partial(weights_first_kernel, heights, size),
+        [jax.ShapeDtypeStruct((patches, 8), F32), part],
+        place,
+        *in_hbm(*[array[None] for array in per_patch], *brick_lists),
+        coeff,
+        specs=[SMEM] + [HBM] * 9 + [VMEM],
+        scratch_shapes=[pltpu.VMEM((6, 1, patches), F32)] + list_scratch + [pltpu.SemaphoreType.DMA((9,))],
+    )
+    coeffs, low = lax.optimization_barrier((coeffs, low))
     parts, before, after = far_parts(coeffs, first, last)
-    numbers, matrix, near, state = call(
-        functools.partial(weights_kernel, heights, size),
-        [
-            jax.ShapeDtypeStruct((patches, 8), F32),
-            jax.ShapeDtypeStruct((patches, 2 * heights * size), BF16),
-            jax.ShapeDtypeStruct(near_blocks.shape, BF16),
-            full,
-        ],
-        jnp.stack([height, core]).astype(jnp.int32),
-        *in_hbm(*[array[None] for array in per_patch], adj_count[None], adj_bricks, adj_weight, near_blocks, state),
+    high, near, state = call(
+        functools.partial(weights_second_kernel, heights, size),
+        [part, jax.ShapeDtypeStruct(near_blocks.shape, BF16), full],
+        place,
+        *in_hbm(*brick_lists, near_blocks, state),
         parts[0],
-        specs=[SMEM] + [HBM] * 11 + [VMEM],
-        scratch_shapes=[
-            pltpu.VMEM((6, 1, patches), F32),
-            pltpu.VMEM((1, patches), jnp.int32),
-            pltpu.VMEM(adj_bricks.shape, jnp.int32),
-            pltpu.VMEM(adj_weight.shape, F32),
-            pltpu.VMEM((BS, slots * 128), F32),
-            pltpu.VMEM((BS, slots * 128), F32),
-            pltpu.SemaphoreType.DMA((11,)),
-        ],
+        specs=[SMEM] + [HBM] * 5 + [VMEM],
+        scratch_shapes=list_scratch + [pltpu.SemaphoreType.DMA((5,))],
     )
     shift, scale, rest, scale_mid = call(
-        prepare_first_kernel, [full] * 4, matrix, own, other, slip, state, numbers, near, rounded, before, after
+        prepare_first_kernel, [full] * 4, low, high, own, other, slip, state, numbers, near, rounded, before, after
     )
     slip_mid, state_mid, rounded, coeff, first, last = call(
         functools.partial(finish_first_kernel, heights),

time: 104 us -> 115 us (1.11)
  Pallas kernels: 40.8 us -> 55.1 us
  local copies, waits for them, and re-layouts: 7.84 us -> 3.84 us
    pallas_call x0 -> x4, Pallas kernels: none -> 15.7 us  [couple(): pl.pallas_call(functools.partial(couple_kernel, sources), grid_spec=pltpu...]
    unnamed x26 -> x20, local copies, waits for them, and re-layouts: 7.59 us -> 3.6 us
    pallas_call x14 -> x13, Pallas kernels: 40.8 us -> 39.5 us  [call(): pl.pallas_call(kernel, in_specs=specs or [VMEM] * len(operands), out_shap...]
  transfers between devices with their start and end apart: 22 -> 22, of which waited for: 7 -> 5; matrix products, arithmetic and copies ran while one was open for 5% -> 0% of each run, Pallas kernels for 28% -> 34%
where the time goes in v3:
time: 115 us; the launch traced here: 114 us
  Pallas kernels  55.1 us (48%)
  starting transfers between devices  36.8 us (32%)
  waiting for transfers between devices  12.6 us (11%)
  other arithmetic  4.63 us (4%)
  local copies, waits for them, and re-layouts  3.84 us (3%)
    pallas_call x13, Pallas kernels, call(): pl.pallas_call(kernel, in_specs=specs or [VMEM] * len(operands), out_shap...  39.5 us
    ppermute x9, starting transfers between devices, to_height(): return lax.ppermute(array, 'col', pairs)  19.1 us
    pallas_call x4, Pallas kernels, couple(): pl.pallas_call(functools.partial(couple_kernel, sources), grid_spec=pltpu...  15.7 us
    ppermute x6, starting transfers between devices, to_row(): lax.ppermute(array, 'row', [(i, (i + d) % row_count) for i in range(row_c...  10.2 us
    ppermute x4, starting transfers between devices, halo(): return (lax.ppermute(last, both, up), lax.ppermute(first, both, down))  6.92 us
    ppermute x9, waiting for transfers between devices, to_height(): return lax.ppermute(array, 'col', pairs)  6.7 us
    ppermute x6, waiting for transfers between devices, to_row(): lax.ppermute(array, 'row', [(i, (i + d) % row_count) for i in range(row_c...  5.87 us
    select_n x1, other arithmetic, masked_coupling(): jnp.where(keep, matrix, jnp.zeros((), BF16)).reshape(sources, rows, width)  4.48 us
  transfers between devices with their start and end apart: 22, of which 5 were waited for; matrix products, arithmetic and copies ran while one was open for 0% of the time, Pallas kernels for 34%

profile of v3, /device:TPU:0, one launch (start us, length us, event | category | flops | bytes accessed | tf_op | source)
XLA Modules:
  0.0 113.9 jit_solution(4861340328394994152)
XLA Ops:
  0.7 0.1 lt.43
  0.7 0.1 pad_add_fusion.where_ref
  0.8 2.2 %shard_map.185 = (f32[4,64,256]{2,1,0:T(8,128)S(1)}, bf16[128,512]{1,0:T(8,128)(2,1)}) custom-call(s32[2]{0:T(128)S(1)} %pad_add_fusion.where_ref, s32[4,8,64]{2,1,0:T(8,128)} %bitcast.25, bf16[128,256]{1,0:T(8,128)(2,1)} %now_hbm.1, bf16[128,256]{1,0:T(8,128)(2,1)} %rate_hbm.1), custom_call_target="tpu_custom_call" | custom-call | tf_op jit(solution)/shard_map/pallas_call | solution.py:33
  3.0 4.5 %fusion.matrix_ref = bf16[4,2048,256]{2,1,0:T(8,128)(2,1)} fusion(bf16[2048,4,256]{2,1,0:T(4,128)(2,1)} %param.29, f32[4,64,256]{2,1,0:T(8,128)S(1)} %get-tuple-element.46, f32[2048]{0:T(1024)S(1)} %lt.43), kind=kLoop, calls=%fused_computation.1 | loop fusion | flops 4194304 | bytes 8658944 | tf_op jit(solution)/shard_map/jit(_where)/select_n | solution.py:369
  7.5 2.4 %shard_map.186 = (bf16[256,256]{1,0:T(8,128)(2,1)S(1)}, bf16[2048,256]{1,0:T(8,128)(2,1)S(1)}, bf16[256,256]{1,0:T(8,128)(2,1)S(1)}, bf16[256,256]{1,0:T(8,128)(2,1)S(1)}, f32[2048,256]{1,0:T(8,128)S(1)}) custom-call(f32[2048,256]{1,0:T(8,128)} %slip_hbm, bf16[32,2048]{1,0:T(8,128)(2,1)} %basis_in_ref.1), custom_call_target="tpu_custom_call" | custom-call | tf_op jit(solution)/shard_map/pallas_call | solution.py:33
  9.8 1.0 copy-done.2
  10.8 0.6 copy-done.6
  11.4 0.6 copy-done.8
  12.1 3.9 %collective-permute-start.2 = (bf16[256,256]{1,0:T(8,128)(2,1)S(1)}, bf16[256,256]{1,0:T(8,128)(2,1)S(1)}, u32[]{:S(2)}, u32[]{:S(2)}) collective-permute-start(bf16[256,256]{1,0:T(8,128)(2,1)S(1)} %get-tuple-element.52.after_ref.refs_0_), channel_id=1, source_target_pairs={{0,24},{8,0},{16,8},{24,16},{1,25},{9,1},{17,9},{25,17},{2,26},{10... | collective-permute-start | bytes 393224 | tf_op jit(solution)/shard_map/ppermute | solution.py:402
  16.0 0.5 collective-permute-start.1
  16.5 0.6 collective-permute-start
  17.1 3.6 %collective-permute-start.6 = (bf16[128,512]{1,0:T(8,128)(2,1)}, bf16[128,512]{1,0:T(8,128)(2,1)}, u32[]{:S(2)}, u32[]{:S(2)}) collective-permute-start(bf16[128,512]{1,0:T(8,128)(2,1)} %get-tuple-element.60.refs_0_), channel_id=1, source_target_pairs={{0,6},{1,7},{2,0},{3,1},{4,2},{5,3},{6,4},{7,5},{8,14},{9,15},{10,... | collective-permute-start | bytes 393224 | tf_op jit(solution)/shard_map/ppermute | solution.py:406
  20.7 1.0 collective-permute-start.4
  21.7 0.1 stack.58.where_ref
  21.8 0.1 pad_add_fusion.1.where_ref
  21.9 8.3 %shard_map.187 = (f32[2048,8]{1,0:T(8,128)S(1)}, bf16[1024,1024]{1,0:T(8,128)(2,1)S(1)}) custom-call(s32[2]{0:T(128)S(1)} %pad_add_fusion.1.where_ref, f32[1,2048]{1,0:T(1,128)} %bitcast.26, f32[1,2048]{1,0:T(1,128)} %bitcast.27, f32[1,2048]{1,0:T(1,128)} %bitcast.28, f32[1,2048]{1,0:T(1,128)} %bitcast.29, f32[1,2048]{1,0:T(1,128)} %bitcast.30, ...), custom_call_target="tpu_custom_call" | custom-call | tf_op jit(solution)/shard_map/pallas_call | solution.py:33
  30.1 1.3 %copy-done = bf16[1024,1024]{1,0:T(8,128)(2,1)} copy-done((bf16[1024,1024]{1,0:T(8,128)(2,1)}, bf16[1024,1024]{1,0:T(8,128)(2,1)S(1)}, u32[]{:S(2)}) %copy-start) | copy-done | bytes 2097176
  31.5 4.6 %shard_map.189 = bf16[1024,256]{1,0:T(8,128)(2,1)} custom-call(s32[6]{0:T(128)S(1)} %stack.58.where_ref, bf16[4,2048,256]{2,1,0:T(8,128)(2,1)} %fusion.matrix_ref, bf16[256,256]{1,0:T(8,128)(2,1)S(1)} %get-tuple-element.52.after_ref.refs_0_, bf16[256,256]{1,0:T(8,128)(2,1)} %collective-permute-done.refs_1_, ...), custom_call_target="tpu_custom_call" | custom-call | tf_op jit(solution)/shard_map/pallas_call | solution.py:229
  36.1 1.9 %shard_map.192.own_ref = bf16[512,512]{1,0:T(8,128)(2,1)} custom-call(bf16[128,512]{1,0:T(8,128)(2,1)} %get-tuple-element.60.refs_0_, bf16[128,512]{1,0:T(8,128)(2,1)} %collective-permute-done.4.refs_1_, bf16[128,512]{1,0:T(8,128)(2,1)} %collective-permute-done.5.refs_2_, bf16[128,512]{1,0:T(8,128)(2,1)} %collective-permute-done.6.refs_3_), custom_call_target="tpu_custom_call" | custom-call | tf_op jit(solution)/shard_map/pallas_call | solution.py:33
  38.1 0.5 collective-permute-start.7
  38.6 0.1 stack.56.where_ref
  38.6 3.7 %shard_map.188.kept_ref = f32[1024,256]{1,0:T(8,128)S(1)} custom-call(s32[6]{0:T(128)S(1)} %stack.56.where_ref, bf16[4,2048,256]{2,1,0:T(8,128)(2,1)} %fusion.matrix_ref, bf16[256,256]{1,0:T(8,128)(2,1)S(1)} %get-tuple-element.52.after_ref.refs_0_, bf16[256,256]{1,0:T(8,128)(2,1)} %collective-permute-done.refs_1_, ...), custom_call_target="tpu_custom_call" | custom-call | tf_op jit(solution)/shard_map/pallas_call | solution.py:229
  42.4 1.3 %shard_map.190 = (bf16[256,256]{1,0:T(8,128)(2,1)S(1)}, bf16[256,256]{1,0:T(8,128)(2,1)S(1)}, bf16[256,256]{1,0:T(8,128)(2,1)S(1)}, bf16[256,256]{1,0:T(8,128)(2,1)S(1)}) custom-call(f32[1024,256]{1,0:T(8,128)S(1)} %shard_map.188.kept_ref, bf16[1024,256]{1,0:T(8,128)(2,1)} %collective-permute-done.3.sent_ref), custom_call_target="tpu_custom_call" | custom-call | tf_op jit(solution)/shard_map/pallas_call | solution.py:33
  43.7 1.9 %collective-permute-start.8 = (bf16[256,256]{1,0:T(8,128)(2,1)S(1)}, bf16[256,256]{1,0:T(8,128)(2,1)S(1)}, u32[]{:S(2)}, u32[]{:S(2)}) collective-permute-start(bf16[256,256]{1,0:T(8,128)(2,1)S(1)} %get-tuple-element.66), channel_id=1, source_target_pairs={{0,1},{1,2},{2,3},{3,4},{4,5},{5,6},{6,7},{7,8},{8,9},{9,10},{10,1... | collective-permute-start | bytes 393224 | tf_op jit(solution)/shard_map/ppermute | solution.py:414
  45.7 1.3 %collective-permute-start.9 = (bf16[256,256]{1,0:T(8,128)(2,1)S(1)}, bf16[256,256]{1,0:T(8,128)(2,1)S(1)}, u32[]{:S(2)}, u32[]{:S(2)}) collective-permute-start(bf16[256,256]{1,0:T(8,128)(2,1)S(1)} %get-tuple-element.67), channel_id=1, source_target_pairs={{1,0},{2,1},{3,2},{4,3},{5,4},{6,5},{7,6},{8,7},{9,8},{10,9},{11,1... | collective-permute-start | bytes 393224 | tf_op jit(solution)/shard_map/ppermute | solution.py:414
  47.0 4.9 %collective-permute-start.10 = (bf16[256,256]{1,0:T(8,128)(2,1)S(1)}, bf16[256,256]{1,0:T(8,128)(2,1)S(1)}, u32[]{:S(2)}, u32[]{:S(2)}) collective-permute-start(bf16[256,256]{1,0:T(8,128)(2,1)S(1)} %get-tuple-element.71), channel_id=1, source_target_pairs={{0,2},{1,3},{2,4},{3,5},{4,6},{5,7},{6,0},{7,1},{8,10},{9,11},{10,... | collective-permute-start | bytes 393224 | tf_op jit(solution)/shard_map/ppermute | solution.py:406
  51.8 0.9 collective-permute-start.11
  52.7 1.9 %collective-permute-start.12 = (bf16[256,256]{1,0:T(8,128)(2,1)S(1)}, bf16[256,256]{1,0:T(8,128)(2,1)S(1)}, u32[]{:S(2)}, u32[]{:S(2)}) collective-permute-start(bf16[256,256]{1,0:T(8,128)(2,1)S(1)} %get-tuple-element.73), channel_id=1, source_target_pairs={{0,6},{1,7},{2,0},{3,1},{4,2},{5,3},{6,4},{7,5},{8,14},{9,15},{10,... | collective-permute-start | bytes 393224 | tf_op jit(solution)/shard_map/ppermute | solution.py:406
  54.6 7.0 %shard_map.191 = (bf16[1024,1024]{1,0:T(8,128)(2,1)S(1)}, bf16[3,2048,256]{2,1,0:T(8,128)(2,1)S(1)}, f32[2048,256]{1,0:T(8,128)S(1)}) custom-call(s32[2]{0:T(128)S(1)} %pad_add_fusion.1.where_ref, s32[1,2048]{1,0:T(1,128)} %bitcast.24, s32[8,2048]{1,0:T(8,128)} %bricks_hbm.3, f32[8,2048]{1,0:T(8,128)} %weight_hbm.3, bf16[3,2048,256]{2,1,0:T(8,128)(2,1)} %near_hbm.1, ...), custom_call_target="tpu_custom_call" | custom-call | tf_op jit(solution)/shard_map/pallas_call | solution.py:33
  61.7 5.9 %shard_map.194 = (f32[2048,256]{1,0:T(8,128)S(1)}, f32[2048,256]{1,0:T(8,128)S(1)}, f32[2048,256]{1,0:T(8,128)S(1)}, f32[2048,256]{1,0:T(8,128)S(1)}) custom-call(bf16[1024,1024]{1,0:T(8,128)(2,1)S(1)} %copy-done.1, bf16[1024,1024]{1,0:T(8,128)(2,1)S(1)} %get-tuple-element.59.high_ref, bf16[512,512]{1,0:T(8,128)(2,1)} %shard_map.192.own_ref, ...), custom_call_target="tpu_custom_call" | custom-call | tf_op jit(solution)/shard_map/pallas_call | solution.py:33
  67.6 3.1 %shard_map.195 = (f32[2048,256]{1,0:T(8,128)S(1)}, f32[2048,256]{1,0:T(8,128)S(1)}, bf16[2048,256]{1,0:T(8,128)(2,1)S(1)}, bf16[256,256]{1,0:T(8,128)(2,1)S(1)},...) custom-call(f32[2048,256]{1,0:T(8,128)S(1)} %get-tuple-element.68.shift_ref, ...), custom_call_target="tpu_custom_call" | custom-call | tf_op jit(solution)/shard_map/pallas_call | solution.py:33
  70.7 4.5 %collective-permute-start.15 = (bf16[256,256]{1,0:T(8,128)(2,1)S(1)}, bf16[256,256]{1,0:T(8,128)(2,1)S(1)}, u32[]{:S(2)}, u32[]{:S(2)}) collective-permute-start(bf16[256,256]{1,0:T(8,128)(2,1)S(1)} %get-tuple-element.80.refs_0_), channel_id=1, source_target_pairs={{0,24},{8,0},{16,8},{24,16},{1,25},{9,1},{17,9},{25,17},{2,26},{10... | collective-permute-start | bytes 393224 | tf_op jit(solution)/shard_map/ppermute | solution.py:402
  75.2 0.7 collective-permute-start.14
  75.9 2.5 %collective-permute-done.15.refs_3_ = bf16[256,256]{1,0:T(8,128)(2,1)S(1)} collective-permute-done((bf16[256,256]{1,0:T(8,128)(2,1)S(1)}, bf16[256,256]{1,0:T(8,128)(2,1)S(1)}, u32[]{:S(2)}, u32[]{:S(2)}) %collective-permute-start.15) | collective-permute-done | bytes 131104 | tf_op jit(solution)/shard_map/ppermute | solution.py:402
  78.4 1.8 %collective-permute-done.14.refs_2_ = bf16[256,256]{1,0:T(8,128)(2,1)S(1)} collective-permute-done((bf16[256,256]{1,0:T(8,128)(2,1)S(1)}, bf16[256,256]{1,0:T(8,128)(2,1)S(1)}, u32[]{:S(2)}, u32[]{:S(2)}) %collective-permute-start.14) | collective-permute-done | bytes 131104 | tf_op jit(solution)/shard_map/ppermute | solution.py:402
  80.2 1.6 %collective-permute-done.13.refs_1_ = bf16[256,256]{1,0:T(8,128)(2,1)S(1)} collective-permute-done((bf16[256,256]{1,0:T(8,128)(2,1)S(1)}, bf16[256,256]{1,0:T(8,128)(2,1)S(1)}, u32[]{:S(2)}, u32[]{:S(2)}) %collective-permute-start.13) | collective-permute-done | bytes 131104 | tf_op jit(solution)/shard_map/ppermute | solution.py:402
  81.8 3.7 %shard_map.197 = bf16[1024,256]{1,0:T(8,128)(2,1)S(1)} custom-call(s32[6]{0:T(128)S(1)} %stack.58.where_ref, bf16[4,2048,256]{2,1,0:T(8,128)(2,1)} %fusion.matrix_ref, bf16[256,256]{1,0:T(8,128)(2,1)S(1)} %get-tuple-element.80.refs_0_, bf16[256,256]{1,0:T(8,128)(2,1)S(1)} %collective-permute-done.13.refs_1_, ...), custom_call_target="tpu_custom_call" | custom-call | tf_op jit(solution)/shard_map/pallas_call | solution.py:229
  85.5 3.7 %shard_map.196.kept_ref = f32[1024,256]{1,0:T(8,128)S(1)} custom-call(s32[6]{0:T(128)S(1)} %stack.56.where_ref, bf16[4,2048,256]{2,1,0:T(8,128)(2,1)} %fusion.matrix_ref, bf16[256,256]{1,0:T(8,128)(2,1)S(1)} %get-tuple-element.80.refs_0_, bf16[256,256]{1,0:T(8,128)(2,1)S(1)} %collective-permute-done.13.refs_1_, ...), custom_call_target="tpu_custom_call" | custom-call | tf_op jit(solution)/shard_map/pallas_call | solution.py:229
  89.2 0.3 shard_map.198
  89.5 2.4 %collective-permute-start.17 = (bf16[256,256]{1,0:T(8,128)(2,1)S(1)}, bf16[256,256]{1,0:T(8,128)(2,1)S(1)}, u32[]{:S(2)}, u32[]{:S(2)}) collective-permute-start(bf16[256,256]{1,0:T(8,128)(2,1)S(1)} %get-tuple-element.82), channel_id=1, source_target_pairs={{0,1},{1,2},{2,3},{3,4},{4,5},{5,6},{6,7},{7,8},{8,9},{9,10},{10,1... | collective-permute-start | bytes 393224 | tf_op jit(solution)/shard_map/ppermute | solution.py:414
  91.9 1.3 %collective-permute-start.18 = (bf16[256,256]{1,0:T(8,128)(2,1)S(1)}, bf16[256,256]{1,0:T(8,128)(2,1)S(1)}, u32[]{:S(2)}, u32[]{:S(2)}) collective-permute-start(bf16[256,256]{1,0:T(8,128)(2,1)S(1)} %get-tuple-element.83), channel_id=1, source_target_pairs={{1,0},{2,1},{3,2},{4,3},{5,4},{6,5},{7,6},{8,7},{9,8},{10,9},{11,1... | collective-permute-start | bytes 393224 | tf_op jit(solution)/shard_map/ppermute | solution.py:414
  93.2 2.7 %collective-permute-start.19 = (bf16[256,256]{1,0:T(8,128)(2,1)S(1)}, bf16[256,256]{1,0:T(8,128)(2,1)S(1)}, u32[]{:S(2)}, u32[]{:S(2)}) collective-permute-start(bf16[256,256]{1,0:T(8,128)(2,1)S(1)} %get-tuple-element.87), channel_id=1, source_target_pairs={{0,2},{1,3},{2,4},{3,5},{4,6},{5,7},{6,0},{7,1},{8,10},{9,11},{10,... | collective-permute-start | bytes 393224 | tf_op jit(solution)/shard_map/ppermute | solution.py:406
  95.9 1.6 %collective-permute-start.20 = (bf16[256,256]{1,0:T(8,128)(2,1)S(1)}, bf16[256,256]{1,0:T(8,128)(2,1)S(1)}, u32[]{:S(2)}, u32[]{:S(2)}) collective-permute-start(bf16[256,256]{1,0:T(8,128)(2,1)S(1)} %get-tuple-element.88), channel_id=1, source_target_pairs={{0,4},{1,5},{2,6},{3,7},{4,0},{5,1},{6,2},{7,3},{8,12},{9,13},{10,... | collective-permute-start | bytes 393224 | tf_op jit(solution)/shard_map/ppermute | solution.py:406
  97.5 2.5 %collective-permute-start.21 = (bf16[256,256]{1,0:T(8,128)(2,1)S(1)}, bf16[256,256]{1,0:T(8,128)(2,1)S(1)}, u32[]{:S(2)}, u32[]{:S(2)}) collective-permute-start(bf16[256,256]{1,0:T(8,128)(2,1)S(1)} %get-tuple-element.89), channel_id=1, source_target_pairs={{0,6},{1,7},{2,0},{3,1},{4,2},{5,3},{6,4},{7,5},{8,14},{9,15},{10,... | collective-permute-start | bytes 393224 | tf_op jit(solution)/shard_map/ppermute | solution.py:406
  100.1 2.7 %shard_map.200 = (f32[2048,256]{1,0:T(8,128)S(1)}, f32[2048,256]{1,0:T(8,128)S(1)}, f32[2048,256]{1,0:T(8,128)S(1)}) custom-call(f32[2048,256]{1,0:T(8,128)S(1)} %get-tuple-element.48.slip_ref, f32[2048,256]{1,0:T(8,128)S(1)} %get-tuple-element.57.state_ref, f32[2048,256]{1,0:T(8,128)S(1)} %get-tuple-element.74.slip_mid_ref, ...), custom_call_target="tpu_custom_call" | custom-call | tf_op jit(solution)/shard_map/pallas_call | solution.py:33
  102.8 1.0 collective-permute-done.19.refs_1_
  103.7 5.7 %collective-permute-done.20.refs_2_ = bf16[256,256]{1,0:T(8,128)(2,1)S(1)} collective-permute-done((bf16[256,256]{1,0:T(8,128)(2,1)S(1)}, bf16[256,256]{1,0:T(8,128)(2,1)S(1)}, u32[]{:S(2)}, u32[]{:S(2)}) %collective-permute-start.20) | collective-permute-done | bytes 131104 | tf_op jit(solution)/shard_map/ppermute | solution.py:406
  109.4 4.5 %shard_map.201 = (f32[2048,256]{1,0:T(8,128)}, f32[2048,256]{1,0:T(8,128)}) custom-call(f32[2048,256]{1,0:T(8,128)S(1)} %get-tuple-element.84.shift_ref, f32[2048,256]{1,0:T(8,128)S(1)} %get-tuple-element.76.scale_ref, f32[2048,256]{1,0:T(8,128)S(1)} %get-tuple-element.85.rest_ref, f32[2048,256]{1,0:T(8,128)S(1)} %get-tuple-element.86.slip_rest_ref, ...), custom_call_target="tpu_custom_call" | custom-call | tf_op jit(solution)/shard_map/pallas_call | solution.py:33
  (41 shorter events, 0.2 us)
Async XLA Ops:
  9.8 1.0 copy-start.2
  10.8 0.6 copy-start.6
  11.4 0.6 copy-start.8
  12.1 8.6 %collective-permute-start.2 = (bf16[256,256]{1,0:T(8,128)(2,1)S(1)}, bf16[256,256]{1,0:T(8,128)(2,1)S(1)}, u32[]{:S(2)}, u32[]{:S(2)}) collective-permute-start(bf16[256,256]{1,0:T(8,128)(2,1)S(1)} %get-tuple-element.52.after_ref.refs_0_), channel_id=1, source_target_pairs={{0,24},{8,0},{16,8},{24,16},{1,25},{9,1},{17,9},{25,17},{2,26},{10... | collective-permute-start | bytes 393224 | tf_op jit(solution)/shard_map/ppermute | solution.py:402
  16.0 15.5 %collective-permute-start.1 = (bf16[256,256]{1,0:T(8,128)(2,1)S(1)}, bf16[256,256]{1,0:T(8,128)(2,1)S(1)}, u32[]{:S(2)}, u32[]{:S(2)}) collective-permute-start(bf16[256,256]{1,0:T(8,128)(2,1)S(1)} %get-tuple-element.52.after_ref.refs_0_), channel_id=1, source_target_pairs={{0,16},{8,24},{16,0},{24,8},{1,17},{9,25},{17,1},{25,9},{2,18},{10... | collective-permute-start | bytes 393224 | tf_op jit(solution)/shard_map/ppermute | solution.py:402
  16.5 15.0 %collective-permute-start = (bf16[256,256]{1,0:T(8,128)(2,1)S(1)}, bf16[256,256]{1,0:T(8,128)(2,1)}, u32[]{:S(2)}, u32[]{:S(2)}) collective-permute-start(bf16[256,256]{1,0:T(8,128)(2,1)S(1)} %get-tuple-element.52.after_ref.refs_0_), channel_id=1, source_target_pairs={{0,8},{8,16},{16,24},{24,0},{1,9},{9,17},{17,25},{25,1},{2,10},{10... | collective-permute-start | bytes 393224 | tf_op jit(solution)/shard_map/ppermute | solution.py:402
  17.1 19.0 %collective-permute-start.6 = (bf16[128,512]{1,0:T(8,128)(2,1)}, bf16[128,512]{1,0:T(8,128)(2,1)}, u32[]{:S(2)}, u32[]{:S(2)}) collective-permute-start(bf16[128,512]{1,0:T(8,128)(2,1)} %get-tuple-element.60.refs_0_), channel_id=1, source_target_pairs={{0,6},{1,7},{2,0},{3,1},{4,2},{5,3},{6,4},{7,5},{8,14},{9,15},{10,... | collective-permute-start | bytes 393224 | tf_op jit(solution)/shard_map/ppermute | solution.py:406
  20.7 15.4 %collective-permute-start.5 = (bf16[128,512]{1,0:T(8,128)(2,1)}, bf16[128,512]{1,0:T(8,128)(2,1)}, u32[]{:S(2)}, u32[]{:S(2)}) collective-permute-start(bf16[128,512]{1,0:T(8,128)(2,1)} %get-tuple-element.60.refs_0_), channel_id=1, source_target_pairs={{0,4},{1,5},{2,6},{3,7},{4,0},{5,1},{6,2},{7,3},{8,12},{9,13},{10,... | collective-permute-start | bytes 393224 | tf_op jit(solution)/shard_map/ppermute | solution.py:406
  20.7 15.4 %collective-permute-start.4 = (bf16[128,512]{1,0:T(8,128)(2,1)}, bf16[128,512]{1,0:T(8,128)(2,1)}, u32[]{:S(2)}, u32[]{:S(2)}) collective-permute-start(bf16[128,512]{1,0:T(8,128)(2,1)} %get-tuple-element.60.refs_0_), channel_id=1, source_target_pairs={{0,2},{1,3},{2,4},{3,5},{4,6},{5,7},{6,0},{7,1},{8,10},{9,11},{10,... | collective-permute-start | bytes 393224 | tf_op jit(solution)/shard_map/ppermute | solution.py:406
  30.1 1.3 %copy-start = (bf16[1024,1024]{1,0:T(8,128)(2,1)}, bf16[1024,1024]{1,0:T(8,128)(2,1)S(1)}, u32[]{:S(2)}) copy-start(bf16[1024,1024]{1,0:T(8,128)(2,1)S(1)} %get-tuple-element.58.low_ref) | copy-start | bytes 6291460
  36.1 6.2 %collective-permute-start.3 = (bf16[1024,256]{1,0:T(8,128)(2,1)}, bf16[1024,256]{1,0:T(8,128)(2,1)}, u32[]{:S(2)}, u32[]{:S(2)}) collective-permute-start(bf16[1024,256]{1,0:T(8,128)(2,1)} %shard_map.189), channel_id=1, source_target_pairs={{0,1},{1,0},{2,3},{3,2},{4,5},{5,4},{6,7},{7,6},{8,9},{9,8},{10,11... | collective-permute-start | bytes 1572872 | tf_op jit(solution)/shard_map/ppermute | solution.py:409
  38.1 14.7 %collective-permute-start.7 = (bf16[512,512]{1,0:T(8,128)(2,1)}, bf16[512,512]{1,0:T(8,128)(2,1)}, u32[]{:S(2)}, u32[]{:S(2)}) collective-permute-start(bf16[512,512]{1,0:T(8,128)(2,1)} %shard_map.192.own_ref), channel_id=1, source_target_pairs={{0,1},{1,0},{2,3},{3,2},{4,5},{5,4},{6,7},{7,6},{8,9},{9,8},{10,11... | collective-permute-start | bytes 1572872 | tf_op jit(solution)/shard_map/ppermute | solution.py:409
  38.6 5.0 %copy-start.7 = (bf16[256,256]{1,0:T(8,128)(2,1)S(1)}, bf16[256,256]{1,0:T(8,128)(2,1)}, u32[]{:S(2)}) copy-start(bf16[256,256]{1,0:T(8,128)(2,1)} %copy-done.6) | copy-start | bytes 393220
  38.6 5.0 %copy-start.9 = (bf16[256,256]{1,0:T(8,128)(2,1)S(1)}, bf16[256,256]{1,0:T(8,128)(2,1)}, u32[]{:S(2)}) copy-start(bf16[256,256]{1,0:T(8,128)(2,1)} %copy-done.8) | copy-start | bytes 393220
  43.7 17.9 %collective-permute-start.8 = (bf16[256,256]{1,0:T(8,128)(2,1)S(1)}, bf16[256,256]{1,0:T(8,128)(2,1)S(1)}, u32[]{:S(2)}, u32[]{:S(2)}) collective-permute-start(bf16[256,256]{1,0:T(8,128)(2,1)S(1)} %get-tuple-element.66), channel_id=1, source_target_pairs={{0,1},{1,2},{2,3},{3,4},{4,5},{5,6},{6,7},{7,8},{8,9},{9,10},{10,1... | collective-permute-start | bytes 393224 | tf_op jit(solution)/shard_map/ppermute | solution.py:414
  45.7 16.0 %collective-permute-start.9 = (bf16[256,256]{1,0:T(8,128)(2,1)S(1)}, bf16[256,256]{1,0:T(8,128)(2,1)S(1)}, u32[]{:S(2)}, u32[]{:S(2)}) collective-permute-start(bf16[256,256]{1,0:T(8,128)(2,1)S(1)} %get-tuple-element.67), channel_id=1, source_target_pairs={{1,0},{2,1},{3,2},{4,3},{5,4},{6,5},{7,6},{8,7},{9,8},{10,9},{11,1... | collective-permute-start | bytes 393224 | tf_op jit(solution)/shard_map/ppermute | solution.py:414
  47.0 20.6 %collective-permute-start.10 = (bf16[256,256]{1,0:T(8,128)(2,1)S(1)}, bf16[256,256]{1,0:T(8,128)(2,1)S(1)}, u32[]{:S(2)}, u32[]{:S(2)}) collective-permute-start(bf16[256,256]{1,0:T(8,128)(2,1)S(1)} %get-tuple-element.71), channel_id=1, source_target_pairs={{0,2},{1,3},{2,4},{3,5},{4,6},{5,7},{6,0},{7,1},{8,10},{9,11},{10,... | collective-permute-start | bytes 393224 | tf_op jit(solution)/shard_map/ppermute | solution.py:406
  51.8 15.8 %collective-permute-start.11 = (bf16[256,256]{1,0:T(8,128)(2,1)S(1)}, bf16[256,256]{1,0:T(8,128)(2,1)S(1)}, u32[]{:S(2)}, u32[]{:S(2)}) collective-permute-start(bf16[256,256]{1,0:T(8,128)(2,1)S(1)} %get-tuple-element.72), channel_id=1, source_target_pairs={{0,4},{1,5},{2,6},{3,7},{4,0},{5,1},{6,2},{7,3},{8,12},{9,13},{10,... | collective-permute-start | bytes 393224 | tf_op jit(solution)/shard_map/ppermute | solution.py:406
  52.7 8.9 %copy-start.1 = (bf16[1024,1024]{1,0:T(8,128)(2,1)S(1)}, bf16[1024,1024]{1,0:T(8,128)(2,1)}, u32[]{:S(2)}) copy-start(bf16[1024,1024]{1,0:T(8,128)(2,1)} %copy-done) | copy-start | bytes 6291460
  52.7 8.9 %copy-start.3 = (bf16[2048,256]{1,0:T(8,128)(2,1)S(1)}, bf16[2048,256]{1,0:T(8,128)(2,1)}, u32[]{:S(2)}) copy-start(bf16[2048,256]{1,0:T(8,128)(2,1)} %copy-done.2) | copy-start | bytes 3145732
  52.7 14.9 %collective-permute-start.12 = (bf16[256,256]{1,0:T(8,128)(2,1)S(1)}, bf16[256,256]{1,0:T(8,128)(2,1)S(1)}, u32[]{:S(2)}, u32[]{:S(2)}) collective-permute-start(bf16[256,256]{1,0:T(8,128)(2,1)S(1)} %get-tuple-element.73), channel_id=1, source_target_pairs={{0,6},{1,7},{2,0},{3,1},{4,2},{5,3},{6,4},{7,5},{8,14},{9,15},{10,... | collective-permute-start | bytes 393224 | tf_op jit(solution)/shard_map/ppermute | solution.py:406
  61.7 6.0 %copy-start.4 = (bf16[32,2048]{1,0:T(8,128)(2,1)S(1)}, bf16[32,2048]{1,0:T(8,128)(2,1)}, u32[]{:S(2)}) copy-start(bf16[32,2048]{1,0:T(8,128)(2,1)} %basis_out_ref.3) | copy-start | bytes 393220
  61.7 6.0 %copy-start.5 = (bf16[32,2048]{1,0:T(8,128)(2,1)S(1)}, bf16[32,2048]{1,0:T(8,128)(2,1)}, u32[]{:S(2)}) copy-start(bf16[32,2048]{1,0:T(8,128)(2,1)} %basis_in_ref.1) | copy-start | bytes 393220
  70.7 7.6 %collective-permute-start.15 = (bf16[256,256]{1,0:T(8,128)(2,1)S(1)}, bf16[256,256]{1,0:T(8,128)(2,1)S(1)}, u32[]{:S(2)}, u32[]{:S(2)}) collective-permute-start(bf16[256,256]{1,0:T(8,128)(2,1)S(1)} %get-tuple-element.80.refs_0_), channel_id=1, source_target_pairs={{0,24},{8,0},{16,8},{24,16},{1,25},{9,1},{17,9},{25,17},{2,26},{10... | collective-permute-start | bytes 393224 | tf_op jit(solution)/shard_map/ppermute | solution.py:402
  75.2 5.0 %collective-permute-start.14 = (bf16[256,256]{1,0:T(8,128)(2,1)S(1)}, bf16[256,256]{1,0:T(8,128)(2,1)S(1)}, u32[]{:S(2)}, u32[]{:S(2)}) collective-permute-start(bf16[256,256]{1,0:T(8,128)(2,1)S(1)} %get-tuple-element.80.refs_0_), channel_id=1, source_target_pairs={{0,16},{8,24},{16,0},{24,8},{1,17},{9,25},{17,1},{25,9},{2,18},{10... | collective-permute-start | bytes 393224 | tf_op jit(solution)/shard_map/ppermute | solution.py:402
  75.9 5.9 %collective-permute-start.13 = (bf16[256,256]{1,0:T(8,128)(2,1)S(1)}, bf16[256,256]{1,0:T(8,128)(2,1)S(1)}, u32[]{:S(2)}, u32[]{:S(2)}) collective-permute-start(bf16[256,256]{1,0:T(8,128)(2,1)S(1)} %get-tuple-element.80.refs_0_), channel_id=1, source_target_pairs={{0,8},{8,16},{16,24},{24,0},{1,9},{9,17},{17,25},{25,1},{2,10},{10... | collective-permute-start | bytes 393224 | tf_op jit(solution)/shard_map/ppermute | solution.py:402
  85.5 3.8 %collective-permute-start.16 = (bf16[1024,256]{1,0:T(8,128)(2,1)S(1)}, bf16[1024,256]{1,0:T(8,128)(2,1)S(1)}, u32[]{:S(2)}, u32[]{:S(2)}) collective-permute-start(bf16[1024,256]{1,0:T(8,128)(2,1)S(1)} %shard_map.197), channel_id=1, source_target_pairs={{0,1},{1,0},{2,3},{3,2},{4,5},{5,4},{6,7},{7,6},{8,9},{9,8},{10,11... | collective-permute-start | bytes 1572872 | tf_op jit(solution)/shard_map/ppermute | solution.py:409
  89.5 10.5 %collective-permute-start.17 = (bf16[256,256]{1,0:T(8,128)(2,1)S(1)}, bf16[256,256]{1,0:T(8,128)(2,1)S(1)}, u32[]{:S(2)}, u32[]{:S(2)}) collective-permute-start(bf16[256,256]{1,0:T(8,128)(2,1)S(1)} %get-tuple-element.82), channel_id=1, source_target_pairs={{0,1},{1,2},{2,3},{3,4},{4,5},{5,6},{6,7},{7,8},{8,9},{9,10},{10,1... | collective-permute-start | bytes 393224 | tf_op jit(solution)/shard_map/ppermute | solution.py:414
  91.9 8.1 %collective-permute-start.18 = (bf16[256,256]{1,0:T(8,128)(2,1)S(1)}, bf16[256,256]{1,0:T(8,128)(2,1)S(1)}, u32[]{:S(2)}, u32[]{:S(2)}) collective-permute-start(bf16[256,256]{1,0:T(8,128)(2,1)S(1)} %get-tuple-element.83), channel_id=1, source_target_pairs={{1,0},{2,1},{3,2},{4,3},{5,4},{6,5},{7,6},{8,7},{9,8},{10,9},{11,1... | collective-permute-start | bytes 393224 | tf_op jit(solution)/shard_map/ppermute | solution.py:414
  93.2 10.5 %collective-permute-start.19 = (bf16[256,256]{1,0:T(8,128)(2,1)S(1)}, bf16[256,256]{1,0:T(8,128)(2,1)S(1)}, u32[]{:S(2)}, u32[]{:S(2)}) collective-permute-start(bf16[256,256]{1,0:T(8,128)(2,1)S(1)} %get-tuple-element.87), channel_id=1, source_target_pairs={{0,2},{1,3},{2,4},{3,5},{4,6},{5,7},{6,0},{7,1},{8,10},{9,11},{10,... | collective-permute-start | bytes 393224 | tf_op jit(solution)/shard_map/ppermute | solution.py:406
  95.9 13.5 %collective-permute-start.20 = (bf16[256,256]{1,0:T(8,128)(2,1)S(1)}, bf16[256,256]{1,0:T(8,128)(2,1)S(1)}, u32[]{:S(2)}, u32[]{:S(2)}) collective-permute-start(bf16[256,256]{1,0:T(8,128)(2,1)S(1)} %get-tuple-element.88), channel_id=1, source_target_pairs={{0,4},{1,5},{2,6},{3,7},{4,0},{5,1},{6,2},{7,3},{8,12},{9,13},{10,... | collective-permute-start | bytes 393224 | tf_op jit(solution)/shard_map/ppermute | solution.py:406
  97.5 11.9 %collective-permute-start.21 = (bf16[256,256]{1,0:T(8,128)(2,1)S(1)}, bf16[256,256]{1,0:T(8,128)(2,1)S(1)}, u32[]{:S(2)}, u32[]{:S(2)}) collective-permute-start(bf16[256,256]{1,0:T(8,128)(2,1)S(1)} %get-tuple-element.89), channel_id=1, source_target_pairs={{0,6},{1,7},{2,0},{3,1},{4,2},{5,3},{6,4},{7,5},{8,14},{9,15},{10,... | collective-permute-start | bytes 393224 | tf_op jit(solution)/shard_map/ppermute | solution.py:406
